TPU v7x, 32 devices: a whole 2x2x4 slice. The times are simulated.
32 devices in a mesh: shard: 4 (over z), ctx: 4 (over x, core), tp: 2 (over y).
Axes of the slice: x: 2, y: 2, z: 4, core: 2. Of those that a mesh axis runs over, the one named last changes fastest.
Arguments:
- frames: bfloat16 [2, 4, 2048, 1280], P(None, 'shard', 'ctx'), may hold values from -6 to 6
- lengths: int32 [2, 4], P(None, 'shard'), may hold values from 256 to 2048, as said below
- norm1_gain: float32 [1280], replicated, may hold values from 0.1 to 1.9
- norm1_bias: float32 [1280], replicated, may hold values from -1.8 to 1.8
- query_weight: bfloat16 [1280, 1280], P('shard', 'tp'), may hold values from -0.15625 to 0.15625
- query_bias: float32 [1280], P('tp'), may hold values from -3 to 3
- key_weight: bfloat16 [1280, 1280], P('shard', 'tp'), may hold values from -0.15625 to 0.15625
- value_weight: bfloat16 [1280, 1280], P('shard', 'tp'), may hold values from -0.15625 to 0.15625
- value_bias: float32 [1280], P('tp'), may hold values from -1.2 to 1.2
- out_weight: bfloat16 [1280, 1280], P('shard', 'tp'), may hold values from -0.625 to 0.625
- out_bias: float32 [1280], replicated, may hold values from -1.8 to 1.8
- norm2_gain: float32 [1280], replicated, may hold values from 0.1 to 1.9
- norm2_bias: float32 [1280], replicated, may hold values from -1.8 to 1.8
- up_weight: bfloat16 [1280, 5120], P('shard', 'tp'), may hold values from -0.15625 to 0.15625
- up_bias: float32 [5120], P('tp'), may hold values from -1.8 to 1.8
- down_weight: bfloat16 [1280, 5120], P('shard', 'tp'), may hold values from -0.125 to 0.125
- down_bias: float32 [1280], replicated, may hold values from -1.8 to 1.8
- cotangent: bfloat16 [2, 4, 2048, 1280], P(None, 'shard', 'ctx'), may hold values from -6 to 6
Outputs:
- output: bfloat16 [2, 4, 2048, 1280], P(None, 'shard', 'ctx')
- frames_grad: float32 [2, 4, 2048, 1280], P(None, 'shard', 'ctx')
- norm1_gain_grad: float32 [1280], replicated
- norm1_bias_grad: float32 [1280], replicated
- query_weight_grad: float32 [1280, 1280], P('shard', 'tp')
- query_bias_grad: float32 [1280], P('tp')
- key_weight_grad: float32 [1280, 1280], P('shard', 'tp')
- value_weight_grad: float32 [1280, 1280], P('shard', 'tp')
- value_bias_grad: float32 [1280], P('tp')
- out_weight_grad: float32 [1280, 1280], P('shard', 'tp')
- out_bias_grad: float32 [1280], replicated
- norm2_gain_grad: float32 [1280], replicated
- norm2_bias_grad: float32 [1280], replicated
- up_weight_grad: float32 [1280, 5120], P('shard', 'tp')
- up_bias_grad: float32 [5120], P('tp')
- down_weight_grad: float32 [1280, 5120], P('shard', 'tp')
- down_bias_grad: float32 [1280], replicated
Inputs may be any that keep to these rules, and one draw needn't show every extreme that they name: Each clip's number of valid frames lies between the stated bounds; of the 2 clips lengths[:, b] that share a column b, one has exactly 2048.
All inputs are finite; a program needn't handle non-finite values.
Results may differ from a plain program's by a relative error of at most 0.02.
Values may be sent and summed in bfloat16 or wider, within the bound.
A program may use at most 224 MiB of HBM per device.

v0:
```python
import jax
import jax.numpy as jnp
from jax import lax
from jax.sharding import PartitionSpec as P

HEAD_DIM = 80


epsilon = 1e-05


def layer_norm(values, gain, bias):
    center = values - jnp.mean(values, axis=-1, keepdims=True)
    spread = jnp.mean(center * center, axis=-1, keepdims=True)
    return center * lax.rsqrt(spread + epsilon) * gain + bias


def exact_gelu(values):
    return jax.nn.gelu(values, approximate=False)


def contract_last(left, right):
    return lax.dot_general(
        left, right, (((1,), (1,)), ((), ())), preferred_element_type=jnp.float32
    )


def contract_first(left, right):
    return lax.dot_general(
        left, right, (((0,), (0,)), ((), ())), preferred_element_type=jnp.float32
    )


def add_up(total, term):
    return term if total is None else total + term


def gather_weights(query_weight, key_weight, value_weight, out_weight, up_weight, down_weight):
    return (
        lax.all_gather(query_weight, "shard", axis=0, tiled=True),
        lax.all_gather(key_weight, "shard", axis=0, tiled=True),
        lax.all_gather(value_weight, "shard", axis=0, tiled=True),
        lax.all_gather(out_weight, "shard", axis=0, tiled=True),
        lax.all_gather(up_weight, "shard", axis=0, tiled=True),
        lax.all_gather(down_weight, "shard", axis=0, tiled=True),
    )


def branch_total(local_term):
    return lax.psum(local_term, "tp")


def grad_total(local_term):
    return lax.psum(local_term, "tp")


def masked_scores(query_heads, key_heads, key_valid, scaling):
    scores = (
        jnp.einsum("qhd,khd->hqk", query_heads, key_heads, preferred_element_type=jnp.float32)
        * scaling
    )
    return jnp.where(key_valid[None, None, :], scores, -1000000000.0)


def body(
    frames,
    lengths,
    norm1_gain,
    norm1_bias,
    query_weight,
    query_bias,
    key_weight,
    value_weight,
    value_bias,
    out_weight,
    out_bias,
    norm2_gain,
    norm2_bias,
    up_weight,
    up_bias,
    down_weight,
    down_bias,
    cotangent,
):
    segment = frames.shape[2]
    width = query_weight.shape[1]
    head_count = width // HEAD_DIM
    scaling = HEAD_DIM ** (-0.5)
    weight_sums = [None] * 6
    small_sums = [None] * 9
    outputs_list = []
    input_grads = []
    for micro_index in range(frames.shape[0]):
        gathered = gather_weights(
            query_weight, key_weight, value_weight, out_weight, up_weight, down_weight
        )
        full_query, full_key, full_value, full_out, full_up, full_down = gathered
        clip_rows = frames[micro_index, 0].astype(jnp.float32)
        length = lengths[micro_index, 0]
        normed, norm1_pull = jax.vjp(layer_norm, clip_rows, norm1_gain, norm1_bias)
        normed_low = normed.astype(jnp.bfloat16)
        queries = (
            jnp.dot(normed_low, full_query, preferred_element_type=jnp.float32) + query_bias
        ).astype(jnp.bfloat16)
        keys_local = jnp.dot(normed_low, full_key, preferred_element_type=jnp.float32).astype(
            jnp.bfloat16
        )
        values_local = (
            jnp.dot(normed_low, full_value, preferred_element_type=jnp.float32) + value_bias
        ).astype(jnp.bfloat16)
        keys_all, values_all = (
            lax.all_gather(keys_local, "ctx", axis=0, tiled=True),
            lax.all_gather(values_local, "ctx", axis=0, tiled=True),
        )
        total_keys = keys_all.shape[0]
        key_valid = jnp.arange(total_keys, dtype=jnp.int32) < length
        query_heads = queries.reshape(segment, head_count, HEAD_DIM)
        key_heads = keys_all.reshape(total_keys, head_count, HEAD_DIM)
        value_heads = values_all.reshape(total_keys, head_count, HEAD_DIM)
        scores = masked_scores(query_heads, key_heads, key_valid, scaling)
        row_max = jnp.max(scores, axis=-1, keepdims=True)
        log_total = row_max + jnp.log(jnp.sum(jnp.exp(scores - row_max), axis=-1, keepdims=True))
        probs_low = jnp.exp(scores - log_total).astype(jnp.bfloat16)
        attended = jnp.einsum(
            "hqk,khd->qhd", probs_low, value_heads, preferred_element_type=jnp.float32
        )
        attended = attended.reshape(segment, width).astype(jnp.bfloat16)
        upstream_low = cotangent[micro_index, 0]
        upstream = upstream_low.astype(jnp.float32)
        mixed = clip_rows + branch_total(contract_last(attended, full_out)) + out_bias
        normed2, norm2_pull = jax.vjp(layer_norm, mixed, norm2_gain, norm2_bias)
        normed2_low = normed2.astype(jnp.bfloat16)
        hidden = jnp.dot(normed2_low, full_up, preferred_element_type=jnp.float32) + up_bias
        activated, gelu_pull = jax.vjp(exact_gelu, hidden)
        activated_low = activated.astype(jnp.bfloat16)
        result = mixed + branch_total(contract_last(activated_low, full_down)) + down_bias
        outputs_list.append(result.astype(jnp.bfloat16))
        hidden_grad = gelu_pull(
            jnp.dot(upstream_low, full_down, preferred_element_type=jnp.float32)
        )[0].astype(jnp.bfloat16)
        normed2_grad = grad_total(contract_last(hidden_grad, full_up))
        mixed_part, gain2_part, bias2_part = norm2_pull(normed2_grad)
        mixed_grad = upstream + mixed_part
        branch_grad = mixed_grad.astype(jnp.bfloat16)
        attended_grad = jnp.dot(branch_grad, full_out, preferred_element_type=jnp.float32).astype(
            jnp.bfloat16
        )
        grad_heads = attended_grad.reshape(segment, head_count, HEAD_DIM)
        attn_probs = jnp.exp(masked_scores(query_heads, key_heads, key_valid, scaling) - log_total)
        probs_grad = jnp.einsum(
            "qhd,khd->hqk", grad_heads, value_heads, preferred_element_type=jnp.float32
        )
        row_delta = jnp.sum(attn_probs * probs_grad, axis=-1, keepdims=True)
        score_grad = (attn_probs * (probs_grad - row_delta)).astype(jnp.bfloat16)
        query_grad = (
            jnp.einsum("hqk,khd->qhd", score_grad, key_heads, preferred_element_type=jnp.float32)
            * scaling
        )
        query_grad = query_grad.reshape(segment, width).astype(jnp.bfloat16)
        key_term = (
            jnp.einsum("hqk,qhd->khd", score_grad, query_heads, preferred_element_type=jnp.float32)
            * scaling
        )
        value_term = jnp.einsum(
            "hqk,qhd->khd", probs_low, grad_heads, preferred_element_type=jnp.float32
        )
        key_grad, value_grad = (
            lax.psum_scatter(
                key_term.reshape(total_keys, width), "ctx", scatter_dimension=0, tiled=True
            ),
            lax.psum_scatter(
                value_term.reshape(total_keys, width), "ctx", scatter_dimension=0, tiled=True
            ),
        )
        key_grad = key_grad.astype(jnp.bfloat16)
        value_grad = value_grad.astype(jnp.bfloat16)
        normed_term = (
            contract_last(query_grad, full_query)
            + contract_last(key_grad, full_key)
            + contract_last(value_grad, full_value)
        )
        clip_part, gain1_part, bias1_part = norm1_pull(grad_total(normed_term))
        input_grads.append(mixed_grad + clip_part)
        row_stats = (gain1_part, bias1_part, jnp.sum(mixed_grad, axis=0), gain2_part, bias2_part)
        weight_terms = (
            contract_first(normed_low, query_grad),
            contract_first(normed_low, key_grad),
            contract_first(normed_low, value_grad),
            contract_first(branch_grad, attended),
            contract_first(normed2_low, hidden_grad),
            contract_first(upstream_low, activated_low),
        )
        weight_sums = [add_up(total, term) for total, term in zip(weight_sums, weight_terms)]
        small_terms = (
            row_stats[0],
            row_stats[1],
            jnp.sum(query_grad.astype(jnp.float32), axis=0),
            jnp.sum(value_grad.astype(jnp.float32), axis=0),
            row_stats[2],
            row_stats[3],
            row_stats[4],
            jnp.sum(hidden_grad.astype(jnp.float32), axis=0),
            jnp.sum(upstream, axis=0),
        )
        small_sums = [add_up(total, term) for total, term in zip(small_sums, small_terms)]
    small_done = (
        lax.psum(small_sums[0].astype(jnp.bfloat16), ("shard", "ctx")).astype(jnp.float32),
        lax.psum(small_sums[1].astype(jnp.bfloat16), ("shard", "ctx")).astype(jnp.float32),
        lax.psum(small_sums[2].astype(jnp.bfloat16), ("shard", "ctx")).astype(jnp.float32),
        lax.psum(small_sums[3].astype(jnp.bfloat16), ("shard", "ctx")).astype(jnp.float32),
        lax.psum(small_sums[4].astype(jnp.bfloat16), ("shard", "ctx")).astype(jnp.float32),
        lax.psum(small_sums[5].astype(jnp.bfloat16), ("shard", "ctx")).astype(jnp.float32),
        lax.psum(small_sums[6].astype(jnp.bfloat16), ("shard", "ctx")).astype(jnp.float32),
        lax.psum(small_sums[7].astype(jnp.bfloat16), ("shard", "ctx")).astype(jnp.float32),
        lax.psum(small_sums[8].astype(jnp.bfloat16), ("shard", "ctx")).astype(jnp.float32),
    )
    pieces = (
        lax.psum_scatter(
            weight_sums[0].astype(jnp.bfloat16), ("shard", "ctx"), scatter_dimension=0, tiled=True
        ).astype(jnp.float32),
        lax.psum_scatter(
            weight_sums[1].astype(jnp.bfloat16), ("shard", "ctx"), scatter_dimension=0, tiled=True
        ).astype(jnp.float32),
        lax.psum_scatter(
            weight_sums[2].astype(jnp.bfloat16), ("shard", "ctx"), scatter_dimension=0, tiled=True
        ).astype(jnp.float32),
        lax.psum_scatter(
            weight_sums[3].astype(jnp.bfloat16), ("shard", "ctx"), scatter_dimension=0, tiled=True
        ).astype(jnp.float32),
        lax.psum_scatter(
            weight_sums[4].astype(jnp.bfloat16), ("shard", "ctx"), scatter_dimension=0, tiled=True
        ).astype(jnp.float32),
        lax.psum_scatter(
            weight_sums[5].astype(jnp.bfloat16), ("shard", "ctx"), scatter_dimension=0, tiled=True
        ).astype(jnp.float32),
    )
    owned_rows = (
        lax.all_gather(pieces[0].astype(jnp.bfloat16), "ctx", axis=0, tiled=True).astype(
            jnp.float32
        ),
        lax.all_gather(pieces[1].astype(jnp.bfloat16), "ctx", axis=0, tiled=True).astype(
            jnp.float32
        ),
        lax.all_gather(pieces[2].astype(jnp.bfloat16), "ctx", axis=0, tiled=True).astype(
            jnp.float32
        ),
        lax.all_gather(pieces[3].astype(jnp.bfloat16), "ctx", axis=0, tiled=True).astype(
            jnp.float32
        ),
        lax.all_gather(pieces[4].astype(jnp.bfloat16), "ctx", axis=0, tiled=True).astype(
            jnp.float32
        ),
        lax.all_gather(pieces[5].astype(jnp.bfloat16), "ctx", axis=0, tiled=True).astype(
            jnp.float32
        ),
    )
    layer_output = jnp.stack(outputs_list)[:, None]
    frames_grad = jnp.stack(input_grads)[:, None]
    return (
        layer_output,
        frames_grad,
        small_done[0],
        small_done[1],
        owned_rows[0],
        small_done[2],
        owned_rows[1],
        owned_rows[2],
        small_done[3],
        owned_rows[3],
        small_done[4],
        small_done[5],
        small_done[6],
        owned_rows[4],
        small_done[7],
        owned_rows[5],
        small_done[8],
    )


def solution(mesh):
    placed = (
        P(None, "shard", "ctx", None),
        P(None, "shard"),
        P(),
        P(),
        P("shard", "tp"),
        P("tp"),
        P("shard", "tp"),
        P("shard", "tp"),
        P("tp"),
        P("shard", "tp"),
        P(),
        P(),
        P(),
        P("shard", "tp"),
        P("tp"),
        P("shard", "tp"),
        P(),
        P(None, "shard", "ctx", None),
    )
    return jax.shard_map(
        body,
        mesh=mesh,
        in_specs=placed,
        out_specs=(
            P(None, "shard", "ctx", None),
            P(None, "shard", "ctx", None),
            P(),
            P(),
            P("shard", "tp"),
            P("tp"),
            P("shard", "tp"),
            P("shard", "tp"),
            P("tp"),
            P("shard", "tp"),
            P(),
            P(),
            P(),
            P("shard", "tp"),
            P("tp"),
            P("shard", "tp"),
            P(),
        ),
        check_vma=False,
    )
```

profile of v0, /device:TPU:9, one launch (start us, length us, event | category | flops | bytes accessed | tf_op | source)
XLA Modules:
  0.0 1848.0 jit_solution(11839419839131768975)
XLA Ops:
  12.5 35.1 %all-gather.19.cloned.1.call-done = bf16[1280,640]{1,0:T(8,128)(2,1)} async-done(((bf16[320,640]{1,0:T(8,128)(2,1)}), bf16[1280,640]{1,0:T(8,128)(2,1)}) %all-gather.19.cloned.1.call-update) | async-done | bytes 1638416 | tf_op jit(solution)/shard_map/all_gather | solution.py:41
  51.4 34.9 %all-gather.13.cloned.1.call-done = bf16[1280,640]{1,0:T(8,128)(2,1)} async-done(((bf16[320,640]{1,0:T(8,128)(2,1)}), bf16[1280,640]{1,0:T(8,128)(2,1)}) %all-gather.13.cloned.1.call-update) | async-done | bytes 1638416 | tf_op jit(solution)/shard_map/all_gather | solution.py:42
  100.0 24.9 %all-gather.17.cloned.1.call-done = bf16[1280,640]{1,0:T(8,128)(2,1)} async-done(((bf16[320,640]{1,0:T(8,128)(2,1)}), bf16[1280,640]{1,0:T(8,128)(2,1)}) %all-gather.17.cloned.1.call-update) | async-done | bytes 1638416 | tf_op jit(solution)/shard_map/all_gather | solution.py:40
  135.9 17.2 all-gather.21.cloned.1.call-done
  157.8 15.4 fusion
  173.2 14.5 exponential_reduce_fusion.1
  192.4 15.8 convolution_convert_fusion.4
  212.6 15.8 fusion.1
  228.4 14.5 exponential_reduce_fusion
  247.9 15.8 convolution_convert_fusion.2
  282.5 129.8 %all-reduce.12.cloned.1.call-done = (f32[512,1280]{1,0:T(8,128)}, f32[512,1280]{1,0:T(8,128)}) async-done(((f32[512,1280]{1,0:T(8,128)}, f32[512,1280]{1,0:T(8,128)}), (f32[512,1280]{1,0:T(8,128)}, f32[512,1280]{1,0:T(8,128)})) %all-reduce.12.cloned.1.call-update) | async-done | bytes 5242896 | tf_op jit(solution)/shard_map/psum | solution.py:50
  418.5 112.2 %all-gather.25.cloned.1.call-done = bf16[1280,2560]{1,0:T(8,128)(2,1)} async-done(((bf16[320,2560]{1,0:T(8,128)(2,1)}), bf16[1280,2560]{1,0:T(8,128)(2,1)}) %all-gather.25.cloned.1.call-update) | async-done | bytes 6553616 | tf_op jit(solution)/shard_map/all_gather | solution.py:44
  530.6 20.2 %multiply_convert_fusion.3 = (bf16[512,2560]{1,0:T(8,128)(2,1)}, f32[512,2560]{1,0:T(8,128)}, f32[512,2560]{1,0:T(8,128)}) fusion(f32[2560]{0:T(1024)S(1)} %copy-done.84, bf16[1280,2560]{1,0:T(8,128)(2,1)} %all-gather.25.cloned.1.call-done, f32[512,1280]{1,0:T(8,128)} %copy-done.2, f32[1280]{0:T(1024)S(1)} %copy-done.85, f32[1280]{0:T(1024)S(1)} %copy-done.56, ...), kind=kOutput, calls=%fused_computation.41 | convolution fusion | flops 3445227520 | bytes 22306816 | tf_op jit(solution)/shard_map/dot_general | solution.py:133
  550.9 99.3 %all-gather.27.cloned.1.call-done = bf16[1280,2560]{1,0:T(8,128)(2,1)} async-done(((bf16[320,2560]{1,0:T(8,128)(2,1)}), bf16[1280,2560]{1,0:T(8,128)(2,1)}) %all-gather.27.cloned.1.call-update) | async-done | bytes 6553616 | tf_op jit(solution)/shard_map/all_gather | solution.py:45
  665.3 16.2 multiply_convert_fusion.2
  739.3 88.3 %all-reduce.10.cloned.1.call-done = (f32[512,1280]{1,0:T(8,128)}, f32[512,1280]{1,0:T(8,128)}) async-done(((f32[512,1280]{1,0:T(8,128)}, f32[512,1280]{1,0:T(8,128)}), (f32[512,1280]{1,0:T(8,128)}, f32[512,1280]{1,0:T(8,128)})) %all-reduce.10.cloned.1.call-update) | async-done | bytes 5242896 | tf_op jit(solution)/shard_map/psum | solution.py:54
  839.0 19.3 %fusion.103 = f32[8,80,2048]{2,1,0:T(8,128)} fusion(bf16[512,8,80]{0,2,1:T(8,128)(2,1)S(1)} %bitcast.265, f32[8,512,2048]{2,1,0:T(8,128)} %get-tuple-element.137, f32[8,512]{1,0:T(8,128)S(1)} %copy-done.43, pred[2048]{0:T(1024)(128)(4,1)S(1)} %copy-done.49), kind=kOutput, calls=%fused_computation.187 | convolution fusion | flops 1375731712 | bytes 39471104 | tf_op jit(solution)/shard_map/hqk,qhd->khd/dot_general | solution.py:164
  865.3 16.6 fusion.100
  883.0 25.8 %multiply_reduce_fusion.1 = (f32[8,512]{1,0:T(8,128)S(1)}, f32[8,512,2048]{2,1,0:T(8,128)}) fusion(f32[8,512,2048]{2,1,0:T(8,128)} %get-tuple-element.137, f32[8,512]{1,0:T(8,128)S(1)} %copy-done.43, pred[2048]{0:T(1024)(128)(4,1)S(1)} %copy-done.49, bf16[512,8,80]{0,2,1:T(8,128)(2,1)S(1)} %bitcast.266, bf16[2048,8,80]{0,2,1:T(8,128)(2,1)} %bitcast.256), kind=kOutput, calls=%fused_computation.3 | convolution fusion | flops 1384116224 | bytes 70420480 | tf_op jit(solution)/shard_map/qhd,khd->hqk/dot_general | solution.py:150
  908.8 29.4 %multiply_convert_fusion.1 = bf16[8,512,2048]{2,1,0:T(8,128)(2,1)} fusion(f32[8,512,2048]{2,1,0:T(8,128)} %get-tuple-element.141, f32[8,512,2048]{2,1,0:T(8,128)} %get-tuple-element.137, f32[8,512]{1,0:T(8,128)S(1)} %get-tuple-element.140, f32[8,512]{1,0:T(8,128)S(1)} %copy-done.43, pred[2048]{0:T(1024)(128)(4,1)S(1)} %copy-done.49), kind=kLoop, calls=%fused_computation.2 | loop fusion | flops 50331648 | bytes 83920896 | tf_op jit(solution)/shard_map/convert_element_type | solution.py:154
  951.6 26.4 %multiply_reduce_fusion = (f32[8,512]{1,0:T(8,128)S(1)}, f32[8,512,2048]{2,1,0:T(8,128)}) fusion(f32[8,512,2048]{2,1,0:T(8,128)} %get-tuple-element.135, f32[8,512]{1,0:T(8,128)S(1)} %copy-done.45, pred[2048]{0:T(1024)(128)(4,1)S(1)} %copy-done.47, bf16[512,8,80]{0,2,1:T(8,128)(2,1)S(1)} %bitcast.264, bf16[2048,8,80]{0,2,1:T(8,128)(2,1)} %bitcast.254), kind=kOutput, calls=%fused_computation.1 | convolution fusion | flops 1384116224 | bytes 70420480 | tf_op jit(solution)/shard_map/qhd,khd->hqk/dot_general | solution.py:150
  978.0 28.7 %multiply_convert_fusion = bf16[8,512,2048]{2,1,0:T(8,128)(2,1)} fusion(f32[8,512,2048]{2,1,0:T(8,128)} %get-tuple-element.143, f32[8,512,2048]{2,1,0:T(8,128)} %get-tuple-element.135, f32[8,512]{1,0:T(8,128)S(1)} %get-tuple-element.142, f32[8,512]{1,0:T(8,128)S(1)} %copy-done.45, pred[2048]{0:T(1024)(128)(4,1)S(1)} %copy-done.47), kind=kLoop, calls=%fused_computation | loop fusion | flops 50331648 | bytes 83920896 | tf_op jit(solution)/shard_map/convert_element_type | solution.py:154
  1066.5 49.1 %reduce-scatter.19.cloned.1.call-done = f32[512,640]{0,1:T(8,128)} async-done(((f32[2048,640]{0,1:T(8,128)}), f32[512,640]{0,1:T(8,128)}) %reduce-scatter.19.cloned.1.call-update) | async-done | bytes 1310736 | tf_op jit(solution)/shard_map/reduce_scatter | solution.py:171
  1129.5 40.6 %reduce-scatter.13.cloned.1.call-done = f32[512,640]{0,1:T(8,128)} async-done(((f32[2048,640]{0,1:T(8,128)}), f32[512,640]{0,1:T(8,128)}) %reduce-scatter.13.cloned.1.call-update) | async-done | bytes 1310736 | tf_op jit(solution)/shard_map/reduce_scatter | solution.py:168
  1174.5 49.5 %reduce-scatter.17.cloned.1.call-done = f32[512,640]{0,1:T(8,128)} async-done(((f32[2048,640]{0,1:T(8,128)}), f32[512,640]{0,1:T(8,128)}) %reduce-scatter.17.cloned.1.call-update) | async-done | bytes 1310736 | tf_op jit(solution)/shard_map/reduce_scatter | solution.py:168
  1255.5 29.3 %reduce-scatter.27.cloned.1.call-done = bf16[80,640]{1,0:T(8,128)(2,1)} async-done(((bf16[1280,640]{1,0:T(8,128)(2,1)}), bf16[80,640]{1,0:T(8,128)(2,1)}) %reduce-scatter.27.cloned.1.call-update) | async-done | bytes 102416 | tf_op jit(solution)/shard_map/reduce_scatter | solution.py:227
  1295.1 52.9 %reduce-scatter.21.cloned.1.call-done = bf16[80,640]{1,0:T(8,128)(2,1)} async-done(((bf16[1280,640]{1,0:T(8,128)(2,1)}), bf16[80,640]{1,0:T(8,128)(2,1)}) %reduce-scatter.21.cloned.1.call-update) | async-done | bytes 102416 | tf_op jit(solution)/shard_map/reduce_scatter | solution.py:218
  1375.0 18.1 all-gather.33.cloned.1.call-done
  1397.2 56.4 %reduce-scatter.25.cloned.1.call-done = bf16[80,640]{1,0:T(8,128)(2,1)} async-done(((bf16[1280,640]{1,0:T(8,128)(2,1)}), bf16[80,640]{1,0:T(8,128)(2,1)}) %reduce-scatter.25.cloned.1.call-update) | async-done | bytes 102416 | tf_op jit(solution)/shard_map/reduce_scatter | solution.py:224
  1463.8 52.3 %reduce-scatter.23.cloned.1.call-done = bf16[80,640]{1,0:T(8,128)(2,1)} async-done(((bf16[1280,640]{1,0:T(8,128)(2,1)}), bf16[80,640]{1,0:T(8,128)(2,1)}) %reduce-scatter.23.cloned.1.call-update) | async-done | bytes 102416 | tf_op jit(solution)/shard_map/reduce_scatter | solution.py:221
  1526.8 238.9 %all-reduce.8.cloned.1.call-done = (f32[512,1280]{1,0:T(8,128)}, f32[512,1280]{1,0:T(8,128)}, f32[512,1280]{1,0:T(8,128)}, f32[512,1280]{1,0:T(8,128)}) async-done(((f32[512,1280]{1,0:T(8,128)}, f32[512,1280]{1,0:T(8,128)}, f32[512,1280]{1,0:T(8,128)}, f32[512,1280]{1,0:T(8,128)}), (f32[512,1280]{1,0:T(8,128)}, f32[512,1280]{1,0:T(8,128)}, f32[512,1280]{1,0:T(8,128)}, ...) | async-done | bytes 10485776 | tf_op jit(solution)/shard_map/psum | solution.py:50
  1772.3 48.9 %all-reduce.3 = (bf16[1280]{0:T(1024)(128)(2,1)S(1)}, bf16[1280]{0:T(1024)(128)(2,1)S(1)}, bf16[640]{0:T(1024)(128)(2,1)S(1)}, bf16[640]{0:T(1024)(128)(2,1)S(1)...) all-reduce(bf16[1280]{0:T(1024)(128)(2,1)S(1)} %add_convert_fusion., ...), channel_id=1, replica_groups=mesh['shard'=4,'ctx'=4,'tp'=2] {'shard','ctx'}, use_global_device_ids=true, to_apply=%region_36.37 | all-reduce | flops 11520 | bytes 46080 | tf_op jit(solution)/shard_map/psum | solution.py:207
  (361 shorter events, 380.0 us)
Async XLA Ops:
  7.2 40.5 %all-gather.19.cloned.1.call-start = ((), (), s32[]{:S(2)}) async-start(), calls=%async_computation.13 | async-start | bytes 2048000 | tf_op jit(solution)/shard_map/all_gather | solution.py:41
  7.9 78.4 %all-gather.13.cloned.1.call-start = ((), (), s32[]{:S(2)}) async-start(), calls=%async_computation.10 | async-start | bytes 2048000 | tf_op jit(solution)/shard_map/all_gather | solution.py:42
  8.7 116.2 %all-gather.17.cloned.1.call-start = ((), (), s32[]{:S(2)}) async-start(), calls=%async_computation.12 | async-start | bytes 2048000 | tf_op jit(solution)/shard_map/all_gather | solution.py:40
  9.4 143.6 %all-gather.21.cloned.1.call-start = ((), (), s32[]{:S(2)}) async-start(), calls=%async_computation.14 | async-start | bytes 3276800 | tf_op jit(solution)/shard_map/all_gather | solution.py:112
  11.6 118.2 %copy-start.54 = (f32[512]{0:T(512)}, f32[512]{0:T(512)S(1)}, u32[]{:S(2)}) copy-start(f32[512]{0:T(512)S(1)} %get-tuple-element.153) | copy-start | bytes 6148
  12.5 117.3 %copy-start.63 = (f32[512]{0:T(512)}, f32[512]{0:T(512)S(1)}, u32[]{:S(2)}) copy-start(f32[512]{0:T(512)S(1)} %fusion.113) | copy-start | bytes 6148
  51.3 136.4 %all-gather.15.cloned.1.call-start = ((), (), s32[]{:S(2)}) async-start(), calls=%async_computation.11 | async-start | bytes 3276800 | tf_op jit(solution)/shard_map/all_gather | solution.py:113
  89.9 118.3 %all-gather.31.cloned.1.call-start = ((), (), s32[]{:S(2)}) async-start(), calls=%async_computation.19 | async-start | bytes 3276800 | tf_op jit(solution)/shard_map/all_gather | solution.py:112
  93.6 149.3 %all-gather.29.cloned.1.call-start = ((), (), s32[]{:S(2)}) async-start(), calls=%async_computation.18 | async-start | bytes 3276800 | tf_op jit(solution)/shard_map/all_gather | solution.py:113
  97.3 176.8 %all-gather.23.cloned.1.call-start = ((), (), s32[]{:S(2)}) async-start(), calls=%async_computation.15 | async-start | bytes 2048000 | tf_op jit(solution)/shard_map/all_gather | solution.py:43
  98.0 314.3 %all-reduce.12.cloned.1.call-start = ((), (), s32[]{:S(2)}) async-start(), calls=%async_computation.34 | async-start | bytes 10485760 | tf_op jit(solution)/shard_map/psum | solution.py:50
  100.0 147.9 %copy-start.46 = (pred[2048]{0:T(1024)(128)(4,1)}, pred[2048]{0:T(1024)(128)(4,1)S(1)}, u32[]{:S(2)}) copy-start(pred[2048]{0:T(1024)(128)(4,1)S(1)} %iota_compare_fusion) | copy-start | bytes 6148
  281.1 131.2 %copy-start.77 = (f32[1280]{0:T(1024)S(1)}, f32[1280]{0:T(1024)}, u32[]{:S(2)}) copy-start(f32[1280]{0:T(1024)} %param.28) | copy-start | bytes 15364
  281.1 249.5 %all-gather.25.cloned.1.call-start = ((), (), s32[]{:S(2)}) async-start(), calls=%async_computation.16 | async-start | bytes 8192000 | tf_op jit(solution)/shard_map/all_gather | solution.py:44
  281.7 368.5 %all-gather.27.cloned.1.call-start = ((), (), s32[]{:S(2)}) async-start(), calls=%async_computation.17 | async-start | bytes 8192000 | tf_op jit(solution)/shard_map/all_gather | solution.py:45
  282.4 545.2 %all-reduce.10.cloned.1.call-start = ((), (), s32[]{:S(2)}) async-start(), calls=%async_computation.33 | async-start | bytes 10485760 | tf_op jit(solution)/shard_map/psum | solution.py:54
  415.6 115.0 %copy-start.56 = (f32[1280]{0:T(1024)S(1)}, f32[1280]{0:T(1024)}, u32[]{:S(2)}) copy-start(f32[1280]{0:T(1024)} %param.29) | copy-start | bytes 15364
  415.6 115.0 %copy-start.84 = (f32[2560]{0:T(1024)S(1)}, f32[2560]{0:T(1024)}, u32[]{:S(2)}) copy-start(f32[2560]{0:T(1024)} %param.32) | copy-start | bytes 30724
  418.5 231.7 %copy-start.12 = (bf16[2,1,512,1280]{3,2,1,0:T(8,128)(2,1)S(1)}, bf16[2,1,512,1280]{3,2,1,0:T(8,128)(2,1)}, u32[]{:S(2)}) copy-start(bf16[2,1,512,1280]{3,2,1,0:T(8,128)(2,1)} %param.35) | copy-start | bytes 7864324
  695.5 364.7 %reduce-scatter.31.cloned.1.call-start = ((), (), s32[]{:S(2)}) async-start(), calls=%async_computation.31 | async-start | bytes 6963200 | tf_op jit(solution)/shard_map/reduce_scatter | solution.py:233
  719.7 341.3 %reduce-scatter.29.cloned.1.call-start = ((), (), s32[]{:S(2)}) async-start(), calls=%async_computation.28 | async-start | bytes 6963200 | tf_op jit(solution)/shard_map/reduce_scatter | solution.py:230
  739.2 322.8 %reduce-scatter.15.cloned.1.call-start = ((), (), s32[]{:S(2)}) async-start(), calls=%async_computation.21 | async-start | bytes 6553600 | tf_op jit(solution)/shard_map/reduce_scatter | solution.py:171
  858.3 257.3 %reduce-scatter.19.cloned.1.call-start = ((), (), s32[]{:S(2)}) async-start(), calls=%async_computation.23 | async-start | bytes 6553600 | tf_op jit(solution)/shard_map/reduce_scatter | solution.py:171
  881.9 288.1 %reduce-scatter.13.cloned.1.call-start = ((), (), s32[]{:S(2)}) async-start(), calls=%async_computation.20 | async-start | bytes 6553600 | tf_op jit(solution)/shard_map/reduce_scatter | solution.py:168
  950.6 273.4 %reduce-scatter.17.cloned.1.call-start = ((), (), s32[]{:S(2)}) async-start(), calls=%async_computation.22 | async-start | bytes 6553600 | tf_op jit(solution)/shard_map/reduce_scatter | solution.py:168
  1018.1 266.7 %reduce-scatter.27.cloned.1.call-start = ((), (), s32[]{:S(2)}) async-start(), calls=%async_computation.27 | async-start | bytes 1740800 | tf_op jit(solution)/shard_map/reduce_scatter | solution.py:227
  1026.4 321.7 %reduce-scatter.21.cloned.1.call-start = ((), (), s32[]{:S(2)}) async-start(), calls=%async_computation.24 | async-start | bytes 1740800 | tf_op jit(solution)/shard_map/reduce_scatter | solution.py:218
  1060.2 311.3 %all-gather.35.cloned.1.call-start = ((), (), s32[]{:S(2)}) async-start(), calls=%async_computation.30 | async-start | bytes 2048000 | tf_op jit(solution)/shard_map/all_gather | solution.py:253
  1061.0 332.1 %all-gather.33.cloned.1.call-start = ((), (), s32[]{:S(2)}) async-start(), calls=%async_computation.29 | async-start | bytes 2048000 | tf_op jit(solution)/shard_map/all_gather | solution.py:250
  1061.7 391.9 %reduce-scatter.25.cloned.1.call-start = ((), (), s32[]{:S(2)}) async-start(), calls=%async_computation.26 | async-start | bytes 1740800 | tf_op jit(solution)/shard_map/reduce_scatter | solution.py:224
  1120.6 395.5 %reduce-scatter.23.cloned.1.call-start = ((), (), s32[]{:S(2)}) async-start(), calls=%async_computation.25 | async-start | bytes 1740800 | tf_op jit(solution)/shard_map/reduce_scatter | solution.py:221
  1229.0 536.6 %all-reduce.8.cloned.1.call-start = ((), (), s32[]{:S(2)}) async-start(), calls=%async_computation.32 | async-start | bytes 20971520 | tf_op jit(solution)/shard_map/psum | solution.py:50
  (88 other events, 1278.4 us)
Sparse Core Ops, SparseCore 0:
  9.6 38.0 all-gather.18
  49.2 37.0 all-gather.12
  87.9 37.0 all-gather.16
  126.9 26.0 all-gather.20
  155.0 25.5 all-gather.14
  182.6 25.5 all-gather.30
  210.3 25.5 all-gather.28
  237.5 36.4 all-gather.22
  281.2 131.0 all-reduce.11
  413.8 116.8 all-gather.24
  532.3 117.8 all-gather.26
  695.7 131.8 all-reduce.9
  831.6 85.9 reduce-scatter.30
  921.9 85.9 reduce-scatter.28
  1010.2 51.3 reduce-scatter.14
  1064.2 51.3 reduce-scatter.18
  1118.6 51.3 reduce-scatter.12
  1172.6 51.3 reduce-scatter.16
  1227.7 57.0 reduce-scatter.26
  1289.4 58.5 reduce-scatter.20
  1349.6 21.8 all-gather.34
  1373.0 20.0 all-gather.32
  1396.8 56.7 reduce-scatter.24
  1457.6 58.4 reduce-scatter.22
  1519.3 246.3 all-reduce.7
where the time goes:
time: 1870 us; the launch traced here: 1850 us
  waiting for transfers between devices  1160 us (62%)
  matrix products  393 us (21%)
  other arithmetic  142 us (8%)
  blocking collectives  86.5 us (5%)
  local copies, waits for them, and re-layouts  51.4 us (3%)
    psum x2, waiting for transfers between devices, branch_total(): return lax.psum(local_term, 'tp')  369 us
    all_gather x1, waiting for transfers between devices, gather_weights(): lax.all_gather(up_weight, 'shard', axis=0, tiled=True)  112 us
    all_gather x1, waiting for transfers between devices, gather_weights(): lax.all_gather(down_weight, 'shard', axis=0, tiled=True)  99.3 us
    reduce_scatter x2, waiting for transfers between devices, body(): lax.psum_scatter(key_term.reshape(total_keys, width), 'ctx', scatter_dime...  90 us
    psum x1, waiting for transfers between devices, grad_total(): return lax.psum(local_term, 'tp')  88.3 us
    dot_general x12, matrix products, contract_first(): lax.dot_general(left, right, (((0,), (0,)), ((), ())), preferred_element_...  66.2 us
    convert_element_type x2, other arithmetic, body(): score_grad = (attn_probs * (probs_grad - row_delta)).astype(jnp.bfloat16)  58.2 us
    reduce_scatter x1, waiting for transfers between devices, body(): lax.psum_scatter(weight_sums[2].astype(jnp.bfloat16), ('shard', 'ctx'), s...  56.4 us
  transfers between devices with their start and end apart: 25, of which 19 were waited for; matrix products, arithmetic and copies ran while one was open for 27% of the time, Pallas kernels for 0%

commit v1 on v0

v1 whole, which is shorter than its diff:
```python
import functools
import math

import jax
import jax.numpy as jnp
from jax import lax
from jax.experimental import pallas as pl
from jax.experimental.pallas import tpu as pltpu
from jax.sharding import PartitionSpec as P

HEAD_DIM = 80
STEP = 512
SUB = 256
EPSILON = 1e-05
SCALE = HEAD_DIM**-0.5
LOW = jnp.bfloat16


def contract(left, right, dims):
    return lax.dot_general(left, right, (dims, ((), ())), preferred_element_type=jnp.float32)

def forward_kernel(valid_ref, q_ref, *refs, blocks, heads):
    k_refs, v_refs = refs[:blocks], refs[blocks:2*blocks]
    a_ref, e_ref, inverse_ref, s0_ref, s1_ref, m0_ref, m1_ref, acc_ref, l_ref = refs[2*blocks:]
    h = pl.program_id(0)
    q = q_ref[...]
    span = k_refs[0].shape[1]
    acc_ref[...] = jnp.zeros(acc_ref.shape, jnp.float32)
    l_ref[...] = jnp.zeros(l_ref.shape, jnp.float32)
    step=min(STEP,span)
    def go(s_now, m_now, s_before, m_before):
        m_now[...] = jnp.full(m_now.shape, -1e30, jnp.float32)
        m_last = m_before[...]
        for b in range(blocks):
            for off in range(0, span, step):
                left = valid_ref[b] - off
                def work():
                    rows = slice(b*span+off, b*span+off+step)
                    s = contract(k_refs[b][:, off:off+step], q, ((0,), (0,)))
                    e = jnp.exp2(s_before[rows] - m_last)
                    row = lax.broadcasted_iota(jnp.int32, (step, 1), 0)
                    s = jnp.where(row < left, s, -1e30)
                    s_now[rows] = s
                    m_now[...] = jnp.maximum(m_now[...], jnp.max(s, axis=0, keepdims=True))
                    l_ref[...] += jnp.sum(e, axis=0, keepdims=True)
                    low = e.astype(jnp.bfloat16)
                    e_ref[0, rows] = low
                    acc_ref[...] += contract(v_refs[b][:, off:off+step], low, ((1,), (0,)))
                work()
    @pl.when(lax.rem(h, 2) == 0)
    def _():
        go(s0_ref, m0_ref, s1_ref, m1_ref)
    @pl.when(lax.rem(h, 2) == 1)
    def _():
        go(s1_ref, m1_ref, s0_ref, m0_ref)
    inverse = 1.0 / l_ref[...]
    a_ref[...] = (acc_ref[...] * inverse).astype(jnp.bfloat16)
    inverse_ref[0] = jnp.broadcast_to(inverse, inverse_ref.shape[1:])

def attention_forward(valid, q, kv):
    width, rows = q.shape
    heads = width // HEAD_DIM
    blocks, span = len(kv), kv[0].shape[1]
    head = lambda h: (jnp.minimum(h, heads-1), 0)
    last = lambda h: (jnp.maximum(h-1, 0), 0)
    value = lambda h: (heads + jnp.maximum(h-1, 0), 0)
    return pl.pallas_call(
        functools.partial(forward_kernel, blocks=blocks, heads=heads),
        grid=(heads+1,),
        in_specs=[pl.BlockSpec(memory_space=pltpu.SMEM), pl.BlockSpec((HEAD_DIM, rows), head)]
          + [pl.BlockSpec((HEAD_DIM, span), head)]*blocks + [pl.BlockSpec((HEAD_DIM, span), value)]*blocks,
        out_specs=[pl.BlockSpec((HEAD_DIM, rows), last), pl.BlockSpec((1, blocks*span, rows), lambda h:(jnp.maximum(h-1,0),0,0)), pl.BlockSpec((1,8,rows), lambda h:(jnp.maximum(h-1,0),0,0))],
        out_shape=[jax.ShapeDtypeStruct((width, rows), jnp.bfloat16), jax.ShapeDtypeStruct((heads, blocks*span, rows), jnp.bfloat16), jax.ShapeDtypeStruct((heads, 8, rows), jnp.float32)],
        scratch_shapes=[pltpu.VMEM((blocks*span, rows), jnp.float32), pltpu.VMEM((blocks*span, rows), jnp.float32), pltpu.VMEM((1, rows), jnp.float32), pltpu.VMEM((1, rows), jnp.float32), pltpu.VMEM((HEAD_DIM, rows), jnp.float32), pltpu.VMEM((1, rows), jnp.float32)],
        compiler_params=pltpu.CompilerParams(vmem_limit_bytes=40<<20),
        cost_estimate=pl.CostEstimate(flops=4*rows*blocks*span*256*heads, bytes_accessed=heads*blocks*span*rows*2, transcendentals=rows*blocks*span*heads),
        name="attention_forward",
    )(valid, q, *kv, *kv)

def backward_kernel(valid_ref, q_ref, g_ref, a_ref, inverse_ref, e_ref, *refs, blocks):
    k_refs, v_refs = refs[:blocks], refs[blocks:2*blocks]
    dq_ref = refs[2*blocks]
    dk_refs, dv_refs = refs[2*blocks+1:3*blocks+1], refs[3*blocks+1:4*blocks+1]
    acc_ref = refs[4*blocks+1]
    q = q_ref[...]
    g32 = g_ref[...].astype(jnp.float32) * inverse_ref[0, 0:1]
    delta = jnp.sum(g32 * a_ref[...].astype(jnp.float32), axis=0, keepdims=True)
    g = g32.astype(jnp.bfloat16)
    span = k_refs[0].shape[1]
    step=min(STEP,span)
    acc_ref[...] = jnp.zeros(acc_ref.shape, jnp.float32)
    for b in range(blocks):
        for off in range(0, span, step):
            left = valid_ref[b] - off
            cols = slice(off, off+step)
            rows = slice(b*span+off, b*span+off+step)
            def work():
                sub = min(SUB, step)
                parts = [(slice(off+o, off+o+sub), slice(b*span+off+o, b*span+off+o+sub)) for o in range(0, step, sub)]
                dps = [contract(v_refs[b][:, c], g, ((0,), (0,))) for c, r in parts]
                total = None
                for (c, r), dp in zip(parts, dps):
                    e = e_ref[0, r]
                    dv_refs[b][:, c] = contract(g, e, ((1,), (1,))).astype(jnp.bfloat16)
                    ds = (e.astype(jnp.float32) * (dp - delta)).astype(jnp.bfloat16)
                    t = contract(k_refs[b][:, c], ds, ((1,), (0,)))
                    total = t if total is None else total + t
                    dk_refs[b][:, c] = (contract(q, ds, ((1,), (1,))) * math.log(2.0)).astype(jnp.bfloat16)
                acc_ref[...] += total
            work()
    dq_ref[...] = (acc_ref[...] * HEAD_DIM**-0.5).astype(jnp.bfloat16)

def attention_backward(valid, q, g, a, inverse, e, kv):
    width, rows = q.shape
    heads = width // HEAD_DIM
    blocks, span = len(kv), kv[0].shape[1]
    head = lambda h: (h, 0)
    value = lambda h: (heads + h, 0)
    hspec = pl.BlockSpec((HEAD_DIM, rows), head)
    kspec = pl.BlockSpec((HEAD_DIM, span), head)
    vspec = pl.BlockSpec((HEAD_DIM, span), value)
    out = jax.ShapeDtypeStruct((width, span), jnp.bfloat16)
    return pl.pallas_call(
        functools.partial(backward_kernel, blocks=blocks),
        grid=(heads,),
        in_specs=[pl.BlockSpec(memory_space=pltpu.SMEM), hspec, hspec, hspec, pl.BlockSpec((1,8,rows), lambda h:(h,0,0)), pl.BlockSpec((1, blocks*span, rows), lambda h:(h,0,0))]
          + [kspec]*blocks + [vspec]*blocks,
        out_specs=[hspec] + [kspec]*(2*blocks),
        out_shape=[jax.ShapeDtypeStruct((width, rows), jnp.bfloat16)] + [out]*(2*blocks),
        scratch_shapes=[pltpu.VMEM((HEAD_DIM, rows), jnp.float32)],
        compiler_params=pltpu.CompilerParams(vmem_limit_bytes=40<<20),
        cost_estimate=pl.CostEstimate(flops=8*rows*blocks*span*256*heads, bytes_accessed=heads*blocks*span*rows*2, transcendentals=0),
        name="attention_backward",
    )(valid, q, g, a, inverse, e, *kv, *kv)


def swap(value, axis, bit, size):
    return lax.ppermute(value, axis, [(k, k ^ bit) for k in range(size)])


def bits_of(size):
    found, bit = [], size // 2
    while bit > 0:
        found.append(bit)
        bit //= 2
    return found


def spread(value, axis, size):
    blocks = {0: value}
    for bit in bits_of(size):
        blocks.update({mask | bit: swap(blocks[mask], axis, bit, size) for mask in list(blocks)})
    return [blocks[mask] for mask in range(size)]


def pair_sum(value, axis, size):
    for bit in reversed(bits_of(size)):
        value = value + swap(value, axis, bit, size)
    return value


def low_sum(value, axis, size):
    if size == 1:
        return value
    total = value.astype(LOW)
    for bit in reversed(bits_of(size)):
        total = (total.astype(jnp.float32) + swap(total, axis, bit, size).astype(jnp.float32)).astype(LOW)
    return total.astype(jnp.float32)


def canonical(blocks, axis, size):
    me = lax.axis_index(axis)
    out = jnp.zeros((size,) + blocks[0].shape, blocks[0].dtype)
    for mask, block in enumerate(blocks):
        out = lax.dynamic_update_index_in_dim(out, block, me ^ mask, 0)
    return out


def gather_rows(piece, size):
    me = lax.axis_index("shard")
    right, left = [piece], [piece]
    for hop in range(1, size):
        right.append(lax.ppermute(right[-1], "shard", [(k, k + 1) for k in range(hop - 1, size - 1)]))
        left.append(lax.ppermute(left[-1], "shard", [(k, k - 1) for k in range(size - hop, 0, -1)]))
    out = jnp.zeros((size,) + piece.shape, piece.dtype)
    out = lax.dynamic_update_index_in_dim(out, piece, me, 0)
    for hop in range(1, size):
        block = jnp.where(me >= hop, right[hop], left[size - hop])
        out = lax.dynamic_update_index_in_dim(out, block, lax.rem(me + size - hop, size), 0)
    return out


def gather_weight(weight, shard, ctx, split):
    part = lax.rem(lax.axis_index("ctx"), split)
    rows = weight.shape[0] // split
    piece = lax.dynamic_slice_in_dim(weight, part * rows, rows, 0)
    mine = gather_rows(piece, shard)
    blocks = {0: mine}
    for bit in bits_of(split):
        blocks.update({mask | bit: swap(blocks[mask], "ctx", bit, ctx) for mask in list(blocks)})
    out = jnp.zeros((shard, split, rows, weight.shape[1]), weight.dtype)
    for mask in range(split):
        out = lax.dynamic_update_index_in_dim(out, blocks[mask], part ^ mask, 1)
    return out.reshape(shard * weight.shape[0], weight.shape[1])


def scatter_ctx(chunk, ctx):
    def total(mask, bits):
        if len(bits) == 0:
            return chunk(mask)
        bit, rest = bits[0], bits[1:]
        away = total(mask | bit, rest).astype(LOW)
        return total(mask, rest) + swap(away, "ctx", bit, ctx).astype(jnp.float32)

    return total(0, bits_of(ctx))


def scatter_rows(full, size):
    me = lax.axis_index("shard")
    rows = full.shape[0] // size
    total = lax.dynamic_slice_in_dim(full, me * rows, rows, 0)
    low = full.astype(LOW)
    for shift in range(1, size):
        there = lax.rem(me + shift, size)
        block = lax.dynamic_slice_in_dim(low, there * rows, rows, 0)
        got = lax.ppermute(block, "shard", [(k, (k + shift) % size) for k in range(size)])
        total = total + got.astype(jnp.float32)
    return total


def weight_grad(left, right, right_dim, shard, ctx):
    count = right.shape[right_dim] // ctx
    me = lax.axis_index("ctx")

    def chunk(mask):
        part = lax.dynamic_slice_in_dim(right, (me ^ mask) * count, count, right_dim)
        return contract(left, part, ((0,), (1 - right_dim,)))

    mine = scatter_rows(scatter_ctx(chunk, ctx), shard).astype(LOW)
    blocks = canonical(spread(mine, "ctx", ctx), "ctx", ctx)
    return jnp.moveaxis(blocks, 0, 1).reshape(mine.shape[0], ctx * count).astype(jnp.float32)


def normalize(values):
    center = values - jnp.mean(values, axis=-1, keepdims=True)
    spread_of = jnp.mean(center * center, axis=-1, keepdims=True)
    inverse = lax.rsqrt(spread_of + EPSILON)
    return center * inverse, inverse


def normalize_grad(grad, hat, inverse):
    return inverse * (
        grad - jnp.mean(grad, axis=-1, keepdims=True) - hat * jnp.mean(grad * hat, axis=-1, keepdims=True)
    )


def body(
    sizes,
    frames,
    lengths,
    norm1_gain,
    norm1_bias,
    query_weight,
    query_bias,
    key_weight,
    value_weight,
    value_bias,
    out_weight,
    out_bias,
    norm2_gain,
    norm2_bias,
    up_weight,
    up_bias,
    down_weight,
    down_bias,
    cotangent,
):
    shard, ctx, tp = sizes
    micros, rows = frames.shape[0], frames.shape[2]
    width = query_weight.shape[1]
    ctx_index = lax.axis_index("ctx")

    full_qkv = gather_weight(
        jnp.concatenate([query_weight, key_weight, value_weight], axis=1), shard, ctx, 4 if ctx % 4 == 0 else 1
    )
    out_both = canonical(spread(out_weight, "tp", tp), "tp", tp)
    out_both = jnp.moveaxis(out_both, 0, 1).reshape(out_weight.shape[0], tp * width)
    full_out = gather_weight(out_both, shard, ctx, 2)
    full_up = gather_weight(up_weight, shard, ctx, 4)
    full_down = gather_weight(down_weight, shard, ctx, 2)
    own_out = lax.dynamic_slice_in_dim(full_out, lax.axis_index("tp") * width, width, 1)

    bias = jnp.concatenate([query_bias, jnp.zeros_like(query_bias), value_bias])[:, None]
    scale = jnp.concatenate(
        [jnp.full((width, 1), SCALE * math.log2(math.e), jnp.float32), jnp.ones((2 * width, 1), jnp.float32)]
    )

    inputs = [frames[m, 0].astype(jnp.float32) for m in range(micros)]
    hats1 = [normalize(x) for x in inputs]
    normed1 = [(hat * norm1_gain + norm1_bias).astype(LOW) for hat, _ in hats1]
    projected = [((contract(full_qkv, h, ((0,), (1,))) + bias) * scale).astype(LOW) for h in normed1]
    queries = [p[:width] for p in projected]
    pairs = [spread(p[width:], "ctx", ctx) for p in projected]
    ids = ctx_index ^ jnp.arange(ctx, dtype=jnp.int32)
    valid = [jnp.clip(lengths[m, 0] - rows * ids, 0, rows) for m in range(micros)]

    attended, kept, inverses = zip(*[attention_forward(valid[m], queries[m], pairs[m]) for m in range(micros)])
    mixed, hats2, normed2, hidden = [], [], [], []
    for m in range(micros):
        all_heads = canonical(spread(attended[m], "tp", tp), "tp", tp).reshape(tp * width, rows)
        mixed.append(inputs[m] + contract(all_heads, full_out, ((0,), (1,))) + out_bias)
        hats2.append(normalize(mixed[m]))
        normed2.append((hats2[m][0] * norm2_gain + norm2_bias).astype(LOW))
        hidden.append(contract(normed2[m], full_up, ((1,), (0,))) + up_bias)
    active, hidden_grads, outputs, mixed_grads, branch_grads = [], [], [], [], []
    normed2_grads = []
    for m in range(micros):
        cdf = 0.5 * (1.0 + lax.erf(hidden[m] * math.sqrt(0.5)))
        pdf = jnp.exp(-0.5 * hidden[m] * hidden[m]) * (1.0 / math.sqrt(2.0 * math.pi))
        active.append((hidden[m] * cdf).astype(LOW))
        slope = cdf + hidden[m] * pdf
        hidden_grads.append((contract(cotangent[m, 0], full_down, ((1,), (0,))) * slope).astype(LOW))
        normed2_grads.append(low_sum(contract(hidden_grads[m], full_up, ((1,), (1,))), "tp", tp))
    for m in range(micros):
        branch = low_sum(contract(active[m], full_down, ((1,), (1,))), "tp", tp)
        outputs.append((mixed[m] + branch + down_bias).astype(LOW))
        hat, inverse = hats2[m]
        mixed_grads.append(
            cotangent[m, 0].astype(jnp.float32) + normalize_grad(normed2_grads[m] * norm2_gain, hat, inverse)
        )
        branch_grads.append(mixed_grads[m].astype(LOW))
    projected_grads, normed1_terms, input_grads = [], [], []
    for m in range(micros):
        attended_grad = contract(own_out, branch_grads[m], ((0,), (1,))).astype(LOW)
        parts = attention_backward(
            valid[m], queries[m], attended_grad, attended[m], inverses[m], kept[m], pairs[m]
        )
        terms = [
            jnp.concatenate([parts[1 + mask], parts[1 + ctx + mask]], axis=0) for mask in range(ctx)
        ]
        pair_grad = scatter_ctx(lambda mask: terms[mask].astype(jnp.float32), ctx).astype(LOW)
        projected_grads.append(jnp.concatenate([parts[0], pair_grad], axis=0))
        normed1_terms.append(contract(projected_grads[m], full_qkv, ((0,), (1,))))
    gain1, bias1 = [], []
    for m in range(micros):
        hat, inverse = hats1[m]
        gain1.append(jnp.sum(normed1_terms[m] * hat, axis=0))
        bias1.append(jnp.sum(normed1_terms[m], axis=0))
        total = low_sum(normed1_terms[m], "tp", tp)
        input_grads.append(mixed_grads[m] + normalize_grad(total * norm1_gain, hat, inverse))

    def over(items, dim):
        return jnp.concatenate(items, axis=dim)

    up_grad = weight_grad(over(normed2, 0), over(hidden_grads, 0), 1, shard, ctx)
    down_grad = weight_grad(over([cotangent[m, 0] for m in range(micros)], 0), over(active, 0), 1, shard, ctx)
    out_grad = weight_grad(over(branch_grads, 0), over(attended, 1), 0, shard, ctx)
    projected_all = over(projected_grads, 1)
    qkv_grad = weight_grad(over(normed1, 0), projected_all, 0, shard, ctx)

    def row_sum(items):
        return sum(jnp.sum(item.astype(jnp.float32), axis=0) for item in items)

    small = jnp.concatenate(
        [
            jnp.sum(projected_all[:width].astype(jnp.float32), axis=1),
            jnp.sum(projected_all[2 * width :].astype(jnp.float32), axis=1),
            row_sum(hidden_grads),
            row_sum(mixed_grads),
            row_sum([normed2_grads[m] * hats2[m][0] for m in range(micros)]),
            row_sum(normed2_grads),
            row_sum([cotangent[m, 0] for m in range(micros)]),
        ]
    )
    first = jnp.concatenate([sum(gain1), sum(bias1)])
    first = pair_sum(first, "tp", tp)
    small = jnp.concatenate([small, first])
    small = pair_sum(pair_sum(small, "ctx", ctx), "shard", shard)
    model = norm1_gain.shape[0]
    cuts, at = [], 0
    for count in (width, width, up_bias.shape[0], model, model, model, model, model, model):
        cuts.append(small[at : at + count])
        at += count
    query_bias_sum, value_bias_sum, up_bias_sum, out_bias_sum, gain2_sum, bias2_sum, down_bias_sum, gain1_sum, bias1_sum = cuts
    return (
        jnp.stack(outputs)[:, None],
        jnp.stack(input_grads)[:, None],
        gain1_sum,
        bias1_sum,
        qkv_grad[:, :width],
        query_bias_sum,
        qkv_grad[:, width : 2 * width],
        qkv_grad[:, 2 * width :],
        value_bias_sum,
        out_grad,
        out_bias_sum,
        gain2_sum,
        bias2_sum,
        up_grad,
        up_bias_sum,
        down_grad,
        down_bias_sum,
    )


def solution(mesh):
    sizes = (mesh.shape["shard"], mesh.shape["ctx"], mesh.shape["tp"])
    rows, weight, hidden, copied = P(None, "shard", "ctx", None), P("shard", "tp"), P("tp"), P()
    return jax.shard_map(
        functools.partial(body, sizes),
        mesh=mesh,
        in_specs=(
            rows,
            P(None, "shard"),
            copied,
            copied,
            weight,
            hidden,
            weight,
            weight,
            hidden,
            weight,
            copied,
            copied,
            copied,
            weight,
            hidden,
            weight,
            copied,
            rows,
        ),
        out_specs=(
            rows,
            rows,
            copied,
            copied,
            weight,
            hidden,
            weight,
            weight,
            hidden,
            weight,
            copied,
            copied,
            copied,
            weight,
            hidden,
            weight,
            copied,
        ),
        check_vma=False,
    )
```

time: 1870 us -> 911 us (0.49)
  waiting for transfers between devices: 1160 us -> 315 us
  matrix products: 393 us -> 124 us
  starting transfers between devices: 1.65 us -> 191 us
  blocking collectives: 86.5 us -> 0 us
  local copies, waits for them, and re-layouts: 51.4 us -> 125 us
  other arithmetic: 142 us -> 72.5 us
  Pallas kernels: 0 us -> 64.6 us
    psum x3 -> x0, waiting for transfers between devices: 457 us -> none  [the longest x2 369 us: branch_total(): return lax.psum(local_term, 'tp')]
    all_gather x12 -> x0, waiting for transfers between devices: 365 us -> none  [the longest x1 112 us: gather_weights(): lax.all_gather(up_weight, 'shard', axis=0, tiled=True)]
    reduce_scatter x10 -> x0, waiting for transfers between devices: 330 us -> none  [the longest x2 90 us: body(): lax.psum_scatter(key_term.reshape(total_keys, width), 'ctx', scatter_dime...]
    ppermute x0 -> x94, waiting for transfers between devices: none -> 315 us  [the longest x58 228 us: swap(): return lax.ppermute(value, axis, [(k, k ^ bit) for k in range(size)])]
    dot_general x48 -> x32, matrix products: 393 us -> 124 us  [contract(): lax.dot_general(left, right, (dims, ((), ())), preferred_element_type=jnp...]
    ppermute x0 -> x94, starting transfers between devices: none -> 191 us  [the longest x58 98.3 us: swap(): return lax.ppermute(value, axis, [(k, k ^ bit) for k in range(size)])]
    dynamic_update_slice x0 -> x35, local copies, waits for them, and re-layouts: none -> 80.1 us  [the longest x20 62.1 us: canonical(): out = lax.dynamic_update_index_in_dim(out, block, me ^ mask, 0)]
    pallas_call x0 -> x4, Pallas kernels: none -> 64.6 us  [the longest x2 37.4 us: attention_backward(): pl.pallas_call(functools.partial(backward_kernel, blocks=blocks), grid=(h...]
  transfers between devices with their start and end apart: 25 -> 94, of which waited for: 19 -> 34; matrix products, arithmetic and copies ran while one was open for 27% -> 28% of each run, Pallas kernels for 0% -> 7%
where the time goes in v1:
time: 911 us; the launch traced here: 896 us
  waiting for transfers between devices  315 us (35%)
  starting transfers between devices  191 us (21%)
  local copies, waits for them, and re-layouts  125 us (14%)
  matrix products  124 us (14%)
  other arithmetic  72.5 us (8%)
  Pallas kernels  64.6 us (7%)
    ppermute x58, waiting for transfers between devices, swap(): return lax.ppermute(value, axis, [(k, k ^ bit) for k in range(size)])  228 us
    dot_general x32, matrix products, contract(): lax.dot_general(left, right, (dims, ((), ())), preferred_element_type=jnp...  124 us
    ppermute x58, starting transfers between devices, swap(): return lax.ppermute(value, axis, [(k, k ^ bit) for k in range(size)])  98.3 us
    dynamic_update_slice x20, local copies, waits for them, and re-layouts, canonical(): out = lax.dynamic_update_index_in_dim(out, block, me ^ mask, 0)  62.1 us
    ppermute x12, waiting for transfers between devices, scatter_rows(): lax.ppermute(block, 'shard', [(k, (k + shift) % size) for k in range(size)])  52.4 us
    ppermute x12, starting transfers between devices, gather_rows(): lax.ppermute(left[-1], 'shard', [(k, k - 1) for k in range(size - hop, 0,...  38.9 us
    pallas_call x2, Pallas kernels, attention_backward(): pl.pallas_call(functools.partial(backward_kernel, blocks=blocks), grid=(h...  37.4 us
    ppermute x12, waiting for transfers between devices, gather_rows(): lax.ppermute(left[-1], 'shard', [(k, k - 1) for k in range(size - hop, 0,...  34.9 us
  transfers between devices with their start and end apart: 94, of which 34 were waited for; matrix products, arithmetic and copies ran while one was open for 28% of the time, Pallas kernels for 7%

profile of v1, /device:TPU:9, one launch (start us, length us, event | category | flops | bytes accessed | tf_op | source)
XLA Modules:
  0.0 895.6 jit_solution(7424630232481766680)
XLA Ops:
  29.1 13.8 %dynamic_update_slice.173 = bf16[2,320,640]{2,0,1:T(2,128)(2,1)S(1)} dynamic-update-slice(bf16[2,320,640]{2,0,1:T(2,128)(2,1)S(1)} %broadcast_in_dim.255, bf16[1,320,640]{2,0,1:T(2,128)(2,1)} %copy.65, s32[]{:T(128)S(6)} %select_n.265, s32[]{:T(128)} %constant.213.clone.1, s32[]{:T(128)} %constant.213.clone.1) | dynamic-update-slice | bytes 819204 | tf_op jit(solution)/shard_map/jit(dynamic_update_index_in_dim)/dynamic_update_slice | solution.py:175
  60.7 13.7 %dynamic_update_slice.174 = bf16[2,320,640]{2,0,1:T(2,128)(2,1)S(1)} dynamic-update-slice(bf16[2,320,640]{2,0,1:T(2,128)(2,1)S(1)} %dynamic_update_slice.173, bf16[1,320,640]{2,0,1:T(2,128)(2,1)} %copy.66, s32[]{:T(128)S(6)} %select_n.266, s32[]{:T(128)} %constant.213.clone.1, s32[]{:T(128)} %constant.213.clone.1) | dynamic-update-slice | bytes 819204 | tf_op jit(solution)/shard_map/jit(dynamic_update_index_in_dim)/dynamic_update_slice | solution.py:175
  128.5 8.0 collective-permute-start.6
  146.1 8.8 collective-permute-done.17
  174.4 11.5 %collective-permute-done.33 = bf16[160,2560]{1,0:T(8,128)(2,1)S(1)} collective-permute-done((bf16[160,2560]{1,0:T(8,128)(2,1)S(1)}, bf16[160,2560]{1,0:T(8,128)(2,1)S(1)}, u32[]{:S(2)}, u32[]{:S(2)}) %collective-permute-start.33) | collective-permute-done | bytes 819232 | tf_op jit(solution)/shard_map/ppermute | solution.py:184
  190.0 18.6 %collective-permute-done.28 = bf16[4,80,2560]{2,1,0:T(8,128)(2,1)} collective-permute-done((bf16[4,80,2560]{2,1,0:T(8,128)(2,1)}, bf16[4,80,2560]{2,1,0:T(8,128)(2,1)}, u32[]{:S(2)}, u32[]{:S(2)}) %collective-permute-start.28) | collective-permute-done | bytes 1638432 | tf_op jit(solution)/shard_map/ppermute | solution.py:138
  225.5 21.7 %collective-permute-done.10.refs_2_.refs_6_ = bf16[1280,512]{1,0:T(8,128)(2,1)S(1)} collective-permute-done((bf16[1280,512]{1,0:T(8,128)(2,1)S(1)}, bf16[1280,512]{1,0:T(8,128)(2,1)S(1)}, u32[]{:S(2)}, u32[]{:S(2)}) %collective-permute-start.10) | collective-permute-done | bytes 1310752 | tf_op jit(solution)/shard_map/ppermute | solution.py:138
  248.6 26.8 %collective-permute-done.39.refs_2_.refs_6_ = bf16[1280,512]{1,0:T(8,128)(2,1)S(1)} collective-permute-done((bf16[1280,512]{1,0:T(8,128)(2,1)S(1)}, bf16[1280,512]{1,0:T(8,128)(2,1)S(1)}, u32[]{:S(2)}, u32[]{:S(2)}) %collective-permute-start.39) | collective-permute-done | bytes 1310752 | tf_op jit(solution)/shard_map/ppermute | solution.py:138
  280.0 13.7 %attention_forward.2 = (bf16[640,512]{1,0:T(8,128)(2,1)S(1)}, bf16[8,2048,512]{2,1,0:T(8,128)(2,1)}, f32[8,8,512]{2,1,0:T(8,128)S(1)}) custom-call(s32[4]{0:T(128)S(1)} %subtract_clamp_fusion.1.valid_ref, bf16[640,512]{1,0:T(8,128)(2,1)S(1)} %slice.102.q_ref, bf16[1280,512]{1,0:T(8,128)(2,1)S(1)} %slice.103.refs_0_.refs_4_, ...), custom_call_target="tpu_custom_call" | custom-call | flops 8589934592 | bytes 16777216 | tf_op jit(solution)/shard_map/attention_forward/pallas_call | solution.py:67
  293.9 13.5 %attention_forward.3 = (bf16[640,512]{1,0:T(8,128)(2,1)S(1)}, bf16[8,2048,512]{2,1,0:T(8,128)(2,1)}, f32[8,8,512]{2,1,0:T(8,128)S(1)}) custom-call(s32[4]{0:T(128)S(1)} %subtract_clamp_fusion.valid_ref, bf16[640,512]{1,0:T(8,128)(2,1)S(1)} %slice.104.q_ref, bf16[1280,512]{1,0:T(8,128)(2,1)S(1)} %slice.105.refs_0_.refs_4_, ...), custom_call_target="tpu_custom_call" | custom-call | flops 8589934592 | bytes 16777216 | tf_op jit(solution)/shard_map/attention_forward/pallas_call | solution.py:67
  334.0 9.3 %convert_reduce_fusion.1 = (f32[2560]{0:T(1024)}, bf16[512,2560]{1,0:T(8,128)(2,1)}) fusion(f32[512,2560]{1,0:T(8,128)S(1)} %get-tuple-element.223, bf16[1280,2560]{1,0:T(8,128)(2,1)} %bitcast.282, bf16[2,1,512,1280]{3,2,1,0:T(8,128)(2,1)S(1)} %copy-done.25), kind=kOutput, calls=%fused_computation.32 | convolution fusion | flops 3371169280 | bytes 15738880 | tf_op jit(solution)/shard_map/dot_general | solution.py:20
  361.6 8.9 convert_reduce_fusion
  410.1 24.0 %collective-permute-done.48 = bf16[512,1280]{1,0:T(8,128)(2,1)} collective-permute-done((bf16[512,1280]{1,0:T(8,128)(2,1)}, bf16[512,1280]{1,0:T(8,128)(2,1)}, u32[]{:S(2)}, u32[]{:S(2)}) %collective-permute-start.48) | collective-permute-done | bytes 1310752 | tf_op jit(solution)/shard_map/ppermute | solution.py:138
  439.4 22.8 %collective-permute-done.42 = bf16[512,1280]{1,0:T(8,128)(2,1)S(1)} collective-permute-done((bf16[512,1280]{1,0:T(8,128)(2,1)S(1)}, bf16[512,1280]{1,0:T(8,128)(2,1)S(1)}, u32[]{:S(2)}, u32[]{:S(2)}) %collective-permute-start.42) | collective-permute-done | bytes 1310752 | tf_op jit(solution)/shard_map/ppermute | solution.py:138
  479.4 18.9 %attention_backward.3 = (bf16[640,512]{1,0:T(8,128)(2,1)S(1)}, bf16[640,512]{1,0:T(8,128)(2,1)S(1)}, bf16[640,512]{1,0:T(8,128)(2,1)S(1)}, bf16[640,512]{1,0:T(8...) custom-call(s32[4]{0:T(128)S(1)} %subtract_clamp_fusion.valid_ref, ...), custom_call_target="tpu_custom_call" | custom-call | flops 17179869184 | bytes 16777216 | tf_op jit(solution)/shard_map/attention_backward/pallas_call | solution.py:123
  500.7 18.5 %attention_backward.2 = (bf16[640,512]{1,0:T(8,128)(2,1)S(1)}, bf16[640,512]{1,0:T(8,128)(2,1)S(1)}, bf16[640,512]{1,0:T(8,128)(2,1)S(1)}, bf16[640,512]{1,0:T(8...) custom-call(s32[4]{0:T(128)S(1)} %copy-done.19, ...), custom_call_target="tpu_custom_call" | custom-call | flops 17179869184 | bytes 16777216 | tf_op jit(solution)/shard_map/attention_backward/pallas_call | solution.py:123
  555.8 32.9 %collective-permute-done.74 = bf16[320,160]{0,1:T(8,128)(2,1)S(1)} collective-permute-done((bf16[320,160]{0,1:T(8,128)(2,1)S(1)}, bf16[320,160]{0,1:T(8,128)(2,1)S(1)}, u32[]{:S(2)}, u32[]{:S(2)}) %collective-permute-start.74) | collective-permute-done | bytes 102432 | tf_op jit(solution)/shard_map/ppermute | solution.py:138
  602.5 25.2 %collective-permute-done.87 = bf16[1280,640]{1,0:T(8,128)(2,1)} collective-permute-done((bf16[1280,640]{1,0:T(8,128)(2,1)}, bf16[1280,640]{1,0:T(8,128)(2,1)}, u32[]{:S(2)}, u32[]{:S(2)}) %collective-permute-start.87) | collective-permute-done | bytes 1638432 | tf_op jit(solution)/shard_map/ppermute | solution.py:138
  642.5 9.5 %collective-permute-done.90 = bf16[320,640]{1,0:T(8,128)(2,1)S(1)} collective-permute-done((bf16[320,640]{1,0:T(8,128)(2,1)S(1)}, bf16[320,640]{1,0:T(8,128)(2,1)S(1)}, u32[]{:S(2)}, u32[]{:S(2)}) %collective-permute-start.90) | collective-permute-done | bytes 409632 | tf_op jit(solution)/shard_map/ppermute | solution.py:226
  652.0 8.0 collective-permute-start.44
  681.4 8.6 collective-permute-done.46
  696.0 10.8 %maximum_maximum_fusion = bf16[1920,1024]{1,0:T(8,128)(2,1)S(1)} fusion(bf16[1280,512]{1,0:T(8,128)(2,1)S(1)} %add_convert_fusion.3, bf16[640,512]{1,0:T(8,128)(2,1)S(1)} %get-tuple-element.56, bf16[1280,512]{1,0:T(8,128)(2,1)S(1)} %add_convert_fusion.7, bf16[640,512]{1,0:T(8,128)(2,1)S(1)} %copy-done.5), kind=kLoop, calls=%fused_computation.39 | loop fusion | flops 15728640 | bytes 7864320 | tf_op jit(solution)/shard_map/concatenate | solution.py:353
  710.4 8.4 collective-permute-start.84
  722.7 15.7 %dynamic_update_slice.208 = bf16[4,320,640]{2,0,1:T(4,128)(2,1)S(1)} dynamic-update-slice(bf16[4,320,640]{2,0,1:T(4,128)(2,1)S(1)} %copy.74, bf16[1,320,640]{2,0,1:T(2,128)(2,1)} %copy.75, s32[]{:T(128)S(6)} %select_n.300, s32[]{:T(128)} %constant.213.clone.1, s32[]{:T(128)} %constant.213.clone.1) | dynamic-update-slice | bytes 819204 | tf_op jit(solution)/shard_map/jit(dynamic_update_index_in_dim)/dynamic_update_slice | solution.py:175
  744.4 13.3 %collective-permute-done.47 = bf16[512,1280]{1,0:T(8,128)(2,1)} collective-permute-done((bf16[512,1280]{1,0:T(8,128)(2,1)}, bf16[512,1280]{1,0:T(8,128)(2,1)}, u32[]{:S(2)}, u32[]{:S(2)}) %collective-permute-start.47) | collective-permute-done | bytes 1310752 | tf_op jit(solution)/shard_map/ppermute | solution.py:138
  764.5 8.7 collective-permute-start.59
  785.6 17.1 %collective-permute-start.56 = (f32[11520]{0:T(1024)S(1)}, f32[11520]{0:T(1024)S(1)}, u32[]{:S(2)}, u32[]{:S(2)}) collective-permute-start(f32[11520]{0:T(1024)S(1)} %add.577), channel_id=1, source_target_pairs={{0,8},{8,0},{16,24},{24,16},{1,9},{9,1},{17,25},{25,17},{2,10},{10... | collective-permute-start | bytes 138248 | tf_op jit(solution)/shard_map/ppermute | solution.py:138
  810.2 17.1 %collective-permute-start.63 = (bf16[320,480]{0,1:T(8,128)(2,1)S(1)}, bf16[320,480]{0,1:T(8,128)(2,1)S(1)}, u32[]{:S(2)}, u32[]{:S(2)}) collective-permute-start(bf16[320,480]{0,1:T(8,128)(2,1)S(1)} %get-tuple-element.196), channel_id=1, source_target_pairs={{0,24},{8,0},{16,8},{24,16},{1,25},{9,1},{17,9},{25,17},{2,26},{10... | collective-permute-start | bytes 921608 | tf_op jit(solution)/shard_map/ppermute | solution.py:226
  834.2 17.0 %collective-permute-done.62 = bf16[320,480]{0,1:T(8,128)(2,1)S(1)} collective-permute-done((bf16[320,480]{0,1:T(8,128)(2,1)S(1)}, bf16[320,480]{0,1:T(8,128)(2,1)S(1)}, u32[]{:S(2)}, u32[]{:S(2)}) %collective-permute-start.62) | collective-permute-done | bytes 307232 | tf_op jit(solution)/shard_map/ppermute | solution.py:226
  851.1 7.9 collective-permute-done.61
  862.3 8.1 collective-permute-done.65
  874.8 12.5 %dynamic_update_slice.200 = bf16[4,320,480]{2,0,1:T(4,128)(2,1)} dynamic-update-slice(bf16[4,320,480]{2,0,1:T(4,128)(2,1)} %copy.72, bf16[1,320,480]{2,0,1:T(2,128)(2,1)S(1)} %copy.73, s32[]{:T(128)S(6)} %select_n.300, s32[]{:T(128)} %constant.213.clone.1, s32[]{:T(128)} %constant.213.clone.1) | dynamic-update-slice | bytes 614404 | tf_op jit(solution)/shard_map/jit(dynamic_update_index_in_dim)/dynamic_update_slice | solution.py:175
  (549 shorter events, 419.5 us)
Async XLA Ops:
  3.8 43.1 %collective-permute-start = (bf16[80,1920]{1,0:T(8,128)(2,1)}, bf16[80,1920]{1,0:T(8,128)(2,1)}, u32[]{:S(2)}, u32[]{:S(2)}) collective-permute-start(bf16[80,1920]{1,0:T(8,128)(2,1)} %get-tuple-element.167), channel_id=1, source_target_pairs={{0,8},{8,16},{16,24},{1,9},{9,17},{17,25},{2,10},{10,18},{18,26},{... | collective-permute-start | bytes 921608 | tf_op jit(solution)/shard_map/ppermute | solution.py:183
  13.0 77.3 %collective-permute-start.21 = (bf16[80,2560]{1,0:T(8,128)(2,1)}, bf16[80,2560]{1,0:T(8,128)(2,1)}, u32[]{:S(2)}, u32[]{:S(2)}) collective-permute-start(bf16[80,2560]{1,0:T(8,128)(2,1)} %get-tuple-element.163), channel_id=1, source_target_pairs={{0,8},{8,16},{16,24},{1,9},{9,17},{17,25},{2,10},{10,18},{18,26},{... | collective-permute-start | bytes 1228808 | tf_op jit(solution)/shard_map/ppermute | solution.py:183
  15.5 67.7 %collective-permute-start.22 = (bf16[80,2560]{1,0:T(8,128)(2,1)}, bf16[80,2560]{1,0:T(8,128)(2,1)}, u32[]{:S(2)}, u32[]{:S(2)}) collective-permute-start(bf16[80,2560]{1,0:T(8,128)(2,1)} %get-tuple-element.163), channel_id=1, source_target_pairs={{24,16},{16,8},{8,0},{25,17},{17,9},{9,1},{26,18},{18,10},{10,2},{... | collective-permute-start | bytes 1228808 | tf_op jit(solution)/shard_map/ppermute | solution.py:184
  56.2 60.2 %collective-permute-start.30 = (bf16[160,2560]{1,0:T(8,128)(2,1)}, bf16[160,2560]{1,0:T(8,128)(2,1)}, u32[]{:S(2)}, u32[]{:S(2)}) collective-permute-start(bf16[160,2560]{1,0:T(8,128)(2,1)} %get-tuple-element.161), channel_id=1, source_target_pairs={{0,8},{8,16},{16,24},{1,9},{9,17},{17,25},{2,10},{10,18},{18,26},{... | collective-permute-start | bytes 2457608 | tf_op jit(solution)/shard_map/ppermute | solution.py:183
  74.7 42.4 %collective-permute-start.31 = (bf16[160,2560]{1,0:T(8,128)(2,1)}, bf16[160,2560]{1,0:T(8,128)(2,1)S(1)}, u32[]{:S(2)}, u32[]{:S(2)}) collective-permute-start(bf16[160,2560]{1,0:T(8,128)(2,1)} %get-tuple-element.161), channel_id=1, source_target_pairs={{24,16},{16,8},{8,0},{25,17},{17,9},{9,1},{26,18},{18,10},{10,2},{... | collective-permute-start | bytes 2457608 | tf_op jit(solution)/shard_map/ppermute | solution.py:184
  117.1 46.2 %collective-permute-start.32 = (bf16[160,2560]{1,0:T(8,128)(2,1)S(1)}, bf16[160,2560]{1,0:T(8,128)(2,1)S(1)}, u32[]{:S(2)}, u32[]{:S(2)}) collective-permute-start(bf16[160,2560]{1,0:T(8,128)(2,1)S(1)} %collective-permute-done.31), channel_id=1, source_target_pairs={{16,8},{8,0},{17,9},{9,1},{18,10},{10,2},{19,11},{11,3},{20,12},{1... | collective-permute-start | bytes 2457608 | tf_op jit(solution)/shard_map/ppermute | solution.py:184
  119.7 49.1 %collective-permute-start.34 = (bf16[160,2560]{1,0:T(8,128)(2,1)}, bf16[160,2560]{1,0:T(8,128)(2,1)S(1)}, u32[]{:S(2)}, u32[]{:S(2)}) collective-permute-start(bf16[160,2560]{1,0:T(8,128)(2,1)} %collective-permute-done.30), channel_id=1, source_target_pairs={{8,16},{16,24},{9,17},{17,25},{10,18},{18,26},{11,19},{19,27},{12,... | collective-permute-start | bytes 2457608 | tf_op jit(solution)/shard_map/ppermute | solution.py:183
  155.8 53.9 %collective-permute-start.27 = (bf16[4,80,2560]{2,1,0:T(8,128)(2,1)}, bf16[4,80,2560]{2,1,0:T(8,128)(2,1)S(1)}, u32[]{:S(2)}, u32[]{:S(2)}) collective-permute-start(bf16[4,80,2560]{2,1,0:T(8,128)(2,1)} %bitcast_dynamic-update-slice_fusion.27), channel_id=1, source_target_pairs={{0,2},{2,0},{4,6},{6,4},{1,3},{3,1},{5,7},{7,5},{8,10},{10,8},{12,... | collective-permute-start | bytes 4915208 | tf_op jit(solution)/shard_map/ppermute | solution.py:138
  163.3 45.3 %collective-permute-start.28 = (bf16[4,80,2560]{2,1,0:T(8,128)(2,1)}, bf16[4,80,2560]{2,1,0:T(8,128)(2,1)}, u32[]{:S(2)}, u32[]{:S(2)}) collective-permute-start(bf16[4,80,2560]{2,1,0:T(8,128)(2,1)} %bitcast_dynamic-update-slice_fusion.27), channel_id=1, source_target_pairs={{0,4},{2,6},{4,0},{6,2},{1,5},{3,7},{5,1},{7,3},{8,12},{10,14},{12... | collective-permute-start | bytes 4915208 | tf_op jit(solution)/shard_map/ppermute | solution.py:138
  168.9 53.1 %collective-permute-start.20 = (bf16[4,160,1280]{2,1,0:T(8,128)(2,1)S(1)}, bf16[4,160,1280]{2,1,0:T(8,128)(2,1)}, u32[]{:S(2)}, u32[]{:S(2)}) collective-permute-start(bf16[4,160,1280]{2,1,0:T(8,128)(2,1)S(1)} %bitcast_dynamic-update-slice_fusion.31), channel_id=1, source_target_pairs={{0,2},{2,0},{4,6},{6,4},{1,3},{3,1},{5,7},{7,5},{8,10},{10,8},{12,... | collective-permute-start | bytes 4915208 | tf_op jit(solution)/shard_map/ppermute | solution.py:138
  188.9 87.1 %collective-permute-start.36 = (bf16[4,160,2560]{2,1,0:T(8,128)(2,1)S(1)}, bf16[4,160,2560]{2,1,0:T(8,128)(2,1)}, u32[]{:S(2)}, u32[]{:S(2)}) collective-permute-start(bf16[4,160,2560]{2,1,0:T(8,128)(2,1)S(1)} %bitcast_dynamic-update-slice_fusion.12), channel_id=1, source_target_pairs={{0,2},{2,0},{4,6},{6,4},{1,3},{3,1},{5,7},{7,5},{8,10},{10,8},{12,... | collective-permute-start | bytes 9830408 | tf_op jit(solution)/shard_map/ppermute | solution.py:138
  221.7 53.7 %collective-permute-start.39 = (bf16[1280,512]{1,0:T(8,128)(2,1)S(1)}, bf16[1280,512]{1,0:T(8,128)(2,1)S(1)}, u32[]{:S(2)}, u32[]{:S(2)}) collective-permute-start(bf16[1280,512]{1,0:T(8,128)(2,1)S(1)} %slice.105.refs_0_.refs_4_), channel_id=1, source_target_pairs={{0,4},{2,6},{4,0},{6,2},{1,5},{3,7},{5,1},{7,3},{8,12},{10,14},{12... | collective-permute-start | bytes 3932168 | tf_op jit(solution)/shard_map/ppermute | solution.py:138
  224.7 55.2 %collective-permute-start.9 = (bf16[1280,512]{1,0:T(8,128)(2,1)S(1)}, bf16[1280,512]{1,0:T(8,128)(2,1)S(1)}, u32[]{:S(2)}, u32[]{:S(2)}) collective-permute-start(bf16[1280,512]{1,0:T(8,128)(2,1)S(1)} %slice.103.refs_0_.refs_4_), channel_id=1, source_target_pairs={{0,2},{2,0},{4,6},{6,4},{1,3},{3,1},{5,7},{7,5},{8,10},{10,8},{12,... | collective-permute-start | bytes 3932168 | tf_op jit(solution)/shard_map/ppermute | solution.py:138
  225.4 68.5 %collective-permute-start.38 = (bf16[1280,512]{1,0:T(8,128)(2,1)S(1)}, bf16[1280,512]{1,0:T(8,128)(2,1)S(1)}, u32[]{:S(2)}, u32[]{:S(2)}) collective-permute-start(bf16[1280,512]{1,0:T(8,128)(2,1)S(1)} %slice.105.refs_0_.refs_4_), channel_id=1, source_target_pairs={{0,2},{2,0},{4,6},{6,4},{1,3},{3,1},{5,7},{7,5},{8,10},{10,8},{12,... | collective-permute-start | bytes 3932168 | tf_op jit(solution)/shard_map/ppermute | solution.py:138
  348.6 61.0 %collective-permute-start.43 = (bf16[512,1280]{1,0:T(8,128)(2,1)S(1)}, bf16[512,1280]{1,0:T(8,128)(2,1)}, u32[]{:S(2)}, u32[]{:S(2)}) collective-permute-start(bf16[512,1280]{1,0:T(8,128)(2,1)S(1)} %convolution_convert_fusion.5), channel_id=1, source_target_pairs={{0,1},{1,0},{2,3},{3,2},{4,5},{5,4},{6,7},{7,6},{8,9},{9,8},{10,11... | collective-permute-start | bytes 3932168 | tf_op jit(solution)/shard_map/ppermute | solution.py:138
  357.1 52.6 %collective-permute-start.37 = (bf16[512,1280]{1,0:T(8,128)(2,1)}, bf16[512,1280]{1,0:T(8,128)(2,1)}, u32[]{:S(2)}, u32[]{:S(2)}) collective-permute-start(bf16[512,1280]{1,0:T(8,128)(2,1)} %convolution_convert_fusion.7), channel_id=1, source_target_pairs={{0,1},{1,0},{2,3},{3,2},{4,5},{5,4},{6,7},{7,6},{8,9},{9,8},{10,11... | collective-permute-start | bytes 3932168 | tf_op jit(solution)/shard_map/ppermute | solution.py:138
  377.0 57.1 %collective-permute-start.48 = (bf16[512,1280]{1,0:T(8,128)(2,1)}, bf16[512,1280]{1,0:T(8,128)(2,1)}, u32[]{:S(2)}, u32[]{:S(2)}) collective-permute-start(bf16[512,1280]{1,0:T(8,128)(2,1)} %convolution_convert_fusion.4), channel_id=1, source_target_pairs={{0,1},{1,0},{2,3},{3,2},{4,5},{5,4},{6,7},{7,6},{8,9},{9,8},{10,11... | collective-permute-start | bytes 3932168 | tf_op jit(solution)/shard_map/ppermute | solution.py:138
  384.6 77.5 %collective-permute-start.42 = (bf16[512,1280]{1,0:T(8,128)(2,1)S(1)}, bf16[512,1280]{1,0:T(8,128)(2,1)S(1)}, u32[]{:S(2)}, u32[]{:S(2)}) collective-permute-start(bf16[512,1280]{1,0:T(8,128)(2,1)S(1)} %convolution_convert_fusion.6), channel_id=1, source_target_pairs={{0,1},{1,0},{2,3},{3,2},{4,5},{5,4},{6,7},{7,6},{8,9},{9,8},{10,11... | collective-permute-start | bytes 3932168 | tf_op jit(solution)/shard_map/ppermute | solution.py:138
  388.6 147.7 %collective-permute-start.77 = (bf16[1280,640]{1,0:T(8,128)(2,1)}, bf16[1280,640]{1,0:T(8,128)(2,1)}, u32[]{:S(2)}, u32[]{:S(2)}) collective-permute-start(bf16[1280,640]{1,0:T(8,128)(2,1)} %convolution_convert_fusion.2), channel_id=1, source_target_pairs={{0,2},{2,0},{4,6},{6,4},{1,3},{3,1},{5,7},{7,5},{8,10},{10,8},{12,... | collective-permute-start | bytes 4915208 | tf_op jit(solution)/shard_map/ppermute | solution.py:138
  409.6 188.4 %collective-permute-start.76 = (bf16[1280,640]{1,0:T(8,128)(2,1)}, bf16[1280,640]{1,0:T(8,128)(2,1)}, u32[]{:S(2)}, u32[]{:S(2)}) collective-permute-start(bf16[1280,640]{1,0:T(8,128)(2,1)} %convolution_convert_fusion.3), channel_id=1, source_target_pairs={{0,2},{2,0},{4,6},{6,4},{1,3},{3,1},{5,7},{7,5},{8,10},{10,8},{12,... | collective-permute-start | bytes 4915208 | tf_op jit(solution)/shard_map/ppermute | solution.py:138
  409.7 140.5 %collective-permute-start.86 = (bf16[1280,640]{1,0:T(8,128)(2,1)}, bf16[1280,640]{1,0:T(8,128)(2,1)}, u32[]{:S(2)}, u32[]{:S(2)}) collective-permute-start(bf16[1280,640]{1,0:T(8,128)(2,1)} %convolution_convert_fusion), channel_id=1, source_target_pairs={{0,2},{2,0},{4,6},{6,4},{1,3},{3,1},{5,7},{7,5},{8,10},{10,8},{12,... | collective-permute-start | bytes 4915208 | tf_op jit(solution)/shard_map/ppermute | solution.py:138
  476.7 44.9 %collective-permute-start.68 = (bf16[1280,160]{0,1:T(8,128)(2,1)}, bf16[1280,160]{0,1:T(8,128)(2,1)}, u32[]{:S(2)}, u32[]{:S(2)}) collective-permute-start(bf16[1280,160]{0,1:T(8,128)(2,1)} %convolution_convert_fusion.10), channel_id=1, source_target_pairs={{0,2},{2,0},{4,6},{6,4},{1,3},{3,1},{5,7},{7,5},{8,10},{10,8},{12,... | collective-permute-start | bytes 1228808 | tf_op jit(solution)/shard_map/ppermute | solution.py:138
  479.3 49.5 %collective-permute-start.67 = (bf16[1280,160]{0,1:T(8,128)(2,1)S(1)}, bf16[1280,160]{0,1:T(8,128)(2,1)S(1)}, u32[]{:S(2)}, u32[]{:S(2)}) collective-permute-start(bf16[1280,160]{0,1:T(8,128)(2,1)S(1)} %convolution_convert_fusion.11), channel_id=1, source_target_pairs={{0,2},{2,0},{4,6},{6,4},{1,3},{3,1},{5,7},{7,5},{8,10},{10,8},{12,... | collective-permute-start | bytes 1228808 | tf_op jit(solution)/shard_map/ppermute | solution.py:138
  544.4 50.7 %collective-permute-start.50 = (bf16[1280,512]{1,0:T(8,128)(2,1)}, bf16[1280,512]{1,0:T(8,128)(2,1)}, u32[]{:S(2)}, u32[]{:S(2)}) collective-permute-start(bf16[1280,512]{1,0:T(8,128)(2,1)} %pad_maximum_fusion.7), channel_id=1, source_target_pairs={{0,2},{2,0},{4,6},{6,4},{1,3},{3,1},{5,7},{7,5},{8,10},{10,8},{12,... | collective-permute-start | bytes 3932168 | tf_op jit(solution)/shard_map/ppermute | solution.py:138
  548.4 49.8 %collective-permute-start.78 = (bf16[1280,640]{1,0:T(8,128)(2,1)}, bf16[1280,640]{1,0:T(8,128)(2,1)}, u32[]{:S(2)}, u32[]{:S(2)}) collective-permute-start(bf16[1280,640]{1,0:T(8,128)(2,1)} %add_convert_fusion.1), channel_id=1, source_target_pairs={{0,4},{2,6},{4,0},{6,2},{1,5},{3,7},{5,1},{7,3},{8,12},{10,14},{12... | collective-permute-start | bytes 4915208 | tf_op jit(solution)/shard_map/ppermute | solution.py:138
  550.2 38.5 %collective-permute-start.74 = (bf16[320,160]{0,1:T(8,128)(2,1)S(1)}, bf16[320,160]{0,1:T(8,128)(2,1)S(1)}, u32[]{:S(2)}, u32[]{:S(2)}) collective-permute-start(bf16[320,160]{0,1:T(8,128)(2,1)S(1)} %get-tuple-element.149), channel_id=1, source_target_pairs={{0,4},{2,6},{4,0},{6,2},{1,5},{3,7},{5,1},{7,3},{8,12},{10,14},{12... | collective-permute-start | bytes 307208 | tf_op jit(solution)/shard_map/ppermute | solution.py:138
  555.3 46.0 %collective-permute-start.85 = (bf16[1280,640]{1,0:T(8,128)(2,1)}, bf16[1280,640]{1,0:T(8,128)(2,1)}, u32[]{:S(2)}, u32[]{:S(2)}) collective-permute-start(bf16[1280,640]{1,0:T(8,128)(2,1)} %convolution_convert_fusion.1), channel_id=1, source_target_pairs={{0,2},{2,0},{4,6},{6,4},{1,3},{3,1},{5,7},{7,5},{8,10},{10,8},{12,... | collective-permute-start | bytes 4915208 | tf_op jit(solution)/shard_map/ppermute | solution.py:138
  598.1 75.8 %collective-permute-start.49 = (bf16[1280,512]{1,0:T(8,128)(2,1)}, bf16[1280,512]{1,0:T(8,128)(2,1)S(1)}, u32[]{:S(2)}, u32[]{:S(2)}) collective-permute-start(bf16[1280,512]{1,0:T(8,128)(2,1)} %pad_maximum_fusion.6), channel_id=1, source_target_pairs={{0,2},{2,0},{4,6},{6,4},{1,3},{3,1},{5,7},{7,5},{8,10},{10,8},{12,... | collective-permute-start | bytes 3932168 | tf_op jit(solution)/shard_map/ppermute | solution.py:138
  598.2 77.0 %collective-permute-start.51 = (bf16[1280,512]{1,0:T(8,128)(2,1)S(1)}, bf16[1280,512]{1,0:T(8,128)(2,1)S(1)}, u32[]{:S(2)}, u32[]{:S(2)}) collective-permute-start(bf16[1280,512]{1,0:T(8,128)(2,1)S(1)} %add_convert_fusion.4), channel_id=1, source_target_pairs={{0,4},{2,6},{4,0},{6,2},{1,5},{3,7},{5,1},{7,3},{8,12},{10,14},{12... | collective-permute-start | bytes 3932168 | tf_op jit(solution)/shard_map/ppermute | solution.py:138
  675.1 43.8 %collective-permute-start.91 = (bf16[320,640]{1,0:T(8,128)(2,1)S(1)}, bf16[320,640]{1,0:T(8,128)(2,1)S(1)}, u32[]{:S(2)}, u32[]{:S(2)}) collective-permute-start(bf16[320,640]{1,0:T(8,128)(2,1)S(1)} %get-tuple-element.141), channel_id=1, source_target_pairs={{0,2},{2,0},{4,6},{6,4},{1,3},{3,1},{5,7},{7,5},{8,10},{10,8},{12,... | collective-permute-start | bytes 1228808 | tf_op jit(solution)/shard_map/ppermute | solution.py:138
  680.4 38.4 %collective-permute-start.92 = (bf16[320,640]{1,0:T(8,128)(2,1)S(1)}, bf16[320,640]{1,0:T(8,128)(2,1)}, u32[]{:S(2)}, u32[]{:S(2)}) collective-permute-start(bf16[320,640]{1,0:T(8,128)(2,1)S(1)} %get-tuple-element.141), channel_id=1, source_target_pairs={{0,4},{2,6},{4,0},{6,2},{1,5},{3,7},{5,1},{7,3},{8,12},{10,14},{12... | collective-permute-start | bytes 1228808 | tf_op jit(solution)/shard_map/ppermute | solution.py:138
  708.4 49.3 %collective-permute-start.47 = (bf16[512,1280]{1,0:T(8,128)(2,1)}, bf16[512,1280]{1,0:T(8,128)(2,1)}, u32[]{:S(2)}, u32[]{:S(2)}) collective-permute-start(bf16[512,1280]{1,0:T(8,128)(2,1)} %get-tuple-element.228), channel_id=1, source_target_pairs={{0,1},{1,0},{2,3},{3,2},{4,5},{5,4},{6,7},{7,6},{8,9},{9,8},{10,11... | collective-permute-start | bytes 3932168 | tf_op jit(solution)/shard_map/ppermute | solution.py:138
  (161 other events, 3287.9 us)

commit v2 on v1

--- a/solution.py
+++ b/solution.py
@@ -19,63 +19,375 @@
 def contract(left, right, dims):
     return lax.dot_general(left, right, (dims, ((), ())), preferred_element_type=jnp.float32)
 
-def forward_kernel(valid_ref, q_ref, *refs, blocks, heads):
-    k_refs, v_refs = refs[:blocks], refs[blocks:2*blocks]
-    a_ref, e_ref, inverse_ref, s0_ref, s1_ref, m0_ref, m1_ref, acc_ref, l_ref = refs[2*blocks:]
-    h = pl.program_id(0)
-    q = q_ref[...]
-    span = k_refs[0].shape[1]
-    acc_ref[...] = jnp.zeros(acc_ref.shape, jnp.float32)
-    l_ref[...] = jnp.zeros(l_ref.shape, jnp.float32)
-    step=min(STEP,span)
-    def go(s_now, m_now, s_before, m_before):
-        m_now[...] = jnp.full(m_now.shape, -1e30, jnp.float32)
-        m_last = m_before[...]
-        for b in range(blocks):
-            for off in range(0, span, step):
-                left = valid_ref[b] - off
-                def work():
-                    rows = slice(b*span+off, b*span+off+step)
-                    s = contract(k_refs[b][:, off:off+step], q, ((0,), (0,)))
-                    e = jnp.exp2(s_before[rows] - m_last)
-                    row = lax.broadcasted_iota(jnp.int32, (step, 1), 0)
-                    s = jnp.where(row < left, s, -1e30)
-                    s_now[rows] = s
-                    m_now[...] = jnp.maximum(m_now[...], jnp.max(s, axis=0, keepdims=True))
-                    l_ref[...] += jnp.sum(e, axis=0, keepdims=True)
-                    low = e.astype(jnp.bfloat16)
-                    e_ref[0, rows] = low
-                    acc_ref[...] += contract(v_refs[b][:, off:off+step], low, ((1,), (0,)))
-                work()
-    @pl.when(lax.rem(h, 2) == 0)
-    def _():
-        go(s0_ref, m0_ref, s1_ref, m1_ref)
-    @pl.when(lax.rem(h, 2) == 1)
-    def _():
-        go(s1_ref, m1_ref, s0_ref, m0_ref)
-    inverse = 1.0 / l_ref[...]
-    a_ref[...] = (acc_ref[...] * inverse).astype(jnp.bfloat16)
-    inverse_ref[0] = jnp.broadcast_to(inverse, inverse_ref.shape[1:])
-
-def attention_forward(valid, q, kv):
-    width, rows = q.shape
+class Weight:
+    def __init__(self, index, piece, full, shard, split, ctx_index):
+        self.index, self.piece, self.full, self.split = index, piece, full, split
+        self.each = full.shape[-2] // shard
+        self.rows = self.each // split
+        self.part = lax.rem(ctx_index, split)
+
+    def slice(self, shard_index, part):
+        rows = pl.ds(pl.multiple_of(shard_index * self.each + part * self.rows, 16), self.rows)
+        return self.full.at[:, rows] if len(self.full.shape) == 3 else self.full.at[rows]
+
+
+def flip(index, bit):
+    return index + bit - 2 * bit * lax.rem(index // bit, 2)
+
+
+def opening_kernel(
+    sizes,
+    valid_ref,
+    normed_ref,
+    bias_ref,
+    qkv_ref,
+    out_ref,
+    up_ref,
+    down_ref,
+    full_qkv,
+    full_out,
+    full_up,
+    full_down,
+    q_ref,
+    kv_ref,
+    a_ref,
+    e_ref,
+    inverse_ref,
+    weights_ref,
+    pairs_ref,
+    mine_ref,
+    s_ref,
+    low_ref,
+    z_send,
+    z_recv,
+    x_send,
+    x_recv,
+    c_send,
+    c_recv,
+    y_send,
+    y_recv,
+    kv_send,
+    kv_recv,
+    a_send,
+    a_recv,
+    own_sem,
+    e_sem,
+    last_sem,
+):
+    shard, ctx, tp = sizes
+    width, rows = q_ref.shape[1], q_ref.shape[2]
     heads = width // HEAD_DIM
-    blocks, span = len(kv), kv[0].shape[1]
-    head = lambda h: (jnp.minimum(h, heads-1), 0)
-    last = lambda h: (jnp.maximum(h-1, 0), 0)
-    value = lambda h: (heads + jnp.maximum(h-1, 0), 0)
+    i, p, me = lax.axis_index("shard"), lax.axis_index("ctx"), lax.axis_index("tp")
+    across, beside = flip(p, 2), flip(p, 1)
+
+    def remote(source, target, send, recv, **device):
+        return pltpu.make_async_remote_copy(
+            src_ref=source, dst_ref=target, send_sem=send, recv_sem=recv,
+            device_id=device, device_id_type=pl.DeviceIdType.MESH,
+        )
+
+    def others():
+        return [lax.rem(me + d, tp) for d in range(1, tp)]
+
+    barrier = pltpu.get_barrier_semaphore()
+
+    def greet(**device):
+        pl.semaphore_signal(barrier, inc=1, device_id=device, device_id_type=pl.DeviceIdType.MESH)
+
+    pl.when(i > 0)(lambda: greet(shard=i - 1))
+    pl.when(i < shard - 1)(lambda: greet(shard=i + 1))
+    greet(ctx=across)
+    greet(ctx=beside)
+    for other in others():
+        greet(tp=other)
+    pl.semaphore_wait(barrier, 2 + (tp - 1) + jnp.where(i > 0, 1, 0) + jnp.where(i < shard - 1, 1, 0))
+
+    qkv = Weight(0, qkv_ref, weights_ref, shard, 4, p)
+    out = Weight(1, out_ref, full_out, shard, 4, p)
+    up = Weight(2, up_ref, full_up, shard, 4, p)
+    down = Weight(3, down_ref, full_down, shard, 2, p)
+    everything = (qkv, out, up, down)
+
+    def z_copy(w, j, way):
+        there = w.slice(j, w.part)
+        return remote(there, there, z_send.at[w.index, (way + 1) // 2, j], z_recv.at[w.index, j], shard=i + way)
+
+    def x_copy(w, j):
+        there = w.slice(j, w.part)
+        return remote(there, there, x_send.at[w.index, j], x_recv.at[w.index, j], ctx=across)
+
+    def c_copy(w, j, which):
+        there = w.slice(j, flip(w.part, 2) if which else w.part)
+        return remote(there, there, c_send.at[w.index, j, which], c_recv.at[w.index, j, which], ctx=beside)
+
+    def x_arriving(w, j):
+        there = w.slice(j, flip(w.part, 2))
+        return remote(there, there, x_send.at[w.index, j], x_recv.at[w.index, j], ctx=across)
+
+    def c_arriving(w, j, which):
+        there = w.slice(j, flip(flip(w.part, 2) if which else w.part, 1))
+        return remote(there, there, c_send.at[w.index, j, which], c_recv.at[w.index, j, which], ctx=beside)
+
+    def share(w, j):
+        if w.split == 4:
+            x_copy(w, j).start()
+        c_copy(w, j, 0).start()
+
+    def begin(w):
+        pl.when(i < shard - 1)(lambda: z_copy(w, i, 1).start())
+        pl.when(i > 0)(lambda: z_copy(w, i, -1).start())
+        share(w, i)
+
+    def arrive(w, hop):
+        for way, there, j in ((1, i >= hop, i - hop), (-1, i + hop < shard, i + hop)):
+
+            @pl.when(there)
+            def _():
+                z_copy(w, j, way).wait_recv()
+                onward = (i < shard - 1) if way == 1 else (i > 0)
+                pl.when(onward)(lambda: z_copy(w, j, way).start())
+                share(w, j)
+
+    def cross(w):
+        def one(j, carry):
+            x_arriving(w, j).wait_recv()
+            c_copy(w, j, 1).start()
+            return carry
+
+        if w.split == 4:
+            lax.fori_loop(0, shard, one, 0)
+
+    def settle(w):
+        def one(j, carry):
+            c_arriving(w, j, 0).wait_recv()
+            if w.split == 4:
+                c_arriving(w, j, 1).wait_recv()
+            return carry
+
+        lax.fori_loop(0, shard, one, 0)
+
+    def drain(w):
+        def one(j, carry):
+            pl.when((j <= i) & (i < shard - 1))(lambda: z_copy(w, j, 1).wait_send())
+            pl.when((j >= i) & (i > 0))(lambda: z_copy(w, j, -1).wait_send())
+            c_copy(w, j, 0).wait_send()
+            if w.split == 4:
+                x_copy(w, j).wait_send()
+                c_copy(w, j, 1).wait_send()
+            return carry
+
+        lax.fori_loop(0, shard, one, 0)
+
+    def own_copy(w):
+        source = w.piece.at[pl.ds(pl.multiple_of(w.part * w.rows, 16), w.rows)]
+        target = w.slice(i, w.part)
+        if w is out:
+            target = target.at[me]
+        return pltpu.make_async_copy(source, target, own_sem.at[w.index])
+
+    for w in everything:
+        own_copy(w).start()
+    own_copy(qkv).wait()
+    begin(qkv)
+
+    def y_copy(source_me, other, slot):
+        there = out.slice(i, out.part).at[source_me]
+        return remote(there, there, y_send.at[slot], y_recv.at[slot], tp=other)
+
+    own_copy(out).wait()
+    for d in range(1, tp):
+        y_copy(me, lax.rem(me + d, tp), d).start()
+    own_copy(up).wait()
+    own_copy(down).wait()
+    for hop in range(1, shard):
+        if hop == shard - 1:
+            for d in range(1, tp):
+                y_copy(lax.rem(me + tp - d, tp), lax.rem(me + tp - d, tp), d).wait_recv()
+            begin(out)
+            begin(up)
+        arrive(qkv, hop)
+    cross(qkv)
+    settle(qkv)
+    keep_qkv = pltpu.make_async_copy(weights_ref, full_qkv, last_sem.at[0])
+    keep_qkv.start()
+
+    def project(m):
+        columns = slice(m * rows, (m + 1) * rows)
+        for which in range(3):
+            for low in range(0, width, 256):
+                high = min(width, low + 256)
+                picked = slice(which * width + low, which * width + high)
+                value = contract(weights_ref[:, picked], normed_ref[:, columns], ((0,), (0,))) + bias_ref[picked, 0:1]
+                if which == 0:
+                    q_ref[m, low:high] = (value * (SCALE * math.log2(math.e))).astype(LOW)
+                else:
+                    pairs_ref[m, 0, (which - 1) * width + low : (which - 1) * width + high] = value.astype(LOW)
+
+    def kv_copy(m, source, target, to):
+        return remote(
+            pairs_ref.at[m, source], pairs_ref.at[m, target], kv_send.at[m, target - 1], kv_recv.at[m, target - 1], ctx=to
+        )
+
+    def send_pair(m):
+        kv_copy(m, 0, 2, across).start()
+        kv_copy(m, 0, 1, beside).start()
+
+    def take_pair(m):
+        kv_copy(m, 0, 2, across).wait_recv()
+        kv_copy(m, 2, 3, beside).start()
+        kv_copy(m, 0, 1, beside).wait_recv()
+        kv_copy(m, 2, 3, beside).wait_recv()
+
+    def e_copy(m, h):
+        slot = lax.rem(h, 2)
+        return pltpu.make_async_copy(low_ref.at[slot], e_ref.at[m, h], e_sem.at[slot])
+
+    def attend(m, first, last):
+        def one(h, carry):
+            lanes = pl.ds(pl.multiple_of(h * HEAD_DIM, 16), HEAD_DIM)
+            values = pl.ds(pl.multiple_of(width + h * HEAD_DIM, 16), HEAD_DIM)
+            slot = lax.rem(h, 2)
+            if m > 0:
+                e_copy(m, h).wait()
+            else:
+                pl.when(h >= 2)(lambda: e_copy(m, h).wait())
+            q = q_ref[m, lanes]
+            top = jnp.full((1, rows), -1e30, jnp.float32)
+            for b in range(ctx):
+                s = contract(pairs_ref[m, b, lanes], q, ((0,), (0,)))
+                at = lax.broadcasted_iota(jnp.int32, (rows, 1), 0)
+                s = jnp.where(at < valid_ref[m, b], s, -1e30)
+                s_ref[b] = s
+                top = jnp.maximum(top, jnp.max(s, axis=0, keepdims=True))
+            norm = jnp.zeros((1, rows), jnp.float32)
+            total = jnp.zeros((HEAD_DIM, rows), jnp.float32)
+            for b in range(ctx):
+                e = jnp.exp2(s_ref[b] - top)
+                norm = norm + jnp.sum(e, axis=0, keepdims=True)
+                low = e.astype(LOW)
+                low_ref[slot, b * rows : (b + 1) * rows] = low
+                total = total + contract(pairs_ref[m, b, values], low, ((1,), (0,)))
+            inverse = 1.0 / norm
+            mine_ref[m, lanes] = (total * inverse).astype(LOW)
+            inverse_ref[m, h] = jnp.broadcast_to(inverse, (8, rows))
+            e_copy(m, h).start()
+            return carry
+
+        lax.fori_loop(first, last, one, 0)
+
+    def a_copy(m, slot, other):
+        return remote(mine_ref.at[m], a_ref.at[m, me], a_send.at[m, slot], a_recv.at[m, slot], tp=other)
+
+    def a_arriving(m, slot, other):
+        return remote(mine_ref.at[m], a_ref.at[m, other], a_send.at[m, slot], a_recv.at[m, slot], tp=other)
+
+    def send_attended(m):
+        for d in range(1, tp):
+            a_copy(m, d, lax.rem(me + d, tp)).start()
+        pltpu.make_async_copy(mine_ref.at[m], a_ref.at[m, me], last_sem.at[1 + m]).start()
+
+    half = heads // 2
+    project(0)
+    send_pair(0)
+    project(1)
+    for hop in range(1, shard):
+        arrive(out, hop)
+    begin(down)
+    arrive(up, 1)
+    cross(out)
+    take_pair(0)
+    send_pair(1)
+    arrive(up, 2)
+    attend(0, 0, half)
+    arrive(up, 3)
+    attend(0, half, heads)
+    send_attended(0)
+    keep_pairs = [pltpu.make_async_copy(pairs_ref.at[m], kv_ref.at[m], last_sem.at[3 + m]) for m in range(2)]
+    keep_pairs[0].start()
+    arrive(down, 1)
+    cross(up)
+    take_pair(1)
+    attend(1, 0, half)
+    arrive(down, 2)
+    attend(1, half, heads)
+    send_attended(1)
+    keep_pairs[1].start()
+    arrive(down, 3)
+    settle(out)
+    settle(up)
+    settle(down)
+    for w in everything:
+        drain(w)
+    for d in range(1, tp):
+        y_copy(me, lax.rem(me + d, tp), d).wait_send()
+    for m in range(2):
+        kv_copy(m, 0, 2, across).wait_send()
+        kv_copy(m, 0, 1, beside).wait_send()
+        kv_copy(m, 2, 3, beside).wait_send()
+        for d in range(1, tp):
+            a_arriving(m, d, lax.rem(me + tp - d, tp)).wait_recv()
+            a_copy(m, d, lax.rem(me + d, tp)).wait_send()
+        pltpu.make_async_copy(mine_ref.at[m], a_ref.at[m, me], last_sem.at[1 + m]).wait()
+        keep_pairs[m].wait()
+    keep_qkv.wait()
+    for h in (heads - 2, heads - 1):
+        e_copy(1, h).wait()
+
+
+def opening(sizes, valid, normed, bias, qkv, out, up, down):
+    shard, ctx, tp = sizes
+    width = qkv.shape[1] // 3
+    model = qkv.shape[0] * shard
+    rows = normed.shape[1] // 2
+    heads = width // HEAD_DIM
+    low = lambda *shape: jax.ShapeDtypeStruct(shape, LOW)
+    anywhere, vmem = pl.BlockSpec(memory_space=pl.ANY), pl.BlockSpec(memory_space=pltpu.VMEM)
+    dma = pltpu.SemaphoreType.DMA
+    keys = ctx * rows
     return pl.pallas_call(
-        functools.partial(forward_kernel, blocks=blocks, heads=heads),
-        grid=(heads+1,),
-        in_specs=[pl.BlockSpec(memory_space=pltpu.SMEM), pl.BlockSpec((HEAD_DIM, rows), head)]
-          + [pl.BlockSpec((HEAD_DIM, span), head)]*blocks + [pl.BlockSpec((HEAD_DIM, span), value)]*blocks,
-        out_specs=[pl.BlockSpec((HEAD_DIM, rows), last), pl.BlockSpec((1, blocks*span, rows), lambda h:(jnp.maximum(h-1,0),0,0)), pl.BlockSpec((1,8,rows), lambda h:(jnp.maximum(h-1,0),0,0))],
-        out_shape=[jax.ShapeDtypeStruct((width, rows), jnp.bfloat16), jax.ShapeDtypeStruct((heads, blocks*span, rows), jnp.bfloat16), jax.ShapeDtypeStruct((heads, 8, rows), jnp.float32)],
-        scratch_shapes=[pltpu.VMEM((blocks*span, rows), jnp.float32), pltpu.VMEM((blocks*span, rows), jnp.float32), pltpu.VMEM((1, rows), jnp.float32), pltpu.VMEM((1, rows), jnp.float32), pltpu.VMEM((HEAD_DIM, rows), jnp.float32), pltpu.VMEM((1, rows), jnp.float32)],
-        compiler_params=pltpu.CompilerParams(vmem_limit_bytes=40<<20),
-        cost_estimate=pl.CostEstimate(flops=4*rows*blocks*span*256*heads, bytes_accessed=heads*blocks*span*rows*2, transcendentals=rows*blocks*span*heads),
-        name="attention_forward",
-    )(valid, q, *kv, *kv)
+        functools.partial(opening_kernel, sizes),
+        in_specs=[pl.BlockSpec(memory_space=pltpu.SMEM), vmem, vmem] + [anywhere] * 4,
+        out_specs=[anywhere] * 4 + [vmem, anywhere, anywhere, anywhere, vmem],
+        out_shape=[
+            low(model, 3 * width),
+            low(tp, model, width),
+            low(model, up.shape[1]),
+            low(model, down.shape[1]),
+            low(2, width, rows),
+            low(2, ctx, 2 * width, rows),
+            low(2, tp, width, rows),
+            low(2, heads, keys, rows),
+            jax.ShapeDtypeStruct((2, heads, 8, rows), jnp.float32),
+        ],
+        scratch_shapes=[
+            pltpu.VMEM((model, 3 * width), LOW),
+            pltpu.VMEM((2, ctx, 2 * width, rows), LOW),
+            pltpu.VMEM((2, width, rows), LOW),
+            pltpu.VMEM((ctx, rows, rows), jnp.float32),
+            pltpu.VMEM((2, keys, rows), LOW),
+            dma((4, 2, shard)),
+            dma((4, shard)),
+            dma((4, shard)),
+            dma((4, shard)),
+            dma((4, shard, 2)),
+            dma((4, shard, 2)),
+            dma((tp,)),
+            dma((tp,)),
+            dma((2, 3)),
+            dma((2, 3)),
+            dma((2, tp)),
+            dma((2, tp)),
+            dma((4,)),
+            dma((2,)),
+            dma((5,)),
+        ],
+        compiler_params=pltpu.CompilerParams(collective_id=0, has_side_effects=True, vmem_limit_bytes=56 << 20),
+        cost_estimate=pl.CostEstimate(
+            flops=8 * heads * rows * keys * 256, bytes_accessed=80 << 20, transcendentals=2 * heads * rows * keys
+        ),
+        name="opening",
+    )(valid, normed, bias, qkv, out, up, down)
+
 
 def backward_kernel(valid_ref, q_ref, g_ref, a_ref, inverse_ref, e_ref, *refs, blocks):
     k_refs, v_refs = refs[:blocks], refs[blocks:2*blocks]
@@ -176,34 +488,6 @@
     return out
 
 
-def gather_rows(piece, size):
-    me = lax.axis_index("shard")
-    right, left = [piece], [piece]
-    for hop in range(1, size):
-        right.append(lax.ppermute(right[-1], "shard", [(k, k + 1) for k in range(hop - 1, size - 1)]))
-        left.append(lax.ppermute(left[-1], "shard", [(k, k - 1) for k in range(size - hop, 0, -1)]))
-    out = jnp.zeros((size,) + piece.shape, piece.dtype)
-    out = lax.dynamic_update_index_in_dim(out, piece, me, 0)
-    for hop in range(1, size):
-        block = jnp.where(me >= hop, right[hop], left[size - hop])
-        out = lax.dynamic_update_index_in_dim(out, block, lax.rem(me + size - hop, size), 0)
-    return out
-
-
-def gather_weight(weight, shard, ctx, split):
-    part = lax.rem(lax.axis_index("ctx"), split)
-    rows = weight.shape[0] // split
-    piece = lax.dynamic_slice_in_dim(weight, part * rows, rows, 0)
-    mine = gather_rows(piece, shard)
-    blocks = {0: mine}
-    for bit in bits_of(split):
-        blocks.update({mask | bit: swap(blocks[mask], "ctx", bit, ctx) for mask in list(blocks)})
-    out = jnp.zeros((shard, split, rows, weight.shape[1]), weight.dtype)
-    for mask in range(split):
-        out = lax.dynamic_update_index_in_dim(out, blocks[mask], part ^ mask, 1)
-    return out.reshape(shard * weight.shape[0], weight.shape[1])
-
-
 def scatter_ctx(chunk, ctx):
     def total(mask, bits):
         if len(bits) == 0:
@@ -280,35 +564,29 @@
     width = query_weight.shape[1]
     ctx_index = lax.axis_index("ctx")
 
-    full_qkv = gather_weight(
-        jnp.concatenate([query_weight, key_weight, value_weight], axis=1), shard, ctx, 4 if ctx % 4 == 0 else 1
-    )
-    out_both = canonical(spread(out_weight, "tp", tp), "tp", tp)
-    out_both = jnp.moveaxis(out_both, 0, 1).reshape(out_weight.shape[0], tp * width)
-    full_out = gather_weight(out_both, shard, ctx, 2)
-    full_up = gather_weight(up_weight, shard, ctx, 4)
-    full_down = gather_weight(down_weight, shard, ctx, 2)
-    own_out = lax.dynamic_slice_in_dim(full_out, lax.axis_index("tp") * width, width, 1)
-
-    bias = jnp.concatenate([query_bias, jnp.zeros_like(query_bias), value_bias])[:, None]
-    scale = jnp.concatenate(
-        [jnp.full((width, 1), SCALE * math.log2(math.e), jnp.float32), jnp.ones((2 * width, 1), jnp.float32)]
-    )
-
     inputs = [frames[m, 0].astype(jnp.float32) for m in range(micros)]
     hats1 = [normalize(x) for x in inputs]
     normed1 = [(hat * norm1_gain + norm1_bias).astype(LOW) for hat, _ in hats1]
-    projected = [((contract(full_qkv, h, ((0,), (1,))) + bias) * scale).astype(LOW) for h in normed1]
-    queries = [p[:width] for p in projected]
-    pairs = [spread(p[width:], "ctx", ctx) for p in projected]
+    bias = jnp.concatenate([query_bias, jnp.zeros_like(query_bias), value_bias])[:, None]
     ids = ctx_index ^ jnp.arange(ctx, dtype=jnp.int32)
     valid = [jnp.clip(lengths[m, 0] - rows * ids, 0, rows) for m in range(micros)]
-
-    attended, kept, inverses = zip(*[attention_forward(valid[m], queries[m], pairs[m]) for m in range(micros)])
+    full_qkv, full_out, full_up, full_down, queries, pairs, all_attended, kept, inverses = opening(
+        sizes,
+        jnp.stack(valid),
+        jnp.concatenate(normed1, axis=0).T,
+        bias,
+        jnp.concatenate([query_weight, key_weight, value_weight], axis=1),
+        out_weight,
+        up_weight,
+        down_weight,
+    )
+    tp_index = lax.axis_index("tp")
+    own_out = lax.dynamic_index_in_dim(full_out, tp_index, 0, keepdims=False)
+    attended = [lax.dynamic_index_in_dim(all_attended[m], tp_index, 0, keepdims=False) for m in range(micros)]
     mixed, hats2, normed2, hidden = [], [], [], []
     for m in range(micros):
-        all_heads = canonical(spread(attended[m], "tp", tp), "tp", tp).reshape(tp * width, rows)
-        mixed.append(inputs[m] + contract(all_heads, full_out, ((0,), (1,))) + out_bias)
+        branch = sum(contract(all_attended[m, t], full_out[t], ((0,), (1,))) for t in range(tp))
+        mixed.append(inputs[m] + branch + out_bias)
         hats2.append(normalize(mixed[m]))
         normed2.append((hats2[m][0] * norm2_gain + norm2_bias).astype(LOW))
         hidden.append(contract(normed2[m], full_up, ((1,), (0,))) + up_bias)
@@ -333,7 +611,7 @@
     for m in range(micros):
         attended_grad = contract(own_out, branch_grads[m], ((0,), (1,))).astype(LOW)
         parts = attention_backward(
-            valid[m], queries[m], attended_grad, attended[m], inverses[m], kept[m], pairs[m]
+            valid[m], queries[m], attended_grad, attended[m], inverses[m], kept[m], [pairs[m, b] for b in range(ctx)]
         )
         terms = [
             jnp.concatenate([parts[1 + mask], parts[1 + ctx + mask]], axis=0) for mask in range(ctx)

time: 911 us -> 814 us (0.89)
  Pallas kernels: 64.6 us -> 247 us
  waiting for transfers between devices: 315 us -> 166 us
  starting transfers between devices: 191 us -> 64 us
  matrix products: 124 us -> 114 us
    pallas_call x2 -> x1, Pallas kernels: 27.2 us -> 210 us  [opening(): pl.pallas_call(functools.partial(opening_kernel, sizes), in_specs=[pl.Blo...]
    ppermute x58 -> x41, waiting for transfers between devices: 228 us -> 113 us  [swap(): return lax.ppermute(value, axis, [(k, k ^ bit) for k in range(size)])]
    ppermute x24 -> x0, starting transfers between devices: 63.3 us -> none  [the longest x12 38.9 us: gather_rows(): lax.ppermute(left[-1], 'shard', [(k, k - 1) for k in range(size - hop, 0,...]
    ppermute x58 -> x41, starting transfers between devices: 98.3 us -> 42.5 us  [swap(): return lax.ppermute(value, axis, [(k, k ^ bit) for k in range(size)])]
    ppermute x24 -> x0, waiting for transfers between devices: 35.2 us -> none  [the longest x12 34.9 us: gather_rows(): lax.ppermute(left[-1], 'shard', [(k, k - 1) for k in range(size - hop, 0,...]
    squeeze x1 -> x6, local copies, waits for them, and re-layouts: 1.64 us -> 30.3 us  [the longest x1 22.7 us: body(): kept[m]]
    dynamic_update_slice x20 -> x14, local copies, waits for them, and re-layouts: 62.1 us -> 35.3 us  [canonical(): out = lax.dynamic_update_index_in_dim(out, block, me ^ mask, 0)]
    dynamic_update_slice x15 -> x0, local copies, waits for them, and re-layouts: 18 us -> none  [the longest x12 15 us: gather_weight(): out = lax.dynamic_update_index_in_dim(out, blocks[mask], part ^ mask, 1)]
  transfers between devices with their start and end apart: 94 -> 53, of which waited for: 34 -> 17; matrix products, arithmetic and copies ran while one was open for 28% -> 31% of each run, Pallas kernels for 7% -> 5%
where the time goes in v2:
time: 814 us; the launch traced here: 800 us
  Pallas kernels  247 us (30%)
  waiting for transfers between devices  166 us (20%)
  local copies, waits for them, and re-layouts  126 us (15%)
  matrix products  114 us (14%)
  other arithmetic  80.6 us (10%)
  starting transfers between devices  64 us (8%)
    pallas_call x1, Pallas kernels, opening(): pl.pallas_call(functools.partial(opening_kernel, sizes), in_specs=[pl.Blo...  210 us
    dot_general x32, matrix products, contract(): lax.dot_general(left, right, (dims, ((), ())), preferred_element_type=jnp...  114 us
    ppermute x41, waiting for transfers between devices, swap(): return lax.ppermute(value, axis, [(k, k ^ bit) for k in range(size)])  113 us
    ppermute x12, waiting for transfers between devices, scatter_rows(): lax.ppermute(block, 'shard', [(k, (k + shift) % size) for k in range(size)])  53.6 us
    ppermute x41, starting transfers between devices, swap(): return lax.ppermute(value, axis, [(k, k ^ bit) for k in range(size)])  42.5 us
    pallas_call x2, Pallas kernels, attention_backward(): pl.pallas_call(functools.partial(backward_kernel, blocks=blocks), grid=(h...  37.2 us
    dynamic_update_slice x14, local copies, waits for them, and re-layouts, canonical(): out = lax.dynamic_update_index_in_dim(out, block, me ^ mask, 0)  35.3 us
    unnamed x240, local copies, waits for them, and re-layouts  33.6 us
  transfers between devices with their start and end apart: 53, of which 17 were waited for; matrix products, arithmetic and copies ran while one was open for 31% of the time, Pallas kernels for 5%

profile of v2, /device:TPU:9, one launch (start us, length us, event | category | flops | bytes accessed | tf_op | source)
XLA Modules:
  0.0 800.1 jit_solution(17260657638680524756)
XLA Ops:
  17.3 209.9 %opening.1 = (bf16[1280,1920]{1,0:T(8,128)(2,1)}, bf16[2,1280,640]{2,1,0:T(8,128)(2,1)}, bf16[1280,2560]{1,0:T(8,128)(2,1)}, bf16[1280,2560]{1,0:T(8,128)(2,1)},...) custom-call(s32[2,4]{1,0:T(2,128)} %pad_add_fusion.valid_ref, ...), custom_call_target="tpu_custom_call" | custom-call | flops 17179869184 | bytes 83886080 | tf_op jit(solution)/shard_map/opening/pallas_call | solution.py:347
  239.0 4.8 multiply_convert_fusion.1
  248.7 5.5 convert_reduce_fusion.1
  264.6 5.5 convert_reduce_fusion
  284.1 5.6 convolution_convert_fusion
  292.4 5.6 convolution_convert_fusion.3
  301.4 5.4 fusion.99
  314.2 22.7 %slice_bitcast_fusion = (bf16[8,2048,512]{2,1,0:T(8,128)(2,1)}, bf16[8,2048,512]{2,1,0:T(8,128)(2,1)}) fusion(bf16[2,8,2048,512]{3,2,1,0:T(8,128)(2,1)} %get-tuple-element.50), kind=kLoop, calls=%fused_computation | loop fusion | bytes 67108864 | tf_op jit(solution)/shard_map/squeeze | solution.py:614
  337.0 5.0 slice_bitcast_fusion.2
  351.3 5.2 fusion.190
  374.7 18.5 %attention_backward.2 = (bf16[640,512]{1,0:T(8,128)(2,1)S(1)}, bf16[640,512]{1,0:T(8,128)(2,1)S(1)}, bf16[640,512]{1,0:T(8,128)(2,1)S(1)}, bf16[640,512]{1,0:T(8...) custom-call(s32[4]{0:T(128)S(1)} %get-tuple-element.223.valid_ref, ...), custom_call_target="tpu_custom_call" | custom-call | flops 17179869184 | bytes 16777216 | tf_op jit(solution)/shard_map/attention_backward/pallas_call | solution.py:435
  394.8 18.7 %attention_backward.3 = (bf16[640,512]{1,0:T(8,128)(2,1)S(1)}, bf16[640,512]{1,0:T(8,128)(2,1)S(1)}, bf16[640,512]{1,0:T(8,128)(2,1)S(1)}, bf16[640,512]{1,0:T(8...) custom-call(s32[4]{0:T(128)S(1)} %get-tuple-element.222.valid_ref, ...), custom_call_target="tpu_custom_call" | custom-call | flops 17179869184 | bytes 16777216 | tf_op jit(solution)/shard_map/attention_backward/pallas_call | solution.py:435
  436.1 6.4 collective-permute-start.30
  442.6 4.8 add_convert_fusion
  453.1 4.8 add_convert_fusion.1
  458.3 30.0 %collective-permute-done.33 = bf16[320,160]{0,1:T(8,128)(2,1)S(1)} collective-permute-done((bf16[320,160]{0,1:T(8,128)(2,1)S(1)}, bf16[320,160]{0,1:T(8,128)(2,1)S(1)}, u32[]{:S(2)}, u32[]{:S(2)}) %collective-permute-start.33) | collective-permute-done | bytes 102432 | tf_op jit(solution)/shard_map/ppermute | solution.py:450
  503.8 25.1 %collective-permute-done.37 = bf16[1280,640]{1,0:T(8,128)(2,1)} collective-permute-done((bf16[1280,640]{1,0:T(8,128)(2,1)}, bf16[1280,640]{1,0:T(8,128)(2,1)}, u32[]{:S(2)}, u32[]{:S(2)}) %collective-permute-start.37) | collective-permute-done | bytes 1638432 | tf_op jit(solution)/shard_map/ppermute | solution.py:450
  533.8 11.5 %collective-permute-done.48 = bf16[320,640]{1,0:T(8,128)(2,1)S(1)} collective-permute-done((bf16[320,640]{1,0:T(8,128)(2,1)S(1)}, bf16[320,640]{1,0:T(8,128)(2,1)S(1)}, u32[]{:S(2)}, u32[]{:S(2)}) %collective-permute-start.48) | collective-permute-done | bytes 409632 | tf_op jit(solution)/shard_map/ppermute | solution.py:510
  549.9 17.3 %collective-permute-done.38 = bf16[320,640]{1,0:T(8,128)(2,1)S(1)} collective-permute-done((bf16[320,640]{1,0:T(8,128)(2,1)S(1)}, bf16[320,640]{1,0:T(8,128)(2,1)S(1)}, u32[]{:S(2)}, u32[]{:S(2)}) %collective-permute-start.38) | collective-permute-done | bytes 409632 | tf_op jit(solution)/shard_map/ppermute | solution.py:510
  567.2 8.1 %collective-permute-start.8 = (bf16[1280,512]{1,0:T(8,128)(2,1)S(1)}, bf16[1280,512]{1,0:T(8,128)(2,1)S(1)}, u32[]{:S(2)}, u32[]{:S(2)}) collective-permute-start(bf16[1280,512]{1,0:T(8,128)(2,1)S(1)} %copy-done.54), channel_id=1, source_target_pairs={{0,2},{2,0},{4,6},{6,4},{1,3},{3,1},{5,7},{7,5},{8,10},{10,8},{12,... | collective-permute-start | bytes 3932168 | tf_op jit(solution)/shard_map/ppermute | solution.py:450
  575.4 5.0 collective-permute-done.39
  586.1 5.1 fusion.200
  591.6 12.4 %collective-permute-done.10 = bf16[1280,512]{1,0:T(8,128)(2,1)S(1)} collective-permute-done((bf16[1280,512]{1,0:T(8,128)(2,1)S(1)}, bf16[1280,512]{1,0:T(8,128)(2,1)S(1)}, u32[]{:S(2)}, u32[]{:S(2)}) %collective-permute-start.10) | collective-permute-done | bytes 1310752 | tf_op jit(solution)/shard_map/ppermute | solution.py:450
  605.1 5.1 fusion.201
  610.1 10.8 %maximum_maximum_fusion = bf16[1920,1024]{1,0:T(8,128)(2,1)S(1)} fusion(bf16[1280,512]{1,0:T(8,128)(2,1)S(1)} %add_convert_fusion.3, bf16[640,512]{1,0:T(8,128)(2,1)S(1)} %copy-done.8, bf16[1280,512]{1,0:T(8,128)(2,1)S(1)} %add_convert_fusion.7, bf16[640,512]{1,0:T(8,128)(2,1)S(1)} %copy-done.6), kind=kLoop, calls=%fused_computation.41 | loop fusion | flops 15728640 | bytes 7864320 | tf_op jit(solution)/shard_map/concatenate | solution.py:631
  657.6 15.4 %dynamic_update_slice.62 = bf16[4,320,640]{2,0,1:T(4,128)(2,1)} dynamic-update-slice(bf16[4,320,640]{2,0,1:T(4,128)(2,1)} %copy.79, bf16[1,320,640]{2,0,1:T(2,128)(2,1)S(1)} %copy.80, s32[]{:T(128)S(6)} %select_n.110, s32[]{:T(128)} %constant.107.clone.1, s32[]{:T(128)} %constant.107.clone.1) | dynamic-update-slice | bytes 819204 | tf_op jit(solution)/shard_map/jit(dynamic_update_index_in_dim)/dynamic_update_slice | solution.py:487
  681.5 25.1 %collective-permute-done.11 = bf16[512,1280]{0,1:T(8,128)(2,1)} collective-permute-done((bf16[512,1280]{0,1:T(8,128)(2,1)}, bf16[512,1280]{0,1:T(8,128)(2,1)}, u32[]{:S(2)}, u32[]{:S(2)}) %collective-permute-start.11) | collective-permute-done | bytes 1310752 | tf_op jit(solution)/shard_map/ppermute | solution.py:450
  734.7 6.1 copy.83
  740.8 10.1 %collective-permute-done.22 = bf16[320,480]{0,1:T(8,128)(2,1)S(1)} collective-permute-done((bf16[320,480]{0,1:T(8,128)(2,1)S(1)}, bf16[320,480]{0,1:T(8,128)(2,1)S(1)}, u32[]{:S(2)}, u32[]{:S(2)}) %collective-permute-start.22) | collective-permute-done | bytes 307232 | tf_op jit(solution)/shard_map/ppermute | solution.py:510
  750.9 8.9 %collective-permute-done.21 = bf16[320,480]{0,1:T(8,128)(2,1)S(1)} collective-permute-done((bf16[320,480]{0,1:T(8,128)(2,1)S(1)}, bf16[320,480]{0,1:T(8,128)(2,1)S(1)}, u32[]{:S(2)}, u32[]{:S(2)}) %collective-permute-start.21) | collective-permute-done | bytes 307232 | tf_op jit(solution)/shard_map/ppermute | solution.py:510
  766.5 8.3 %collective-permute-done.24 = bf16[320,480]{0,1:T(8,128)(2,1)S(1)} collective-permute-done((bf16[320,480]{0,1:T(8,128)(2,1)S(1)}, bf16[320,480]{0,1:T(8,128)(2,1)S(1)}, u32[]{:S(2)}, u32[]{:S(2)}) %collective-permute-start.24) | collective-permute-done | bytes 307232 | tf_op jit(solution)/shard_map/ppermute | solution.py:450
  779.3 12.5 %dynamic_update_slice.54 = bf16[4,320,480]{2,0,1:T(4,128)(2,1)} dynamic-update-slice(bf16[4,320,480]{2,0,1:T(4,128)(2,1)} %copy.77, bf16[1,320,480]{2,0,1:T(2,128)(2,1)S(1)} %copy.78, s32[]{:T(128)S(6)} %select_n.110, s32[]{:T(128)} %constant.107.clone.1, s32[]{:T(128)} %constant.107.clone.1) | dynamic-update-slice | bytes 614404 | tf_op jit(solution)/shard_map/jit(dynamic_update_index_in_dim)/dynamic_update_slice | solution.py:487
  (472 shorter events, 252.2 us)
Async XLA Ops:
  248.5 102.1 %collective-permute-start = (bf16[512,1280]{0,1:T(8,128)(2,1)}, bf16[512,1280]{0,1:T(8,128)(2,1)}, u32[]{:S(2)}, u32[]{:S(2)}) collective-permute-start(bf16[512,1280]{0,1:T(8,128)(2,1)} %convolution_convert_fusion.7), channel_id=1, source_target_pairs={{0,1},{1,0},{2,3},{3,2},{4,5},{5,4},{6,7},{7,6},{8,9},{9,8},{10,11... | collective-permute-start | bytes 3932168 | tf_op jit(solution)/shard_map/ppermute | solution.py:450
  258.9 88.3 %collective-permute-start.2 = (bf16[512,1280]{0,1:T(8,128)(2,1)}, bf16[512,1280]{0,1:T(8,128)(2,1)}, u32[]{:S(2)}, u32[]{:S(2)}) collective-permute-start(bf16[512,1280]{0,1:T(8,128)(2,1)} %convolution_convert_fusion.5), channel_id=1, source_target_pairs={{0,1},{1,0},{2,3},{3,2},{4,5},{5,4},{6,7},{7,6},{8,9},{9,8},{10,11... | collective-permute-start | bytes 3932168 | tf_op jit(solution)/shard_map/ppermute | solution.py:450
  274.8 76.5 %collective-permute-start.7 = (bf16[512,1280]{0,1:T(8,128)(2,1)}, bf16[512,1280]{0,1:T(8,128)(2,1)}, u32[]{:S(2)}, u32[]{:S(2)}) collective-permute-start(bf16[512,1280]{0,1:T(8,128)(2,1)} %convolution_convert_fusion.4), channel_id=1, source_target_pairs={{0,1},{1,0},{2,3},{3,2},{4,5},{5,4},{6,7},{7,6},{8,9},{9,8},{10,11... | collective-permute-start | bytes 3932168 | tf_op jit(solution)/shard_map/ppermute | solution.py:450
  279.6 83.9 %collective-permute-start.1 = (bf16[512,1280]{0,1:T(8,128)(2,1)}, bf16[512,1280]{0,1:T(8,128)(2,1)}, u32[]{:S(2)}, u32[]{:S(2)}) collective-permute-start(bf16[512,1280]{0,1:T(8,128)(2,1)} %convolution_convert_fusion.6), channel_id=1, source_target_pairs={{0,1},{1,0},{2,3},{3,2},{4,5},{5,4},{6,7},{7,6},{8,9},{9,8},{10,11... | collective-permute-start | bytes 3932168 | tf_op jit(solution)/shard_map/ppermute | solution.py:450
  289.6 146.5 %collective-permute-start.45 = (bf16[1280,640]{1,0:T(8,128)(2,1)}, bf16[1280,640]{1,0:T(8,128)(2,1)}, u32[]{:S(2)}, u32[]{:S(2)}) collective-permute-start(bf16[1280,640]{1,0:T(8,128)(2,1)} %convolution_convert_fusion), channel_id=1, source_target_pairs={{0,2},{2,0},{4,6},{6,4},{1,3},{3,1},{5,7},{7,5},{8,10},{10,8},{12,... | collective-permute-start | bytes 4915208 | tf_op jit(solution)/shard_map/ppermute | solution.py:450
  347.1 104.3 %collective-permute-start.36 = (bf16[1280,640]{1,0:T(8,128)(2,1)}, bf16[1280,640]{1,0:T(8,128)(2,1)}, u32[]{:S(2)}, u32[]{:S(2)}) collective-permute-start(bf16[1280,640]{1,0:T(8,128)(2,1)} %convolution_convert_fusion.2), channel_id=1, source_target_pairs={{0,2},{2,0},{4,6},{6,4},{1,3},{3,1},{5,7},{7,5},{8,10},{10,8},{12,... | collective-permute-start | bytes 4915208 | tf_op jit(solution)/shard_map/ppermute | solution.py:450
  350.6 147.3 %collective-permute-start.44 = (bf16[1280,640]{1,0:T(8,128)(2,1)}, bf16[1280,640]{1,0:T(8,128)(2,1)}, u32[]{:S(2)}, u32[]{:S(2)}) collective-permute-start(bf16[1280,640]{1,0:T(8,128)(2,1)} %convolution_convert_fusion.1), channel_id=1, source_target_pairs={{0,2},{2,0},{4,6},{6,4},{1,3},{3,1},{5,7},{7,5},{8,10},{10,8},{12,... | collective-permute-start | bytes 4915208 | tf_op jit(solution)/shard_map/ppermute | solution.py:450
  372.1 43.9 %collective-permute-start.27 = (bf16[1280,160]{0,1:T(8,128)(2,1)S(1)}, bf16[1280,160]{0,1:T(8,128)(2,1)S(1)}, u32[]{:S(2)}, u32[]{:S(2)}) collective-permute-start(bf16[1280,160]{0,1:T(8,128)(2,1)S(1)} %convolution_convert_fusion.10), channel_id=1, source_target_pairs={{0,2},{2,0},{4,6},{6,4},{1,3},{3,1},{5,7},{7,5},{8,10},{10,8},{12,... | collective-permute-start | bytes 1228808 | tf_op jit(solution)/shard_map/ppermute | solution.py:450
  372.9 53.6 %collective-permute-start.26 = (bf16[1280,160]{0,1:T(8,128)(2,1)}, bf16[1280,160]{0,1:T(8,128)(2,1)}, u32[]{:S(2)}, u32[]{:S(2)}) collective-permute-start(bf16[1280,160]{0,1:T(8,128)(2,1)} %convolution_convert_fusion.11), channel_id=1, source_target_pairs={{0,2},{2,0},{4,6},{6,4},{1,3},{3,1},{5,7},{7,5},{8,10},{10,8},{12,... | collective-permute-start | bytes 1228808 | tf_op jit(solution)/shard_map/ppermute | solution.py:450
  447.4 47.7 %collective-permute-start.4 = (bf16[1280,512]{1,0:T(8,128)(2,1)}, bf16[1280,512]{1,0:T(8,128)(2,1)}, u32[]{:S(2)}, u32[]{:S(2)}) collective-permute-start(bf16[1280,512]{1,0:T(8,128)(2,1)} %pad_maximum_fusion.5), channel_id=1, source_target_pairs={{0,2},{2,0},{4,6},{6,4},{1,3},{3,1},{5,7},{7,5},{8,10},{10,8},{12,... | collective-permute-start | bytes 3932168 | tf_op jit(solution)/shard_map/ppermute | solution.py:450
  449.5 48.4 %collective-permute-start.46 = (bf16[1280,640]{1,0:T(8,128)(2,1)}, bf16[1280,640]{1,0:T(8,128)(2,1)}, u32[]{:S(2)}, u32[]{:S(2)}) collective-permute-start(bf16[1280,640]{1,0:T(8,128)(2,1)} %add_convert_fusion), channel_id=1, source_target_pairs={{0,4},{2,6},{4,0},{6,2},{1,5},{3,7},{5,1},{7,3},{8,12},{10,14},{12... | collective-permute-start | bytes 4915208 | tf_op jit(solution)/shard_map/ppermute | solution.py:450
  451.5 36.8 %collective-permute-start.33 = (bf16[320,160]{0,1:T(8,128)(2,1)S(1)}, bf16[320,160]{0,1:T(8,128)(2,1)S(1)}, u32[]{:S(2)}, u32[]{:S(2)}) collective-permute-start(bf16[320,160]{0,1:T(8,128)(2,1)S(1)} %get-tuple-element.133), channel_id=1, source_target_pairs={{0,4},{2,6},{4,0},{6,2},{1,5},{3,7},{5,1},{7,3},{8,12},{10,14},{12... | collective-permute-start | bytes 307208 | tf_op jit(solution)/shard_map/ppermute | solution.py:450
  457.9 44.4 %collective-permute-start.35 = (bf16[1280,640]{1,0:T(8,128)(2,1)}, bf16[1280,640]{1,0:T(8,128)(2,1)}, u32[]{:S(2)}, u32[]{:S(2)}) collective-permute-start(bf16[1280,640]{1,0:T(8,128)(2,1)} %convolution_convert_fusion.3), channel_id=1, source_target_pairs={{0,2},{2,0},{4,6},{6,4},{1,3},{3,1},{5,7},{7,5},{8,10},{10,8},{12,... | collective-permute-start | bytes 4915208 | tf_op jit(solution)/shard_map/ppermute | solution.py:450
  491.6 37.3 %collective-permute-start.37 = (bf16[1280,640]{1,0:T(8,128)(2,1)}, bf16[1280,640]{1,0:T(8,128)(2,1)}, u32[]{:S(2)}, u32[]{:S(2)}) collective-permute-start(bf16[1280,640]{1,0:T(8,128)(2,1)} %add_convert_fusion.1), channel_id=1, source_target_pairs={{0,4},{2,6},{4,0},{6,2},{1,5},{3,7},{5,1},{7,3},{8,12},{10,14},{12... | collective-permute-start | bytes 4915208 | tf_op jit(solution)/shard_map/ppermute | solution.py:450
  497.9 85.8 %collective-permute-start.3 = (bf16[1280,512]{1,0:T(8,128)(2,1)}, bf16[1280,512]{1,0:T(8,128)(2,1)S(1)}, u32[]{:S(2)}, u32[]{:S(2)}) collective-permute-start(bf16[1280,512]{1,0:T(8,128)(2,1)} %pad_maximum_fusion.4), channel_id=1, source_target_pairs={{0,2},{2,0},{4,6},{6,4},{1,3},{3,1},{5,7},{7,5},{8,10},{10,8},{12,... | collective-permute-start | bytes 3932168 | tf_op jit(solution)/shard_map/ppermute | solution.py:450
  498.0 85.7 %collective-permute-start.5 = (bf16[1280,512]{1,0:T(8,128)(2,1)S(1)}, bf16[1280,512]{1,0:T(8,128)(2,1)S(1)}, u32[]{:S(2)}, u32[]{:S(2)}) collective-permute-start(bf16[1280,512]{1,0:T(8,128)(2,1)S(1)} %add_convert_fusion.8), channel_id=1, source_target_pairs={{0,4},{2,6},{4,0},{6,2},{1,5},{3,7},{5,1},{7,3},{8,12},{10,14},{12... | collective-permute-start | bytes 3932168 | tf_op jit(solution)/shard_map/ppermute | solution.py:450
  502.3 29.3 %collective-permute-start.47 = (bf16[320,640]{1,0:T(8,128)(2,1)S(1)}, bf16[320,640]{1,0:T(8,128)(2,1)S(1)}, u32[]{:S(2)}, u32[]{:S(2)}) collective-permute-start(bf16[320,640]{1,0:T(8,128)(2,1)S(1)} %get-tuple-element.167), channel_id=1, source_target_pairs={{0,8},{8,16},{16,24},{24,0},{1,9},{9,17},{17,25},{25,1},{2,10},{10... | collective-permute-start | bytes 1228808 | tf_op jit(solution)/shard_map/ppermute | solution.py:510
  503.1 29.8 %collective-permute-start.49 = (bf16[320,640]{1,0:T(8,128)(2,1)S(1)}, bf16[320,640]{1,0:T(8,128)(2,1)S(1)}, u32[]{:S(2)}, u32[]{:S(2)}) collective-permute-start(bf16[320,640]{1,0:T(8,128)(2,1)S(1)} %get-tuple-element.168), channel_id=1, source_target_pairs={{0,24},{8,0},{16,8},{24,16},{1,25},{9,1},{17,9},{25,17},{2,26},{10... | collective-permute-start | bytes 1228808 | tf_op jit(solution)/shard_map/ppermute | solution.py:510
  531.6 35.6 %collective-permute-start.38 = (bf16[320,640]{1,0:T(8,128)(2,1)S(1)}, bf16[320,640]{1,0:T(8,128)(2,1)S(1)}, u32[]{:S(2)}, u32[]{:S(2)}) collective-permute-start(bf16[320,640]{1,0:T(8,128)(2,1)S(1)} %get-tuple-element.170), channel_id=1, source_target_pairs={{0,8},{8,16},{16,24},{24,0},{1,9},{9,17},{17,25},{25,1},{2,10},{10... | collective-permute-start | bytes 1228808 | tf_op jit(solution)/shard_map/ppermute | solution.py:510
  532.9 42.5 %collective-permute-start.40 = (bf16[320,640]{1,0:T(8,128)(2,1)S(1)}, bf16[320,640]{1,0:T(8,128)(2,1)S(1)}, u32[]{:S(2)}, u32[]{:S(2)}) collective-permute-start(bf16[320,640]{1,0:T(8,128)(2,1)S(1)} %get-tuple-element.171), channel_id=1, source_target_pairs={{0,24},{8,0},{16,8},{24,16},{1,25},{9,1},{17,9},{25,17},{2,26},{10... | collective-permute-start | bytes 1228808 | tf_op jit(solution)/shard_map/ppermute | solution.py:510
  545.3 35.1 %collective-permute-start.39 = (bf16[320,640]{1,0:T(8,128)(2,1)S(1)}, bf16[320,640]{1,0:T(8,128)(2,1)S(1)}, u32[]{:S(2)}, u32[]{:S(2)}) collective-permute-start(bf16[320,640]{1,0:T(8,128)(2,1)S(1)} %get-tuple-element.172), channel_id=1, source_target_pairs={{0,16},{8,24},{16,0},{24,8},{1,17},{9,25},{17,1},{25,9},{2,18},{10... | collective-permute-start | bytes 1228808 | tf_op jit(solution)/shard_map/ppermute | solution.py:510
  575.3 28.6 %collective-permute-start.10 = (bf16[1280,512]{1,0:T(8,128)(2,1)S(1)}, bf16[1280,512]{1,0:T(8,128)(2,1)S(1)}, u32[]{:S(2)}, u32[]{:S(2)}) collective-permute-start(bf16[1280,512]{1,0:T(8,128)(2,1)S(1)} %add_convert_fusion.4), channel_id=1, source_target_pairs={{0,4},{2,6},{4,0},{6,2},{1,5},{3,7},{5,1},{7,3},{8,12},{10,14},{12... | collective-permute-start | bytes 3932168 | tf_op jit(solution)/shard_map/ppermute | solution.py:450
  580.4 66.7 %collective-permute-start.50 = (bf16[320,640]{1,0:T(8,128)(2,1)}, bf16[320,640]{1,0:T(8,128)(2,1)}, u32[]{:S(2)}, u32[]{:S(2)}) collective-permute-start(bf16[320,640]{1,0:T(8,128)(2,1)} %get-tuple-element.125), channel_id=1, source_target_pairs={{0,2},{2,0},{4,6},{6,4},{1,3},{3,1},{5,7},{7,5},{8,10},{10,8},{12,... | collective-permute-start | bytes 1228808 | tf_op jit(solution)/shard_map/ppermute | solution.py:450
  583.6 65.9 %collective-permute-start.51 = (bf16[320,640]{1,0:T(8,128)(2,1)}, bf16[320,640]{1,0:T(8,128)(2,1)S(1)}, u32[]{:S(2)}, u32[]{:S(2)}) collective-permute-start(bf16[320,640]{1,0:T(8,128)(2,1)} %get-tuple-element.125), channel_id=1, source_target_pairs={{0,4},{2,6},{4,0},{6,2},{1,5},{3,7},{5,1},{7,3},{8,12},{10,14},{12... | collective-permute-start | bytes 1228808 | tf_op jit(solution)/shard_map/ppermute | solution.py:450
  583.7 64.6 %collective-permute-start.41 = (bf16[320,640]{1,0:T(8,128)(2,1)}, bf16[320,640]{1,0:T(8,128)(2,1)}, u32[]{:S(2)}, u32[]{:S(2)}) collective-permute-start(bf16[320,640]{1,0:T(8,128)(2,1)} %get-tuple-element.129), channel_id=1, source_target_pairs={{0,2},{2,0},{4,6},{6,4},{1,3},{3,1},{5,7},{7,5},{8,10},{10,8},{12,... | collective-permute-start | bytes 1228808 | tf_op jit(solution)/shard_map/ppermute | solution.py:450
  591.2 59.8 %collective-permute-start.42 = (bf16[320,640]{1,0:T(8,128)(2,1)}, bf16[320,640]{1,0:T(8,128)(2,1)S(1)}, u32[]{:S(2)}, u32[]{:S(2)}) collective-permute-start(bf16[320,640]{1,0:T(8,128)(2,1)} %get-tuple-element.129), channel_id=1, source_target_pairs={{0,4},{2,6},{4,0},{6,2},{1,5},{3,7},{5,1},{7,3},{8,12},{10,14},{12... | collective-permute-start | bytes 1228808 | tf_op jit(solution)/shard_map/ppermute | solution.py:450
  629.2 47.8 %collective-permute-start.18 = (bf16[1280,480]{0,1:T(8,128)(2,1)}, bf16[1280,480]{0,1:T(8,128)(2,1)}, u32[]{:S(2)}, u32[]{:S(2)}) collective-permute-start(bf16[1280,480]{0,1:T(8,128)(2,1)} %convolution_convert_fusion.8), channel_id=1, source_target_pairs={{0,2},{2,0},{4,6},{6,4},{1,3},{3,1},{5,7},{7,5},{8,10},{10,8},{12,... | collective-permute-start | bytes 3686408 | tf_op jit(solution)/shard_map/ppermute | solution.py:450
  647.1 78.6 %collective-permute-start.17 = (bf16[1280,480]{0,1:T(8,128)(2,1)}, bf16[1280,480]{0,1:T(8,128)(2,1)}, u32[]{:S(2)}, u32[]{:S(2)}) collective-permute-start(bf16[1280,480]{0,1:T(8,128)(2,1)} %convolution_convert_fusion.9), channel_id=1, source_target_pairs={{0,2},{2,0},{4,6},{6,4},{1,3},{3,1},{5,7},{7,5},{8,10},{10,8},{12,... | collective-permute-start | bytes 3686408 | tf_op jit(solution)/shard_map/ppermute | solution.py:450
  648.3 33.2 %collective-permute-start.6 = (bf16[512,1280]{0,1:T(8,128)(2,1)}, bf16[512,1280]{0,1:T(8,128)(2,1)}, u32[]{:S(2)}, u32[]{:S(2)}) collective-permute-start(bf16[512,1280]{0,1:T(8,128)(2,1)} %convert_element_type.420), channel_id=1, source_target_pairs={{0,1},{1,0},{2,3},{3,2},{4,5},{5,4},{6,7},{7,6},{8,9},{9,8},{10,11... | collective-permute-start | bytes 3932168 | tf_op jit(solution)/shard_map/ppermute | solution.py:450
  649.6 57.0 %collective-permute-start.11 = (bf16[512,1280]{0,1:T(8,128)(2,1)}, bf16[512,1280]{0,1:T(8,128)(2,1)}, u32[]{:S(2)}, u32[]{:S(2)}) collective-permute-start(bf16[512,1280]{0,1:T(8,128)(2,1)} %convert_element_type.441), channel_id=1, source_target_pairs={{0,1},{1,0},{2,3},{3,2},{4,5},{5,4},{6,7},{7,6},{8,9},{9,8},{10,11... | collective-permute-start | bytes 3932168 | tf_op jit(solution)/shard_map/ppermute | solution.py:450
  681.4 44.3 %collective-permute-start.19 = (bf16[1280,480]{0,1:T(8,128)(2,1)S(1)}, bf16[1280,480]{0,1:T(8,128)(2,1)S(1)}, u32[]{:S(2)}, u32[]{:S(2)}) collective-permute-start(bf16[1280,480]{0,1:T(8,128)(2,1)S(1)} %add_convert_fusion.16), channel_id=1, source_target_pairs={{0,4},{2,6},{4,0},{6,2},{1,5},{3,7},{5,1},{7,3},{8,12},{10,14},{12... | collective-permute-start | bytes 3686408 | tf_op jit(solution)/shard_map/ppermute | solution.py:450
  731.0 28.8 %collective-permute-start.21 = (bf16[320,480]{0,1:T(8,128)(2,1)S(1)}, bf16[320,480]{0,1:T(8,128)(2,1)S(1)}, u32[]{:S(2)}, u32[]{:S(2)}) collective-permute-start(bf16[320,480]{0,1:T(8,128)(2,1)S(1)} %get-tuple-element.179), channel_id=1, source_target_pairs={{0,16},{8,24},{16,0},{24,8},{1,17},{9,25},{17,1},{25,9},{2,18},{10... | collective-permute-start | bytes 921608 | tf_op jit(solution)/shard_map/ppermute | solution.py:510
  (136 other events, 1873.1 us)

commit v3 on v2

--- a/solution.py
+++ b/solution.py
@@ -129,9 +129,16 @@
         return remote(there, there, c_send.at[w.index, j, which], c_recv.at[w.index, j, which], ctx=beside)
 
     def share(w, j):
-        if w.split == 4:
+        if w.split == 4 and w is not up:
             x_copy(w, j).start()
         c_copy(w, j, 0).start()
+
+    def push(w):
+        def one(j, carry):
+            x_copy(w, j).start()
+            return carry
+
+        lax.fori_loop(0, shard, one, 0)
 
     def begin(w):
         pl.when(i < shard - 1)(lambda: z_copy(w, i, 1).start())
@@ -179,11 +186,10 @@
         lax.fori_loop(0, shard, one, 0)
 
     def own_copy(w):
-        source = w.piece.at[pl.ds(pl.multiple_of(w.part * w.rows, 16), w.rows)]
         target = w.slice(i, w.part)
         if w is out:
             target = target.at[me]
-        return pltpu.make_async_copy(source, target, own_sem.at[w.index])
+        return pltpu.make_async_copy(w.piece, target, own_sem.at[w.index])
 
     for w in everything:
         own_copy(w).start()
@@ -204,7 +210,6 @@
             for d in range(1, tp):
                 y_copy(lax.rem(me + tp - d, tp), lax.rem(me + tp - d, tp), d).wait_recv()
             begin(out)
-            begin(up)
         arrive(qkv, hop)
     cross(qkv)
     settle(qkv)
@@ -291,28 +296,31 @@
     send_pair(0)
     project(1)
     for hop in range(1, shard):
+        if hop == shard - 1:
+            begin(up)
         arrive(out, hop)
+    for hop in range(1, shard - 1):
+        arrive(up, hop)
     begin(down)
-    arrive(up, 1)
     cross(out)
     take_pair(0)
     send_pair(1)
-    arrive(up, 2)
+    arrive(up, shard - 1)
+    push(up)
     attend(0, 0, half)
-    arrive(up, 3)
+    arrive(down, 1)
     attend(0, half, heads)
     send_attended(0)
     keep_pairs = [pltpu.make_async_copy(pairs_ref.at[m], kv_ref.at[m], last_sem.at[3 + m]) for m in range(2)]
     keep_pairs[0].start()
-    arrive(down, 1)
-    cross(up)
+    for hop in range(2, shard - 1):
+        arrive(down, hop)
     take_pair(1)
-    attend(1, 0, half)
-    arrive(down, 2)
-    attend(1, half, heads)
+    attend(1, 0, heads)
     send_attended(1)
     keep_pairs[1].start()
-    arrive(down, 3)
+    cross(up)
+    arrive(down, shard - 1)
     settle(out)
     settle(up)
     settle(down)
@@ -337,7 +345,7 @@
 def opening(sizes, valid, normed, bias, qkv, out, up, down):
     shard, ctx, tp = sizes
     width = qkv.shape[1] // 3
-    model = qkv.shape[0] * shard
+    model = qkv.shape[0] * 4 * shard
     rows = normed.shape[1] // 2
     heads = width // HEAD_DIM
     low = lambda *shape: jax.ShapeDtypeStruct(shape, LOW)
@@ -346,7 +354,7 @@
     keys = ctx * rows
     return pl.pallas_call(
         functools.partial(opening_kernel, sizes),
-        in_specs=[pl.BlockSpec(memory_space=pltpu.SMEM), vmem, vmem] + [anywhere] * 4,
+        in_specs=[pl.BlockSpec(memory_space=pltpu.SMEM)] + [vmem] * 6,
         out_specs=[anywhere] * 4 + [vmem, anywhere, anywhere, anywhere, vmem],
         out_shape=[
             low(model, 3 * width),
@@ -389,61 +397,65 @@
     )(valid, normed, bias, qkv, out, up, down)
 
 
-def backward_kernel(valid_ref, q_ref, g_ref, a_ref, inverse_ref, e_ref, *refs, blocks):
-    k_refs, v_refs = refs[:blocks], refs[blocks:2*blocks]
-    dq_ref = refs[2*blocks]
-    dk_refs, dv_refs = refs[2*blocks+1:3*blocks+1], refs[3*blocks+1:4*blocks+1]
-    acc_ref = refs[4*blocks+1]
-    q = q_ref[...]
-    g32 = g_ref[...].astype(jnp.float32) * inverse_ref[0, 0:1]
-    delta = jnp.sum(g32 * a_ref[...].astype(jnp.float32), axis=0, keepdims=True)
-    g = g32.astype(jnp.bfloat16)
-    span = k_refs[0].shape[1]
-    step=min(STEP,span)
+def backward_kernel(q_ref, g_ref, a_ref, inverse_ref, e_ref, pairs_ref, dq_ref, pairs_grad_ref, acc_ref):
+    ctx, rows = pairs_ref.shape[1], pairs_ref.shape[4]
+    q = q_ref[0]
+    g32 = g_ref[...].astype(jnp.float32) * inverse_ref[0, 0, 0:1]
+    delta = jnp.sum(g32 * a_ref[0, 0].astype(jnp.float32), axis=0, keepdims=True)
+    g = g32.astype(LOW)
+    sub = min(SUB, rows)
     acc_ref[...] = jnp.zeros(acc_ref.shape, jnp.float32)
-    for b in range(blocks):
-        for off in range(0, span, step):
-            left = valid_ref[b] - off
-            cols = slice(off, off+step)
-            rows = slice(b*span+off, b*span+off+step)
-            def work():
-                sub = min(SUB, step)
-                parts = [(slice(off+o, off+o+sub), slice(b*span+off+o, b*span+off+o+sub)) for o in range(0, step, sub)]
-                dps = [contract(v_refs[b][:, c], g, ((0,), (0,))) for c, r in parts]
-                total = None
-                for (c, r), dp in zip(parts, dps):
-                    e = e_ref[0, r]
-                    dv_refs[b][:, c] = contract(g, e, ((1,), (1,))).astype(jnp.bfloat16)
-                    ds = (e.astype(jnp.float32) * (dp - delta)).astype(jnp.bfloat16)
-                    t = contract(k_refs[b][:, c], ds, ((1,), (0,)))
-                    total = t if total is None else total + t
-                    dk_refs[b][:, c] = (contract(q, ds, ((1,), (1,))) * math.log(2.0)).astype(jnp.bfloat16)
-                acc_ref[...] += total
-            work()
-    dq_ref[...] = (acc_ref[...] * HEAD_DIM**-0.5).astype(jnp.bfloat16)
-
-def attention_backward(valid, q, g, a, inverse, e, kv):
-    width, rows = q.shape
-    heads = width // HEAD_DIM
-    blocks, span = len(kv), kv[0].shape[1]
-    head = lambda h: (h, 0)
-    value = lambda h: (heads + h, 0)
-    hspec = pl.BlockSpec((HEAD_DIM, rows), head)
-    kspec = pl.BlockSpec((HEAD_DIM, span), head)
-    vspec = pl.BlockSpec((HEAD_DIM, span), value)
-    out = jax.ShapeDtypeStruct((width, span), jnp.bfloat16)
+    for b in range(ctx):
+        to = (b % 2) * 2 + b // 2
+        parts = [(slice(o, o + sub), slice(b * rows + o, b * rows + o + sub)) for o in range(0, rows, sub)]
+        grads = [contract(pairs_ref[0, b, 1, :, c], g, ((0,), (0,))) for c, _ in parts]
+        total = None
+        for (c, r), grad in zip(parts, grads):
+            e = e_ref[0, 0, r]
+            pairs_grad_ref[to, 1, :, c] = contract(g, e, ((1,), (1,))).astype(LOW)
+            ds = (e.astype(jnp.float32) * (grad - delta)).astype(LOW)
+            term = contract(pairs_ref[0, b, 0, :, c], ds, ((1,), (0,)))
+            total = term if total is None else total + term
+            pairs_grad_ref[to, 0, :, c] = (contract(q, ds, ((1,), (1,))) * math.log(2.0)).astype(LOW)
+        acc_ref[...] += total
+    dq_ref[...] = (acc_ref[...] * SCALE).astype(LOW)
+
+
+def attention_backward(micro, own, queries, grad, attended, inverses, kept, pairs):
+    _, width, rows = queries.shape
+    heads, ctx = width // HEAD_DIM, pairs.shape[1]
+    keys = ctx * rows
+    pairs = pairs.reshape(pairs.shape[0], ctx, 2, width, rows)
+    grid = pltpu.PrefetchScalarGridSpec(
+        num_scalar_prefetch=1,
+        grid=(heads,),
+        in_specs=[
+            pl.BlockSpec((1, HEAD_DIM, rows), lambda h, own: (micro, h, 0)),
+            pl.BlockSpec((HEAD_DIM, rows), lambda h, own: (h, 0)),
+            pl.BlockSpec((1, 1, HEAD_DIM, rows), lambda h, own: (micro, own[0], h, 0)),
+            pl.BlockSpec((1, 1, 8, rows), lambda h, own: (micro, h, 0, 0)),
+            pl.BlockSpec((1, 1, keys, rows), lambda h, own: (micro, h, 0, 0)),
+            pl.BlockSpec((1, ctx, 2, HEAD_DIM, rows), lambda h, own: (micro, 0, 0, h, 0)),
+        ],
+        out_specs=[
+            pl.BlockSpec((HEAD_DIM, rows), lambda h, own: (h, 0)),
+            pl.BlockSpec((ctx, 2, HEAD_DIM, rows), lambda h, own: (0, 0, h, 0)),
+        ],
+        scratch_shapes=[pltpu.VMEM((HEAD_DIM, rows), jnp.float32)],
+    )
     return pl.pallas_call(
-        functools.partial(backward_kernel, blocks=blocks),
-        grid=(heads,),
-        in_specs=[pl.BlockSpec(memory_space=pltpu.SMEM), hspec, hspec, hspec, pl.BlockSpec((1,8,rows), lambda h:(h,0,0)), pl.BlockSpec((1, blocks*span, rows), lambda h:(h,0,0))]
-          + [kspec]*blocks + [vspec]*blocks,
-        out_specs=[hspec] + [kspec]*(2*blocks),
-        out_shape=[jax.ShapeDtypeStruct((width, rows), jnp.bfloat16)] + [out]*(2*blocks),
-        scratch_shapes=[pltpu.VMEM((HEAD_DIM, rows), jnp.float32)],
-        compiler_params=pltpu.CompilerParams(vmem_limit_bytes=40<<20),
-        cost_estimate=pl.CostEstimate(flops=8*rows*blocks*span*256*heads, bytes_accessed=heads*blocks*span*rows*2, transcendentals=0),
+        lambda own_ref, *refs: backward_kernel(*refs),
+        grid_spec=grid,
+        out_shape=[
+            jax.ShapeDtypeStruct((width, rows), LOW),
+            jax.ShapeDtypeStruct((ctx, 2, width, rows), LOW),
+        ],
+        compiler_params=pltpu.CompilerParams(vmem_limit_bytes=40 << 20),
+        cost_estimate=pl.CostEstimate(
+            flops=8 * rows * keys * 256 * heads, bytes_accessed=heads * keys * rows * 2, transcendentals=0
+        ),
         name="attention_backward",
-    )(valid, q, g, a, inverse, e, *kv, *kv)
+    )(own, queries, grad, attended, inverses, kept, pairs)
 
 
 def swap(value, axis, bit, size):
@@ -458,71 +470,324 @@
     return found
 
 
-def spread(value, axis, size):
-    blocks = {0: value}
-    for bit in bits_of(size):
-        blocks.update({mask | bit: swap(blocks[mask], axis, bit, size) for mask in list(blocks)})
-    return [blocks[mask] for mask in range(size)]
-
-
-def pair_sum(value, axis, size):
+def low_sum_start(value, axis, size):
+    total = value.astype(LOW)
+    if size == 1:
+        return total, jnp.zeros_like(total)
     for bit in reversed(bits_of(size)):
-        value = value + swap(value, axis, bit, size)
-    return value
+        got = swap(total, axis, bit, size)
+        if bit == size // 2:
+            return total, got
+        total = (total.astype(jnp.float32) + got.astype(jnp.float32)).astype(LOW)
 
 
 def low_sum(value, axis, size):
-    if size == 1:
-        return value
-    total = value.astype(LOW)
-    for bit in reversed(bits_of(size)):
-        total = (total.astype(jnp.float32) + swap(total, axis, bit, size).astype(jnp.float32)).astype(LOW)
-    return total.astype(jnp.float32)
-
-
-def canonical(blocks, axis, size):
-    me = lax.axis_index(axis)
-    out = jnp.zeros((size,) + blocks[0].shape, blocks[0].dtype)
-    for mask, block in enumerate(blocks):
-        out = lax.dynamic_update_index_in_dim(out, block, me ^ mask, 0)
-    return out
-
-
-def scatter_ctx(chunk, ctx):
-    def total(mask, bits):
-        if len(bits) == 0:
-            return chunk(mask)
-        bit, rest = bits[0], bits[1:]
-        away = total(mask | bit, rest).astype(LOW)
-        return total(mask, rest) + swap(away, "ctx", bit, ctx).astype(jnp.float32)
-
-    return total(0, bits_of(ctx))
-
-
-def scatter_rows(full, size):
-    me = lax.axis_index("shard")
-    rows = full.shape[0] // size
-    total = lax.dynamic_slice_in_dim(full, me * rows, rows, 0)
-    low = full.astype(LOW)
-    for shift in range(1, size):
-        there = lax.rem(me + shift, size)
-        block = lax.dynamic_slice_in_dim(low, there * rows, rows, 0)
-        got = lax.ppermute(block, "shard", [(k, (k + shift) % size) for k in range(size)])
-        total = total + got.astype(jnp.float32)
-    return total
-
-
-def weight_grad(left, right, right_dim, shard, ctx):
-    count = right.shape[right_dim] // ctx
+    total, got = low_sum_start(value, axis, size)
+    return (total.astype(jnp.float32) + got.astype(jnp.float32)).astype(LOW).astype(jnp.float32)
+
+
+class Gradient:
+    def __init__(self, index, across_first, terms, refs):
+        self.index, self.across_first, self.terms = index, across_first, terms
+        self.result, self.near, self.far, self.hops, self.crossed = refs
+        self.sums = (self.near, self.far)
+        self.halves = (0,) if across_first else (0, 1)
+
+
+def closing_kernel(sizes, across_first, small_ref, first_ref, *refs):
+    shard, ctx, tp = sizes
+    units = len(across_first)
+    terms, refs = refs[: 4 * units], refs[4 * units :]
+    results, refs = refs[:units], refs[units:]
+    small_out, first_out, refs = refs[0], refs[1], refs[2:]
+    scratch, refs = refs[: 4 * units], refs[4 * units :]
+    small_got, first_got, c_send, c_recv, x_send, x_recv, z_send, z_recv, g_send, g_recv, v_send, v_recv = refs
+    i, p, me = lax.axis_index("shard"), lax.axis_index("ctx"), lax.axis_index("tp")
+    across, beside = flip(p, 2), flip(p, 1)
+    grads = [
+        Gradient(u, across_first[u], terms[4 * u : 4 * u + 4], (results[u],) + tuple(scratch[4 * u : 4 * u + 4]))
+        for u in range(units)
+    ]
+
+    def remote(source, target, send, recv, **device):
+        return pltpu.make_async_remote_copy(
+            src_ref=source, dst_ref=target, send_sem=send, recv_sem=recv,
+            device_id=device, device_id_type=pl.DeviceIdType.MESH,
+        )
+
+    barrier = pltpu.get_barrier_semaphore()
+
+    def greet(**device):
+        pl.semaphore_signal(barrier, inc=1, device_id=device, device_id_type=pl.DeviceIdType.MESH)
+
+    partners = [("tp", me, bit) for bit in reversed(bits_of(tp))]
+    partners += [("ctx", p, bit) for bit in reversed(bits_of(ctx))]
+    partners += [("shard", i, bit) for bit in reversed(bits_of(shard))]
+    for axis, index, bit in partners:
+        greet(**{axis: flip(index, bit)})
+    skipped = jnp.where(i > 0, jnp.where(lax.rem(i, 2) == 0, 1, 0), 0)
+    ahead = jnp.where(i < shard - 1, jnp.where(lax.rem(i, 2) == 1, 1, 0), 0)
+    pl.when(skipped == 1)(lambda: greet(shard=i - 1))
+    pl.when(ahead == 1)(lambda: greet(shard=i + 1))
+    pl.semaphore_wait(barrier, len(partners) + skipped + ahead)
+
+    def rows_of(ref, j):
+        each = ref.shape[-2] // shard
+        return ref.at[pl.ds(pl.multiple_of(j * each, 16), each)]
+
+    def c_copy(g, j, which):
+        source = g.terms[3 if which else 1]
+        target = g.far if which else g.near
+        return remote(
+            rows_of(source, j), rows_of(target, j),
+            c_send.at[g.index, j, which], c_recv.at[g.index, j, which], ctx=beside,
+        )
+
+    def x_copy(g, j):
+        return remote(
+            rows_of(g.sums[1], j), rows_of(g.crossed, j), x_send.at[g.index, j], x_recv.at[g.index, j], ctx=across
+        )
+
+    def z_copy(g, half, way, step, j):
+        return remote(
+            rows_of(g.sums[half], j), g.hops.at[half, way, step],
+            z_send.at[g.index, half, way, step], z_recv.at[g.index, half, way, step], shard=i + 1 - 2 * way,
+        )
+
+    def add_to(target, value):
+        target[...] = (target[...].astype(jnp.float32) + value.astype(jnp.float32)).astype(LOW)
+
+    def every_shard(one):
+        lax.fori_loop(0, shard, lambda j, carry: (one(j), carry)[1], 0)
+
+    for g in grads:
+        for j in range(shard):
+            c_copy(g, j, 0).start()
+            c_copy(g, j, 1).start()
+
+    def meet(g, j):
+        c_copy(g, j, 0).wait_recv()
+        c_copy(g, j, 1).wait_recv()
+        for half, got in ((0, g.near), (1, g.far)):
+            add_to(rows_of(got, j), rows_of(g.terms[2 * half], j)[...])
+        if g.across_first:
+            x_copy(g, j).start()
+
+    def joined(g, j):
+        x_copy(g, j).wait_recv()
+        add_to(rows_of(g.sums[0], j), rows_of(g.crossed, j)[...])
+
+    def hop(g, step):
+        for half in g.halves:
+            for way, at in ((0, i), (1, shard - 1 - i)):
+                j = shard - 1 - step + at if way == 0 else step - at
+
+                @pl.when((at <= step) & (at < shard - 1))
+                def _():
+                    @pl.when(at > 0)
+                    def _():
+                        z_copy(g, half, way, step - 1, j).wait_recv()
+                        add_to(rows_of(g.sums[half], j), g.hops[half, way, step - 1])
+
+                    z_copy(g, half, way, step, j).start()
+
+    def arrive(g):
+        for half in g.halves:
+            for way, at in ((0, i), (1, shard - 1 - i)):
+
+                @pl.when(at > 0)
+                def _():
+                    z_copy(g, half, way, shard - 2, i).wait_recv()
+                    add_to(rows_of(g.sums[half], i), g.hops[half, way, shard - 2])
+
+    def side_copy(g):
+        return remote(rows_of(g.sums[1], i), g.crossed, x_send.at[g.index, 0], x_recv.at[g.index, 0], ctx=across)
+
+    def spread_copy(g, which):
+        owner = across if which == 2 else p
+        to = across if which == 0 else beside
+        return remote(
+            g.result.at[owner], g.result.at[owner], g_send.at[g.index, which], g_recv.at[g.index, which], ctx=to
+        )
+
+    def spread_arriving(g, which):
+        owner = (across, beside, flip(across, 1))[which]
+        to = across if which == 0 else beside
+        return remote(
+            g.result.at[owner], g.result.at[owner], g_send.at[g.index, which], g_recv.at[g.index, which], ctx=to
+        )
+
+    def finish(g):
+        g.result[p] = rows_of(g.sums[0], i)[...]
+        spread_copy(g, 0).start()
+        spread_copy(g, 1).start()
+
+    vectors = ((0, small_ref, small_out, small_got), (1, first_ref, first_out, first_got))
+
+    def v_copy(number, which):
+        axis, index, bit = partners[number]
+        _, _, total, got = vectors[which]
+        return remote(
+            total.at[number], got.at[number], v_send.at[number, which], v_recv.at[number, which], **{axis: flip(index, bit)}
+        )
+
+    def meant(number):
+        return (1,) if partners[number][0] == "tp" else (0, 1)
+
+    def vector_start(number):
+        for which in meant(number):
+            v_copy(number, which).start()
+
+    def vector_take(number):
+        for which, _, total, got in vectors:
+            if which in meant(number):
+                v_copy(number, which).wait_recv()
+                total[number + 1] = total[number] + got[number]
+            else:
+                total[number + 1] = total[number]
+
+    small_out[0] = small_ref[...]
+    first_out[0] = first_ref[...]
+    vector_start(0)
+    sent_across = [g for g in grads if g.across_first]
+    sent_along = [g for g in grads if not g.across_first]
+    for g in sent_across[:1] + sent_along + sent_across[1:]:
+        every_shard(lambda j: meet(g, j))
+        if not g.across_first:
+            for step in range(1):
+                hop(g, step)
+    number = 0
+
+    def next_vector():
+        nonlocal number
+        if number < len(partners):
+            vector_take(number)
+            number += 1
+            if number < len(partners):
+                vector_start(number)
+
+    for step in range(1, shard - 1):
+        for g in sent_along:
+            hop(g, step)
+        next_vector()
+    for g in sent_across:
+        every_shard(lambda j: joined(g, j))
+        hop(g, 0)
+        next_vector()
+    for g in sent_along:
+        arrive(g)
+        side_copy(g).start()
+    for step in range(1, shard - 1):
+        for g in sent_across:
+            hop(g, step)
+        next_vector()
+    for g in sent_along:
+        side_copy(g).wait_recv()
+        add_to(rows_of(g.sums[0], i), g.crossed[...])
+        finish(g)
+    for g in sent_across:
+        arrive(g)
+        finish(g)
+    while number < len(partners):
+        next_vector()
+    for g in grads:
+        spread_arriving(g, 0).wait_recv()
+        spread_copy(g, 2).start()
+    for g in grads:
+        spread_arriving(g, 1).wait_recv()
+        spread_arriving(g, 2).wait_recv()
+    for g in grads:
+
+        def drain(j):
+            c_copy(g, j, 0).wait_send()
+            c_copy(g, j, 1).wait_send()
+            if g.across_first:
+                x_copy(g, j).wait_send()
+
+        every_shard(drain)
+        if not g.across_first:
+            side_copy(g).wait_send()
+        for half in g.halves:
+            for way, at in ((0, i), (1, shard - 1 - i)):
+                for step in range(shard - 1):
+                    j = shard - 1 - step + at if way == 0 else step - at
+
+                    @pl.when((at <= step) & (at < shard - 1))
+                    def _():
+                        z_copy(g, half, way, step, j).wait_send()
+
+        for which in range(3):
+            spread_copy(g, which).wait_send()
+    for n in range(len(partners)):
+        for which in meant(n):
+            v_copy(n, which).wait_send()
+
+
+def closing(sizes, across_first, small, first, terms):
+    shard, ctx, tp = sizes
+    units = len(across_first)
+    vmem = pl.BlockSpec(memory_space=pltpu.VMEM)
+    dma = pltpu.SemaphoreType.DMA
+    stages = len(bits_of(tp)) + len(bits_of(ctx)) + len(bits_of(shard))
+    shapes = [t[0].shape for t in terms]
+    scratch = []
+    for (model, n), early in zip(shapes, across_first):
+        each, halves = model // shard, 1 if early else 2
+        scratch += [
+            pltpu.VMEM((model, n), LOW),
+            pltpu.VMEM((model, n), LOW),
+            pltpu.VMEM((halves, 2, shard - 1, each, n), LOW),
+            pltpu.VMEM((model, n) if early else (each, n), LOW),
+        ]
+    found = pl.pallas_call(
+        functools.partial(closing_kernel, sizes, across_first),
+        in_specs=[vmem] * (2 + 4 * units),
+        out_specs=[vmem] * (units + 2),
+        out_shape=[jax.ShapeDtypeStruct((ctx, model // shard, n), LOW) for model, n in shapes]
+        + [jax.ShapeDtypeStruct((stages + 1,) + v.shape, jnp.float32) for v in (small, first)],
+        scratch_shapes=scratch
+        + [pltpu.VMEM((stages,) + v.shape, jnp.float32) for v in (small, first)]
+        + [
+            dma((units, shard, 2)),
+            dma((units, shard, 2)),
+            dma((units, shard)),
+            dma((units, shard)),
+            dma((units, 2, 2, shard - 1)),
+            dma((units, 2, 2, shard - 1)),
+            dma((units, 3)),
+            dma((units, 3)),
+            dma((stages, 2)),
+            dma((stages, 2)),
+        ],
+        compiler_params=pltpu.CompilerParams(collective_id=1, has_side_effects=True, vmem_limit_bytes=56 << 20),
+        cost_estimate=pl.CostEstimate(flops=0, bytes_accessed=200 << 20, transcendentals=0),
+        name="closing",
+    )(small, first, *[t for four in terms for t in four])
+    return found[:units], found[units][stages], found[units + 1][stages]
+
+
+def weight_terms(lefts, rights, right_dim, ctx):
+    count = rights[0].shape[right_dim] // ctx
     me = lax.axis_index("ctx")
 
-    def chunk(mask):
-        part = lax.dynamic_slice_in_dim(right, (me ^ mask) * count, count, right_dim)
-        return contract(left, part, ((0,), (1 - right_dim,)))
-
-    mine = scatter_rows(scatter_ctx(chunk, ctx), shard).astype(LOW)
-    blocks = canonical(spread(mine, "ctx", ctx), "ctx", ctx)
-    return jnp.moveaxis(blocks, 0, 1).reshape(mine.shape[0], ctx * count).astype(jnp.float32)
+    def term(mask):
+        total = 0.0
+        for left, right in zip(lefts, rights):
+            part = lax.dynamic_slice_in_dim(right, (me ^ mask) * count, count, right_dim)
+            total = total + contract(left, part, ((0,), (1 - right_dim,)))
+        return total.astype(LOW)
+
+    return [term(mask) for mask in range(ctx)]
+
+
+def whole_rows(blocks):
+    ctx, each, n = blocks.shape
+    return jnp.moveaxis(blocks, 0, 1).reshape(each, ctx * n).astype(jnp.float32)
+
+
+def as_tiles(vector):
+    count = -(-vector.shape[0] // 1024) * 1024
+    return jnp.pad(vector, (0, count - vector.shape[0])).reshape(-1, 128)
 
 
 def normalize(values):
@@ -570,15 +835,20 @@
     bias = jnp.concatenate([query_bias, jnp.zeros_like(query_bias), value_bias])[:, None]
     ids = ctx_index ^ jnp.arange(ctx, dtype=jnp.int32)
     valid = [jnp.clip(lengths[m, 0] - rows * ids, 0, rows) for m in range(micros)]
+
+    def own_part(weight, split):
+        count = weight.shape[0] // split
+        return lax.dynamic_slice_in_dim(weight, lax.rem(ctx_index, split) * count, count, 0)
+
     full_qkv, full_out, full_up, full_down, queries, pairs, all_attended, kept, inverses = opening(
         sizes,
         jnp.stack(valid),
         jnp.concatenate(normed1, axis=0).T,
         bias,
-        jnp.concatenate([query_weight, key_weight, value_weight], axis=1),
-        out_weight,
-        up_weight,
-        down_weight,
+        jnp.concatenate([own_part(w, 4) for w in (query_weight, key_weight, value_weight)], axis=1),
+        own_part(out_weight, 4),
+        own_part(up_weight, 4),
+        own_part(down_weight, 2),
     )
     tp_index = lax.axis_index("tp")
     own_out = lax.dynamic_index_in_dim(full_out, tp_index, 0, keepdims=False)
@@ -608,41 +878,42 @@
         )
         branch_grads.append(mixed_grads[m].astype(LOW))
     projected_grads, normed1_terms, input_grads = [], [], []
+
+    def finish_pairs(query_grad, chip):
+        pair_grad = (chip[0].astype(jnp.float32) + swap(chip[1], "ctx", 2, ctx).astype(jnp.float32)).astype(LOW)
+        return jnp.concatenate([query_grad, pair_grad.reshape(2 * width, rows)], axis=0)
+
     for m in range(micros):
         attended_grad = contract(own_out, branch_grads[m], ((0,), (1,))).astype(LOW)
-        parts = attention_backward(
-            valid[m], queries[m], attended_grad, attended[m], inverses[m], kept[m], [pairs[m, b] for b in range(ctx)]
+        if m > 0:
+            attended_grad, chip = lax.optimization_barrier((attended_grad, chip))
+            projected_grads.append(finish_pairs(query_grad, chip))
+        query_grad, pairs_grad = attention_backward(
+            m, tp_index[None], queries, attended_grad, all_attended, inverses, kept, pairs
         )
-        terms = [
-            jnp.concatenate([parts[1 + mask], parts[1 + ctx + mask]], axis=0) for mask in range(ctx)
-        ]
-        pair_grad = scatter_ctx(lambda mask: terms[mask].astype(jnp.float32), ctx).astype(LOW)
-        projected_grads.append(jnp.concatenate([parts[0], pair_grad], axis=0))
+        chip = (
+            pairs_grad[: ctx // 2].astype(jnp.float32) + swap(pairs_grad[ctx // 2 :], "ctx", 1, ctx).astype(jnp.float32)
+        ).astype(LOW)
+    projected_grads.append(finish_pairs(query_grad, chip))
+    for m in range(micros):
         normed1_terms.append(contract(projected_grads[m], full_qkv, ((0,), (1,))))
-    gain1, bias1 = [], []
+    gain1, bias1, normed1_grads = [], [], []
     for m in range(micros):
         hat, inverse = hats1[m]
         gain1.append(jnp.sum(normed1_terms[m] * hat, axis=0))
         bias1.append(jnp.sum(normed1_terms[m], axis=0))
-        total = low_sum(normed1_terms[m], "tp", tp)
-        input_grads.append(mixed_grads[m] + normalize_grad(total * norm1_gain, hat, inverse))
+        normed1_grads.append(low_sum_start(normed1_terms[m], "tp", tp))
 
     def over(items, dim):
         return jnp.concatenate(items, axis=dim)
 
-    up_grad = weight_grad(over(normed2, 0), over(hidden_grads, 0), 1, shard, ctx)
-    down_grad = weight_grad(over([cotangent[m, 0] for m in range(micros)], 0), over(active, 0), 1, shard, ctx)
-    out_grad = weight_grad(over(branch_grads, 0), over(attended, 1), 0, shard, ctx)
-    projected_all = over(projected_grads, 1)
-    qkv_grad = weight_grad(over(normed1, 0), projected_all, 0, shard, ctx)
-
     def row_sum(items):
         return sum(jnp.sum(item.astype(jnp.float32), axis=0) for item in items)
 
     small = jnp.concatenate(
         [
-            jnp.sum(projected_all[:width].astype(jnp.float32), axis=1),
-            jnp.sum(projected_all[2 * width :].astype(jnp.float32), axis=1),
+            sum(jnp.sum(g[:width].astype(jnp.float32), axis=1) for g in projected_grads),
+            sum(jnp.sum(g[2 * width :].astype(jnp.float32), axis=1) for g in projected_grads),
             row_sum(hidden_grads),
             row_sum(mixed_grads),
             row_sum([normed2_grads[m] * hats2[m][0] for m in range(micros)]),
@@ -651,9 +922,25 @@
         ]
     )
     first = jnp.concatenate([sum(gain1), sum(bias1)])
-    first = pair_sum(first, "tp", tp)
-    small = jnp.concatenate([small, first])
-    small = pair_sum(pair_sum(small, "ctx", ctx), "shard", shard)
+    blocks, small_sum, first_sum = closing(
+        sizes,
+        (False, False, True, True),
+        as_tiles(small),
+        as_tiles(first),
+        (
+            weight_terms(normed1, projected_grads, 0, ctx),
+            weight_terms(branch_grads, attended, 0, ctx),
+            weight_terms([over(normed2, 0)], [over(hidden_grads, 0)], 1, ctx),
+            weight_terms([over([cotangent[m, 0] for m in range(micros)], 0)], [over(active, 0)], 1, ctx),
+        ),
+    )
+    mine, blocks = lax.optimization_barrier(([total for total, _ in normed1_grads], blocks))
+    normed1_grads = [a.astype(jnp.float32) + b[1].astype(jnp.float32) for a, b in zip(mine, normed1_grads)]
+    for m in range(micros):
+        hat, inverse = hats1[m]
+        input_grads.append(mixed_grads[m] + normalize_grad(normed1_grads[m] * norm1_gain, hat, inverse))
+    qkv_grad, out_grad, up_grad, down_grad = [whole_rows(b) for b in blocks]
+    small = jnp.concatenate([small_sum.reshape(-1)[: small.shape[0]], first_sum.reshape(-1)[: first.shape[0]]])
     model = norm1_gain.shape[0]
     cuts, at = [], 0
     for count in (width, width, up_bias.shape[0], model, model, model, model, model, model):

time: 814 us -> 711 us (0.87)
  waiting for transfers between devices: 166 us -> 26.4 us
  Pallas kernels: 247 us -> 357 us
  starting transfers between devices: 64 us -> 9.31 us
  local copies, waits for them, and re-layouts: 126 us -> 99.3 us
  matrix products: 114 us -> 140 us
  other arithmetic: 80.6 us -> 68 us
    pallas_call x2 -> x3, Pallas kernels: 37.2 us -> 203 us  [the longest x1 165 us: closing(): pl.pallas_call(functools.partial(closing_kernel, sizes, across_first), in...]
    ppermute x41 -> x10, waiting for transfers between devices: 113 us -> 26.4 us  [swap(): return lax.ppermute(value, axis, [(k, k ^ bit) for k in range(size)])]
    pallas_call x1, Pallas kernels: 210 us -> 154 us  [opening(): pl.pallas_call(functools.partial(opening_kernel, sizes), in_specs=[pl.Blo...]
    ppermute x12 -> x0, waiting for transfers between devices: 53.6 us -> none  [scatter_rows(): lax.ppermute(block, 'shard', [(k, (k + shift) % size) for k in range(size)])]
    dynamic_update_slice x14 -> x0, local copies, waits for them, and re-layouts: 35.3 us -> none  [canonical(): out = lax.dynamic_update_index_in_dim(out, block, me ^ mask, 0)]
    ppermute x41 -> x10, starting transfers between devices: 42.5 us -> 9.31 us  [swap(): return lax.ppermute(value, axis, [(k, k ^ bit) for k in range(size)])]
    squeeze x6 -> x2, local copies, waits for them, and re-layouts: 30.3 us -> 1.39 us  [finish_pairs(): chip[1]]
    dot_general x32 -> x40, matrix products: 114 us -> 140 us  [contract(): lax.dot_general(left, right, (dims, ((), ())), preferred_element_type=jnp...]
  transfers between devices with their start and end apart: 53 -> 10, of which waited for: 17 -> 2; matrix products, arithmetic and copies ran while one was open for 31% -> 31% of each run, Pallas kernels for 5% -> 29%
where the time goes in v3:
time: 711 us; the launch traced here: 703 us
  Pallas kernels  357 us (50%)
  matrix products  140 us (20%)
  local copies, waits for them, and re-layouts  99.3 us (14%)
  other arithmetic  68 us (10%)
  waiting for transfers between devices  26.4 us (4%)
  starting transfers between devices  9.31 us (1%)
    pallas_call x1, Pallas kernels, closing(): pl.pallas_call(functools.partial(closing_kernel, sizes, across_first), in...  165 us
    pallas_call x1, Pallas kernels, opening(): pl.pallas_call(functools.partial(opening_kernel, sizes), in_specs=[pl.Blo...  154 us
    dot_general x40, matrix products, contract(): lax.dot_general(left, right, (dims, ((), ())), preferred_element_type=jnp...  140 us
    pallas_call x2, Pallas kernels, attention_backward(): pl.pallas_call(lambda own_ref, *refs: backward_kernel(*refs), grid_spec=g...  37.8 us
    unnamed x193, local copies, waits for them, and re-layouts  34.8 us
    ppermute x10, waiting for transfers between devices, swap(): return lax.ppermute(value, axis, [(k, k ^ bit) for k in range(size)])  26.4 us
    convert_element_type x5, local copies, waits for them, and re-layouts, whole_rows(): return jnp.moveaxis(blocks, 0, 1).reshape(each, ctx * n).astype(jnp.float32)  16.7 us
    reduce_sum x3, other arithmetic, row_sum(): return sum((jnp.sum(item.astype(jnp.float32), axis=0) for item in items))  15.1 us
  transfers between devices with their start and end apart: 10, of which 2 were waited for; matrix products, arithmetic and copies ran while one was open for 31% of the time, Pallas kernels for 29%

profile of v3, /device:TPU:9, one launch (start us, length us, event | category | flops | bytes accessed | tf_op | source)
XLA Modules:
  0.0 702.5 jit_solution(9750491563834999928)
XLA Ops:
  29.8 154.0 %opening.1 = (bf16[1280,1920]{1,0:T(8,128)(2,1)}, bf16[2,1280,640]{2,1,0:T(8,128)(2,1)}, bf16[1280,2560]{1,0:T(8,128)(2,1)}, bf16[1280,2560]{1,0:T(8,128)(2,1)},...) custom-call(s32[2,4]{1,0:T(2,128)} %pad_add_fusion.valid_ref, ...), custom_call_target="tpu_custom_call" | custom-call | flops 17179869184 | bytes 83886080 | tf_op jit(solution)/shard_map/opening/pallas_call | solution.py:355
  197.4 4.5 multiply_convert_fusion.1
  202.0 6.0 convert_reduce_fusion.1
  208.0 4.8 convolution_convert_fusion.9
  214.0 4.8 convolution_convert_fusion.11
  219.0 4.5 multiply_convert_fusion
  223.5 5.5 convert_reduce_fusion
  229.0 4.8 convolution_convert_fusion.8
  235.0 4.8 convolution_convert_fusion.10
  246.9 5.5 convolution_convert_fusion.7.refs_8_
  252.4 5.6 convolution_convert_fusion.6.refs_9_
  264.9 5.5 convolution_convert_fusion.5.refs_10_
  270.4 5.6 convolution_convert_fusion.1.refs_14_
  281.3 5.7 convolution_convert_fusion.refs_15_
  290.9 8.8 %collective-permute-done.3 = bf16[512,1280]{0,1:T(8,128)(2,1)} collective-permute-done((bf16[512,1280]{0,1:T(8,128)(2,1)}, bf16[512,1280]{0,1:T(8,128)(2,1)}, u32[]{:S(2)}, u32[]{:S(2)}) %collective-permute-start.3) | collective-permute-done | bytes 1310752 | tf_op jit(solution)/shard_map/ppermute | solution.py:462
  299.8 5.8 fusion.206
  310.2 18.9 %attention_backward.2 = (bf16[640,512]{1,0:T(8,128)(2,1)S(1)}, bf16[4,2,640,512]{3,2,1,0:T(8,128)(2,1)S(1)}) custom-call(s32[1]{0:T(128)} %bitcast.16.own_ref, bf16[2,640,512]{2,1,0:T(8,128)(2,1)S(1)} %copy-done.6, bf16[640,512]{1,0:T(8,128)(2,1)S(1)} %fusion.84.refs_1_, bf16[2,2,640,512]{3,2,1,0:T(8,128)(2,1)S(1)} %copy-done.2, ...), custom_call_target="tpu_custom_call" | custom-call | flops 17179869184 | bytes 16777216 | tf_op jit(solution)/shard_map/attention_backward/pallas_call | solution.py:446
  331.9 5.4 fusion.205
  362.4 18.9 %attention_backward.3 = (bf16[640,512]{1,0:T(8,128)(2,1)S(1)}, bf16[4,2,640,512]{3,2,1,0:T(8,128)(2,1)S(1)}) custom-call(s32[1]{0:T(128)} %bitcast.16.own_ref, bf16[2,640,512]{2,1,0:T(8,128)(2,1)S(1)} %copy-done.7, bf16[640,512]{1,0:T(8,128)(2,1)S(1)} %fusion.87.refs_1_, bf16[2,2,640,512]{3,2,1,0:T(8,128)(2,1)S(1)} %copy-done.3, ...), custom_call_target="tpu_custom_call" | custom-call | flops 17179869184 | bytes 16777216 | tf_op jit(solution)/shard_map/attention_backward/pallas_call | solution.py:446
  396.4 7.3 %fusion.214 = (f32[1280]{0:T(1024)S(1)}, f32[512,1280]{1,0:T(8,128)}) fusion(bf16[1280,1920]{1,0:T(8,128)(2,1)} %get-tuple-element.55, bf16[640,512]{1,0:T(8,128)(2,1)S(1)} %get-tuple-element.52, bf16[1280,512]{1,0:T(8,128)(2,1)S(1)} %bitcast.258), kind=kOutput, calls=%fused_computation.355 | convolution fusion | flops 2521168640 | bytes 9507840 | tf_op jit(solution)/shard_map/dot_general | solution.py:20
  407.2 4.2 fusion.47
  427.8 17.6 %collective-permute-done.7 = bf16[2,640,512]{2,1,0:T(8,128)(2,1)S(1)} collective-permute-done((bf16[2,640,512]{2,1,0:T(8,128)(2,1)S(1)}, bf16[2,640,512]{2,1,0:T(8,128)(2,1)S(1)}, u32[]{:S(2)}, u32[]{:S(2)}) %collective-permute-start.7) | collective-permute-done | bytes 1310752 | tf_op jit(solution)/shard_map/ppermute | solution.py:462
  446.0 4.4 fusion.215
  453.8 4.7 fusion.38
  465.2 4.1 convolution_add_fusion.6
  471.9 4.2 convolution_add_fusion.5
  478.5 4.2 convolution_add_fusion.4
  487.0 165.5 %closing.1 = (bf16[4,320,480]{2,1,0:T(8,128)(2,1)}, bf16[4,320,160]{2,1,0:T(8,128)(2,1)}, bf16[4,320,640]{2,1,0:T(8,128)(2,1)}, bf16[4,320,640]{2,1,0:T(8,128)(2...) custom-call(f32[72,128]{1,0:T(8,128)} %pad_bitcast_fusion.small_ref, f32[24,128]{1,0:T(8,128)} %fusion.158.first_ref, ...), custom_call_target="tpu_custom_call" | custom-call | bytes 209715200 | tf_op jit(solution)/shard_map/closing/pallas_call | solution.py:742
  662.7 4.5 reshape.212
  672.2 4.2 copy.153
  689.3 3.9 fusion.52
  696.1 6.0 copy.139
  (325 shorter events, 186.1 us)
Async XLA Ops:
  0.7 27.4 %copy-start = (bf16[320,2560]{1,0:T(8,128)(2,1)S(1)}, bf16[320,2560]{1,0:T(8,128)(2,1)}, u32[]{:S(2)}) copy-start(bf16[320,2560]{1,0:T(8,128)(2,1)} %param.33) | copy-start | bytes 4915204
  7.0 10.2 %copy-start.9 = (bf16[1,1,512,1280]{2,3,1,0:T(8,128)(2,1)}, bf16[1,1,512,1280]{2,3,1,0:T(8,128)(2,1)S(1)}, u32[]{:S(2)}) copy-start(bf16[1,1,512,1280]{2,3,1,0:T(8,128)(2,1)S(1)} %copy.149) | copy-start | bytes 3932164
  11.6 5.8 copy-start.51
  11.6 7.9 %copy-start.53 = (f32[512]{0:T(512)}, f32[512]{0:T(512)S(1)}, u32[]{:S(2)}) copy-start(f32[512]{0:T(512)S(1)} %broadcast_multiply_fusion.10) | copy-start | bytes 6148
  13.7 5.8 copy-start.55
  194.4 7.6 %slice-start.4 = ((s8[6553600]{0:T(1024)(128)(4,1)}), s8[4194304]{0:T(1024)(128)(4,1)S(1)}, s32[]{:S(2)}) async-start(s8[6553600]{0:T(1024)(128)(4,1)} %bitcast.285), calls=%async_computation.4 | async-start | bytes 8388608
  195.5 6.4 copy-start.45
  195.5 23.5 %copy-start.47 = (bf16[512,1280]{0,1:T(8,128)(2,1)}, bf16[512,1280]{0,1:T(8,128)(2,1)S(1)}, u32[]{:S(2)}) copy-start(bf16[512,1280]{0,1:T(8,128)(2,1)S(1)} %get-tuple-element.168) | copy-start | bytes 3932164
  201.9 12.1 %copy-start.79 = (bf16[512,2560]{1,0:T(8,128)(2,1)}, bf16[512,2560]{1,0:T(8,128)(2,1)S(1)}, u32[]{:S(2)}) copy-start(bf16[512,2560]{1,0:T(8,128)(2,1)S(1)} %get-tuple-element.184) | copy-start | bytes 7864324
  212.8 74.3 %collective-permute-start.2 = (bf16[512,1280]{0,1:T(8,128)(2,1)}, bf16[512,1280]{0,1:T(8,128)(2,1)}, u32[]{:S(2)}, u32[]{:S(2)}) collective-permute-start(bf16[512,1280]{0,1:T(8,128)(2,1)} %convolution_convert_fusion.9), channel_id=1, source_target_pairs={{0,1},{1,0},{2,3},{3,2},{4,5},{5,4},{6,7},{7,6},{8,9},{9,8},{10,11... | collective-permute-start | bytes 3932168 | tf_op jit(solution)/shard_map/ppermute | solution.py:462
  218.8 72.2 %collective-permute-start = (bf16[512,1280]{0,1:T(8,128)(2,1)}, bf16[512,1280]{0,1:T(8,128)(2,1)}, u32[]{:S(2)}, u32[]{:S(2)}) collective-permute-start(bf16[512,1280]{0,1:T(8,128)(2,1)} %convolution_convert_fusion.11), channel_id=1, source_target_pairs={{0,1},{1,0},{2,3},{3,2},{4,5},{5,4},{6,7},{7,6},{8,9},{9,8},{10,11... | collective-permute-start | bytes 3932168 | tf_op jit(solution)/shard_map/ppermute | solution.py:462
  223.5 11.5 %copy-start.81 = (bf16[512,2560]{1,0:T(8,128)(2,1)}, bf16[512,2560]{1,0:T(8,128)(2,1)S(1)}, u32[]{:S(2)}) copy-start(bf16[512,2560]{1,0:T(8,128)(2,1)S(1)} %get-tuple-element.186) | copy-start | bytes 7864324
  233.8 65.9 %collective-permute-start.3 = (bf16[512,1280]{0,1:T(8,128)(2,1)}, bf16[512,1280]{0,1:T(8,128)(2,1)}, u32[]{:S(2)}, u32[]{:S(2)}) collective-permute-start(bf16[512,1280]{0,1:T(8,128)(2,1)} %convolution_convert_fusion.8), channel_id=1, source_target_pairs={{0,1},{1,0},{2,3},{3,2},{4,5},{5,4},{6,7},{7,6},{8,9},{9,8},{10,11... | collective-permute-start | bytes 3932168 | tf_op jit(solution)/shard_map/ppermute | solution.py:462
  239.8 92.0 %collective-permute-start.1 = (bf16[512,1280]{0,1:T(8,128)(2,1)}, bf16[512,1280]{0,1:T(8,128)(2,1)}, u32[]{:S(2)}, u32[]{:S(2)}) collective-permute-start(bf16[512,1280]{0,1:T(8,128)(2,1)} %convolution_convert_fusion.10), channel_id=1, source_target_pairs={{0,1},{1,0},{2,3},{3,2},{4,5},{5,4},{6,7},{7,6},{8,9},{9,8},{10,11... | collective-permute-start | bytes 3932168 | tf_op jit(solution)/shard_map/ppermute | solution.py:462
  287.0 12.7 %copy-start.16 = (f32[512,1280]{0,1:T(8,128)S(1)}, f32[512,1280]{0,1:T(8,128)}, u32[]{:S(2)}) copy-start(f32[512,1280]{0,1:T(8,128)} %copy-done.15) | copy-start | bytes 7864324
  287.0 12.7 %copy-start.37 = (bf16[1,1,512,1280]{2,3,1,0:T(8,128)(2,1)S(1)}, bf16[1,1,512,1280]{2,3,1,0:T(8,128)(2,1)}, u32[]{:S(2)}) copy-start(bf16[1,1,512,1280]{2,3,1,0:T(8,128)(2,1)} %copy.151) | copy-start | bytes 3932164
  287.0 12.7 %copy-start.62 = (f32[1280]{0:T(1024)S(1)}, f32[1280]{0:T(1024)}, u32[]{:S(2)}) copy-start(f32[1280]{0:T(1024)} %param.34) | copy-start | bytes 15364
  329.2 8.1 %copy-start.5 = (bf16[4,2,640,512]{3,2,1,0:T(8,128)(2,1)}, bf16[4,2,640,512]{3,2,1,0:T(8,128)(2,1)S(1)}, u32[]{:S(2)}) copy-start(bf16[4,2,640,512]{3,2,1,0:T(8,128)(2,1)S(1)} %get-tuple-element.53) | copy-start | bytes 15728644
  330.8 26.1 %collective-permute-start.4 = (bf16[2,2,640,512]{3,2,1,0:T(8,128)(2,1)}, bf16[2,2,640,512]{3,2,1,0:T(8,128)(2,1)}, u32[]{:S(2)}, u32[]{:S(2)}) collective-permute-start(bf16[2,2,640,512]{3,2,1,0:T(8,128)(2,1)} %slice.175), channel_id=1, source_target_pairs={{0,2},{2,0},{4,6},{6,4},{1,3},{3,1},{5,7},{7,5},{8,10},{10,8},{12,... | collective-permute-start | bytes 7864328 | tf_op jit(solution)/shard_map/ppermute | solution.py:462
  362.3 32.0 %collective-permute-start.5 = (bf16[2,640,512]{2,1,0:T(8,128)(2,1)}, bf16[2,640,512]{2,1,0:T(8,128)(2,1)}, u32[]{:S(2)}, u32[]{:S(2)}) collective-permute-start(bf16[2,640,512]{2,1,0:T(8,128)(2,1)} %slice_bitcast_fusion.2), channel_id=1, source_target_pairs={{0,4},{2,6},{4,0},{6,2},{1,5},{3,7},{5,1},{7,3},{8,12},{10,14},{12... | collective-permute-start | bytes 3932168 | tf_op jit(solution)/shard_map/ppermute | solution.py:462
  385.4 26.0 %collective-permute-start.6 = (bf16[2,2,640,512]{3,2,1,0:T(8,128)(2,1)}, bf16[2,2,640,512]{3,2,1,0:T(8,128)(2,1)}, u32[]{:S(2)}, u32[]{:S(2)}) collective-permute-start(bf16[2,2,640,512]{3,2,1,0:T(8,128)(2,1)} %slice.179), channel_id=1, source_target_pairs={{0,2},{2,0},{4,6},{6,4},{1,3},{3,1},{5,7},{7,5},{8,10},{10,8},{12,... | collective-permute-start | bytes 7864328 | tf_op jit(solution)/shard_map/ppermute | solution.py:462
  396.4 7.3 %copy-start.21 = (bf16[2,640,512]{2,1,0:T(8,128)(2,1)}, bf16[2,640,512]{2,1,0:T(8,128)(2,1)S(1)}, u32[]{:S(2)}) copy-start(bf16[2,640,512]{2,1,0:T(8,128)(2,1)S(1)} %fusion.63) | copy-start | bytes 3932164
  414.8 30.6 %collective-permute-start.7 = (bf16[2,640,512]{2,1,0:T(8,128)(2,1)S(1)}, bf16[2,640,512]{2,1,0:T(8,128)(2,1)S(1)}, u32[]{:S(2)}, u32[]{:S(2)}) collective-permute-start(bf16[2,640,512]{2,1,0:T(8,128)(2,1)S(1)} %slice_bitcast_fusion), channel_id=1, source_target_pairs={{0,4},{2,6},{4,0},{6,2},{1,5},{3,7},{5,1},{7,3},{8,12},{10,14},{12... | collective-permute-start | bytes 3932168 | tf_op jit(solution)/shard_map/ppermute | solution.py:462
  416.3 269.3 %collective-permute-start.8 = (bf16[512,1280]{0,1:T(8,128)(2,1)}, bf16[512,1280]{0,1:T(8,128)(2,1)}, u32[]{:S(2)}, u32[]{:S(2)}) collective-permute-start(bf16[512,1280]{0,1:T(8,128)(2,1)} %get-tuple-element.63), channel_id=1, source_target_pairs={{0,1},{1,0},{2,3},{3,2},{4,5},{5,4},{6,7},{7,6},{8,9},{9,8},{10,11... | collective-permute-start | bytes 3932168 | tf_op jit(solution)/shard_map/ppermute | solution.py:462
  422.7 23.3 %slice-start.2 = ((s8[4915200]{0:T(1024)(128)(4,1)}), s8[4194304]{0:T(1024)(128)(4,1)S(1)}, s32[]{:S(2)}) async-start(s8[4915200]{0:T(1024)(128)(4,1)} %bitcast.283), calls=%async_computation.2 | async-start | bytes 8388608
  425.3 20.7 %slice-start.3 = ((s8[4915200]{0:T(1024)(128)(4,1)}), s8[720896]{0:T(1024)(128)(4,1)S(1)}, s32[]{:S(2)}) async-start(s8[4915200]{0:T(1024)(128)(4,1)} %bitcast.283), calls=%async_computation.3 | async-start | bytes 1441792
  485.1 200.5 %collective-permute-start.9 = (bf16[512,1280]{0,1:T(8,128)(2,1)}, bf16[512,1280]{0,1:T(8,128)(2,1)S(1)}, u32[]{:S(2)}, u32[]{:S(2)}) collective-permute-start(bf16[512,1280]{0,1:T(8,128)(2,1)} %get-tuple-element.64), channel_id=1, source_target_pairs={{0,1},{1,0},{2,3},{3,2},{4,5},{5,4},{6,7},{7,6},{8,9},{9,8},{10,11... | collective-permute-start | bytes 3932168 | tf_op jit(solution)/shard_map/ppermute | solution.py:462
  676.5 7.7 %copy-start.35 = (f32[320,1920]{1,0:T(8,128)S(1)}, f32[320,1920]{1,0:T(8,128)}, u32[]{:S(2)}) copy-start(f32[320,1920]{1,0:T(8,128)} %reshape.212) | copy-start | bytes 7372804
  678.6 7.1 %copy-start.14 = (bf16[1,1,512,1280]{2,3,1,0:T(8,128)(2,1)S(1)}, bf16[1,1,512,1280]{2,3,1,0:T(8,128)(2,1)}, u32[]{:S(2)}) copy-start(bf16[1,1,512,1280]{2,3,1,0:T(8,128)(2,1)} %copy.150) | copy-start | bytes 3932164
  678.6 7.1 %copy-start.33 = (bf16[512,1280]{0,1:T(8,128)(2,1)S(1)}, bf16[512,1280]{0,1:T(8,128)(2,1)}, u32[]{:S(2)}) copy-start(bf16[512,1280]{0,1:T(8,128)(2,1)} %get-tuple-element.64) | copy-start | bytes 3932164
  678.6 7.1 %copy-start.52 = (f32[1280]{0:T(1024)S(1)}, f32[1280]{0:T(1024)}, u32[]{:S(2)}) copy-start(f32[1280]{0:T(1024)} %param.20) | copy-start | bytes 15364
  696.1 6.0 copy-start.1
  (71 other events, 264.3 us)

commit v4 on v3

--- a/solution.py
+++ b/solution.py
@@ -494,13 +494,15 @@
         self.halves = (0,) if across_first else (0, 1)
 
 
-def closing_kernel(sizes, across_first, small_ref, first_ref, *refs):
+def closing_kernel(sizes, across_first, normed_ref, projected_ref, small_ref, first_ref, *refs):
     shard, ctx, tp = sizes
     units = len(across_first)
-    terms, refs = refs[: 4 * units], refs[4 * units :]
+    given, refs = refs[: 4 * units - 4], refs[4 * units - 4 :]
     results, refs = refs[:units], refs[units:]
     small_out, first_out, refs = refs[0], refs[1], refs[2:]
     scratch, refs = refs[: 4 * units], refs[4 * units :]
+    product_near, product_far, refs = refs[0], refs[1], refs[2:]
+    terms = (None, product_near, None, product_far) + tuple(given)
     small_got, first_got, c_send, c_recv, x_send, x_recv, z_send, z_recv, g_send, g_recv, v_send, v_recv = refs
     i, p, me = lax.axis_index("shard"), lax.axis_index("ctx"), lax.axis_index("tp")
     across, beside = flip(p, 2), flip(p, 1)
@@ -560,10 +562,35 @@
     def every_shard(one):
         lax.fori_loop(0, shard, lambda j, carry: (one(j), carry)[1], 0)
 
-    for g in grads:
-        for j in range(shard):
+    def send_near(g):
+        def one(j):
             c_copy(g, j, 0).start()
             c_copy(g, j, 1).start()
+
+        every_shard(one)
+
+    def product(owner, store):
+        count = projected_ref.shape[1] // ctx
+        rows = pl.ds(pl.multiple_of(owner * count, math.gcd(count, 16)), count)
+        model = normed_ref.shape[2]
+        for low in range(0, model, 256):
+            cols = slice(low, min(model, low + 256))
+            total = 0.0
+            for m in range(2):
+                total = total + contract(projected_ref[m, rows], normed_ref[m, :, cols], ((1,), (0,)))
+            store(cols, total.T)
+
+    def put(target):
+        def store(cols, value):
+            target[cols] = value.astype(LOW)
+
+        return store
+
+    def add(target):
+        def store(cols, value):
+            target[cols] = (target[cols].astype(jnp.float32) + value).astype(LOW)
+
+        return store
 
     def meet(g, j):
         c_copy(g, j, 0).wait_recv()
@@ -649,13 +676,17 @@
     small_out[0] = small_ref[...]
     first_out[0] = first_ref[...]
     vector_start(0)
-    sent_across = [g for g in grads if g.across_first]
-    sent_along = [g for g in grads if not g.across_first]
-    for g in sent_across[:1] + sent_along + sent_across[1:]:
-        every_shard(lambda j: meet(g, j))
-        if not g.across_first:
-            for step in range(1):
-                hop(g, step)
+    qkv, out, up, down = grads
+    for g in (down, up, out):
+        send_near(g)
+    every_shard(lambda j: meet(down, j))
+    hop(down, 0)
+    every_shard(lambda j: meet(up, j))
+    product(beside, put(product_near))
+    product(flip(across, 1), put(product_far))
+    send_near(qkv)
+    every_shard(lambda j: meet(out, j))
+    hop(down, 1)
     number = 0
 
     def next_vector():
@@ -666,28 +697,45 @@
             if number < len(partners):
                 vector_start(number)
 
-    for step in range(1, shard - 1):
-        for g in sent_along:
-            hop(g, step)
-        next_vector()
-    for g in sent_across:
-        every_shard(lambda j: joined(g, j))
-        hop(g, 0)
-        next_vector()
-    for g in sent_along:
-        arrive(g)
-        side_copy(g).start()
-    for step in range(1, shard - 1):
-        for g in sent_across:
-            hop(g, step)
-        next_vector()
-    for g in sent_along:
-        side_copy(g).wait_recv()
-        add_to(rows_of(g.sums[0], i), g.crossed[...])
-        finish(g)
-    for g in sent_across:
-        arrive(g)
-        finish(g)
+    def met(j):
+        c_copy(qkv, j, 0).wait_recv()
+        c_copy(qkv, j, 1).wait_recv()
+
+    every_shard(met)
+    product(across, add(qkv.far))
+    every_shard(lambda j: x_copy(qkv, j).start())
+    product(p, add(qkv.near))
+    for step in range(2, shard - 1):
+        hop(down, step)
+    next_vector()
+    every_shard(lambda j: joined(up, j))
+    hop(up, 0)
+    next_vector()
+    arrive(down)
+    side_copy(down).start()
+    every_shard(lambda j: joined(out, j))
+    hop(out, 0)
+    hop(up, 1)
+    next_vector()
+    every_shard(lambda j: joined(qkv, j))
+    hop(qkv, 0)
+    hop(out, 1)
+    next_vector()
+    side_copy(down).wait_recv()
+    add_to(rows_of(down.sums[0], i), down.crossed[...])
+    finish(down)
+    for step in range(2, shard - 1):
+        hop(up, step)
+    hop(qkv, 1)
+    arrive(up)
+    finish(up)
+    for step in range(2, shard - 1):
+        hop(out, step)
+        hop(qkv, step)
+    arrive(out)
+    finish(out)
+    arrive(qkv)
+    finish(qkv)
     while number < len(partners):
         next_vector()
     for g in grads:
@@ -723,13 +771,13 @@
             v_copy(n, which).wait_send()
 
 
-def closing(sizes, across_first, small, first, terms):
+def closing(sizes, across_first, normed, projected, small, first, terms):
     shard, ctx, tp = sizes
     units = len(across_first)
     vmem = pl.BlockSpec(memory_space=pltpu.VMEM)
     dma = pltpu.SemaphoreType.DMA
     stages = len(bits_of(tp)) + len(bits_of(ctx)) + len(bits_of(shard))
-    shapes = [t[0].shape for t in terms]
+    shapes = [(normed.shape[2], projected.shape[1] // ctx)] + [t[0].shape for t in terms]
     scratch = []
     for (model, n), early in zip(shapes, across_first):
         each, halves = model // shard, 1 if early else 2
@@ -741,11 +789,12 @@
         ]
     found = pl.pallas_call(
         functools.partial(closing_kernel, sizes, across_first),
-        in_specs=[vmem] * (2 + 4 * units),
+        in_specs=[vmem] * (4 + 4 * units - 4),
         out_specs=[vmem] * (units + 2),
         out_shape=[jax.ShapeDtypeStruct((ctx, model // shard, n), LOW) for model, n in shapes]
         + [jax.ShapeDtypeStruct((stages + 1,) + v.shape, jnp.float32) for v in (small, first)],
         scratch_shapes=scratch
+        + [pltpu.VMEM(shapes[0], LOW)] * 2
         + [pltpu.VMEM((stages,) + v.shape, jnp.float32) for v in (small, first)]
         + [
             dma((units, shard, 2)),
@@ -762,7 +811,7 @@
         compiler_params=pltpu.CompilerParams(collective_id=1, has_side_effects=True, vmem_limit_bytes=56 << 20),
         cost_estimate=pl.CostEstimate(flops=0, bytes_accessed=200 << 20, transcendentals=0),
         name="closing",
-    )(small, first, *[t for four in terms for t in four])
+    )(normed, projected, small, first, *[t for four in terms for t in four])
     return found[:units], found[units][stages], found[units + 1][stages]
 
 
@@ -868,10 +917,18 @@
         active.append((hidden[m] * cdf).astype(LOW))
         slope = cdf + hidden[m] * pdf
         hidden_grads.append((contract(cotangent[m, 0], full_down, ((1,), (0,))) * slope).astype(LOW))
-        normed2_grads.append(low_sum(contract(hidden_grads[m], full_up, ((1,), (1,))), "tp", tp))
+        normed2_grads.append(low_sum_start(contract(hidden_grads[m], full_up, ((1,), (1,))), "tp", tp))
+
+    def over(items, dim):
+        return jnp.concatenate(items, axis=dim)
+
+    up_terms = weight_terms([over(normed2, 0)], [over(hidden_grads, 0)], 1, ctx)
+    mine, up_terms = lax.optimization_barrier(([total for total, _ in normed2_grads], up_terms))
+    normed2_grads = [
+        (a.astype(jnp.float32) + b[1].astype(jnp.float32)).astype(LOW).astype(jnp.float32)
+        for a, b in zip(mine, normed2_grads)
+    ]
     for m in range(micros):
-        branch = low_sum(contract(active[m], full_down, ((1,), (1,))), "tp", tp)
-        outputs.append((mixed[m] + branch + down_bias).astype(LOW))
         hat, inverse = hats2[m]
         mixed_grads.append(
             cotangent[m, 0].astype(jnp.float32) + normalize_grad(normed2_grads[m] * norm2_gain, hat, inverse)
@@ -894,6 +951,11 @@
         chip = (
             pairs_grad[: ctx // 2].astype(jnp.float32) + swap(pairs_grad[ctx // 2 :], "ctx", 1, ctx).astype(jnp.float32)
         ).astype(LOW)
+        if m == 0:
+            late, query_grad = lax.optimization_barrier((active, query_grad))
+            branches = low_sum_start(contract(over(late, 0), full_down, ((1,), (1,))), "tp", tp)
+    active, query_grad, projected_grads = lax.optimization_barrier((active, query_grad, projected_grads))
+    down_terms = weight_terms([over([cotangent[m, 0] for m in range(micros)], 0)], [over(active, 0)], 1, ctx)
     projected_grads.append(finish_pairs(query_grad, chip))
     for m in range(micros):
         normed1_terms.append(contract(projected_grads[m], full_qkv, ((0,), (1,))))
@@ -902,10 +964,7 @@
         hat, inverse = hats1[m]
         gain1.append(jnp.sum(normed1_terms[m] * hat, axis=0))
         bias1.append(jnp.sum(normed1_terms[m], axis=0))
-        normed1_grads.append(low_sum_start(normed1_terms[m], "tp", tp))
-
-    def over(items, dim):
-        return jnp.concatenate(items, axis=dim)
+    normed1_grads = low_sum_start(over(normed1_terms, 0), "tp", tp)
 
     def row_sum(items):
         return sum(jnp.sum(item.astype(jnp.float32), axis=0) for item in items)
@@ -924,18 +983,23 @@
     first = jnp.concatenate([sum(gain1), sum(bias1)])
     blocks, small_sum, first_sum = closing(
         sizes,
-        (False, False, True, True),
+        (True, True, True, False),
+        jnp.stack(normed1),
+        jnp.stack(projected_grads),
         as_tiles(small),
         as_tiles(first),
         (
-            weight_terms(normed1, projected_grads, 0, ctx),
             weight_terms(branch_grads, attended, 0, ctx),
-            weight_terms([over(normed2, 0)], [over(hidden_grads, 0)], 1, ctx),
-            weight_terms([over([cotangent[m, 0] for m in range(micros)], 0)], [over(active, 0)], 1, ctx),
+            up_terms,
+            down_terms,
         ),
     )
-    mine, blocks = lax.optimization_barrier(([total for total, _ in normed1_grads], blocks))
-    normed1_grads = [a.astype(jnp.float32) + b[1].astype(jnp.float32) for a, b in zip(mine, normed1_grads)]
+    mine, own_branch, blocks = lax.optimization_barrier((normed1_grads[0], branches[0], blocks))
+    normed1_grads = (mine.astype(jnp.float32) + normed1_grads[1].astype(jnp.float32)).reshape(micros, rows, -1)
+    branches = (own_branch.astype(jnp.float32) + branches[1].astype(jnp.float32)).astype(LOW).astype(jnp.float32)
+    branches = branches.reshape(micros, rows, -1)
+    for m in range(micros):
+        outputs.append((mixed[m] + branches[m] + down_bias).astype(LOW))
     for m in range(micros):
         hat, inverse = hats1[m]
         input_grads.append(mixed_grads[m] + normalize_grad(normed1_grads[m] * norm1_gain, hat, inverse))

time: 711 us -> 629 us (0.88)
  matrix products: 140 us -> 101 us
  local copies, waits for them, and re-layouts: 99.3 us -> 72.4 us
  other arithmetic: 68 us -> 58.8 us
    dot_general x40 -> x31, matrix products: 140 us -> 101 us  [contract(): lax.dot_general(left, right, (dims, ((), ())), preferred_element_type=jnp...]
    unnamed x193 -> x136, local copies, waits for them, and re-layouts: 34.8 us -> 23.1 us
    reduce_sum x3 -> x1, other arithmetic: 12.4 us -> 1.83 us  [normalize_grad(): jnp.mean(grad * hat, axis=-1, keepdims=True)]
    add x8 -> x4, local copies, waits for them, and re-layouts: 14.2 us -> 4.37 us  [term(): total = total + contract(left, part, ((0,), (1 - right_dim,)))]
    reduce_sum x3 -> x2, other arithmetic: 15.1 us -> 8.13 us  [row_sum(): return sum((jnp.sum(item.astype(jnp.float32), axis=0) for item in items))]
    ppermute x10 -> x8, waiting for transfers between devices: 26.4 us -> 28.8 us  [swap(): return lax.ppermute(value, axis, [(k, k ^ bit) for k in range(size)])]
  transfers between devices with their start and end apart: 10 -> 8, of which waited for: 2 -> 3; matrix products, arithmetic and copies ran while one was open for 31% -> 23% of each run, Pallas kernels for 29% -> 29%
where the time goes in v4:
time: 629 us; the launch traced here: 621 us
  Pallas kernels  352 us (56%)
  matrix products  101 us (16%)
  local copies, waits for them, and re-layouts  72.4 us (12%)
  other arithmetic  58.8 us (9%)
  waiting for transfers between devices  28.8 us (5%)
  starting transfers between devices  7.02 us (1%)
    pallas_call x1, Pallas kernels, closing(): pl.pallas_call(functools.partial(closing_kernel, sizes, across_first), in...  159 us
    pallas_call x1, Pallas kernels, opening(): pl.pallas_call(functools.partial(opening_kernel, sizes), in_specs=[pl.Blo...  154 us
    dot_general x31, matrix products, contract(): lax.dot_general(left, right, (dims, ((), ())), preferred_element_type=jnp...  101 us
    pallas_call x2, Pallas kernels, attention_backward(): pl.pallas_call(lambda own_ref, *refs: backward_kernel(*refs), grid_spec=g...  38 us
    ppermute x8, waiting for transfers between devices, swap(): return lax.ppermute(value, axis, [(k, k ^ bit) for k in range(size)])  28.8 us
    unnamed x136, local copies, waits for them, and re-layouts  23.1 us
    convert_element_type x5, local copies, waits for them, and re-layouts, whole_rows(): return jnp.moveaxis(blocks, 0, 1).reshape(each, ctx * n).astype(jnp.float32)  16.7 us
  transfers between devices with their start and end apart: 8, of which 3 were waited for; matrix products, arithmetic and copies ran while one was open for 23% of the time, Pallas kernels for 29%

profile of v4, /device:TPU:9, one launch (start us, length us, event | category | flops | bytes accessed | tf_op | source)
XLA Modules:
  0.0 621.3 jit_solution(17231123500798413339)
XLA Ops:
  8.0 4.4 copy.63.normed_ref
  21.7 154.1 %opening.1 = (bf16[1280,1920]{1,0:T(8,128)(2,1)}, bf16[2,1280,640]{2,1,0:T(8,128)(2,1)}, bf16[1280,2560]{1,0:T(8,128)(2,1)}, bf16[1280,2560]{1,0:T(8,128)(2,1)},...) custom-call(s32[2,4]{1,0:T(2,128)} %pad_add_fusion.valid_ref, ...), custom_call_target="tpu_custom_call" | custom-call | flops 17179869184 | bytes 83886080 | tf_op jit(solution)/shard_map/opening/pallas_call | solution.py:355
  189.0 5.2 multiply_convert_fusion
  194.3 5.6 convert_reduce_fusion
  199.8 4.6 convolution_convert_fusion.8
  205.7 5.1 multiply_convert_fusion.1
  210.8 4.9 convert_reduce_fusion.1
  215.7 4.7 convolution_convert_fusion.9
  220.6 3.7 fusion.71
  224.3 5.5 convolution_convert_fusion.7.refs_4_
  229.8 5.5 convolution_convert_fusion.6.refs_5_
  235.3 5.6 convolution_convert_fusion.5.refs_6_
  240.9 5.5 convolution_convert_fusion.4.refs_7_
  253.4 9.9 %collective-permute-done.1 = bf16[512,1280]{1,0:T(8,128)(2,1)} collective-permute-done((bf16[512,1280]{1,0:T(8,128)(2,1)}, bf16[512,1280]{1,0:T(8,128)(2,1)}, u32[]{:S(2)}, u32[]{:S(2)}) %collective-permute-start.1) | collective-permute-done | bytes 1310752 | tf_op jit(solution)/shard_map/ppermute | solution.py:462
  263.3 4.6 fusion.77
  268.0 3.5 convert_reduce_fusion.7
  271.7 3.7 copy-done.29
  276.7 18.9 %attention_backward.2 = (bf16[640,512]{1,0:T(8,128)(2,1)S(1)}, bf16[4,2,640,512]{3,2,1,0:T(8,128)(2,1)S(1)}) custom-call(s32[1]{0:T(128)} %bitcast.11.own_ref, bf16[2,640,512]{2,1,0:T(8,128)(2,1)S(1)} %copy-done.6, bf16[640,512]{1,0:T(8,128)(2,1)S(1)} %fusion.107.refs_1_, bf16[2,2,640,512]{3,2,1,0:T(8,128)(2,1)S(1)} %copy-done.2, ...), custom_call_target="tpu_custom_call" | custom-call | flops 17179869184 | bytes 16777216 | tf_op jit(solution)/shard_map/attention_backward/pallas_call | solution.py:446
  298.6 12.7 %fusion.16 = bf16[1024,1280]{1,0:T(8,128)(2,1)} fusion(bf16[1280,2560]{1,0:T(8,128)(2,1)} %get-tuple-element.61, bf16[512,2560]{1,0:T(8,128)(2,1)S(1)} %copy-done.33, bf16[512,2560]{1,0:T(8,128)(2,1)} %get-tuple-element.83), kind=kOutput, calls=%fused_computation.52 | convolution fusion | flops 6722682880 | bytes 14417920 | tf_op jit(solution)/shard_map/dot_general | solution.py:20
  324.1 19.1 %attention_backward.3 = (bf16[640,512]{1,0:T(8,128)(2,1)S(1)}, bf16[4,2,640,512]{3,2,1,0:T(8,128)(2,1)S(1)}) custom-call(s32[1]{0:T(128)} %bitcast.11.own_ref, bf16[2,640,512]{2,1,0:T(8,128)(2,1)S(1)} %copy-done.6, bf16[640,512]{1,0:T(8,128)(2,1)S(1)} %fusion.104.refs_1_, bf16[2,2,640,512]{3,2,1,0:T(8,128)(2,1)S(1)} %copy-done.2, ...), custom_call_target="tpu_custom_call" | custom-call | flops 17179869184 | bytes 16777216 | tf_op jit(solution)/shard_map/attention_backward/pallas_call | solution.py:446
  360.8 3.4 convolution_convert_fusion.3.refs_8_
  364.3 3.4 convolution_convert_fusion.2.refs_9_
  370.6 3.4 convolution_convert_fusion.1.refs_10_
  374.0 3.9 convolution_convert_fusion.refs_11_
  380.9 17.8 %collective-permute-done.5 = bf16[2,640,512]{2,1,0:T(8,128)(2,1)S(1)} collective-permute-done((bf16[2,640,512]{2,1,0:T(8,128)(2,1)S(1)}, bf16[2,640,512]{2,1,0:T(8,128)(2,1)S(1)}, u32[]{:S(2)}, u32[]{:S(2)}) %collective-permute-start.5) | collective-permute-done | bytes 1310752 | tf_op jit(solution)/shard_map/ppermute | solution.py:462
  400.9 4.1 fusion.54
  412.0 159.5 %closing.1 = (bf16[4,320,480]{2,1,0:T(8,128)(2,1)}, bf16[4,320,160]{2,1,0:T(8,128)(2,1)}, bf16[4,320,640]{2,1,0:T(8,128)(2,1)}, bf16[4,320,640]{2,1,0:T(8,128)(2...) custom-call(bf16[2,512,1280]{2,1,0:T(8,128)(2,1)} %pad_maximum_fusion.3.normed_ref, ...), custom_call_target="tpu_custom_call" | custom-call | bytes 209715200 | tf_op jit(solution)/shard_map/closing/pallas_call | solution.py:790
  582.3 3.2 copy.69
  585.5 4.5 reshape.432
  595.0 4.2 copy.76
  604.3 3.2 fusion.79
  610.8 3.1 convert_add_fusion
  (254 shorter events, 119.0 us)
Async XLA Ops:
  0.7 19.3 %copy-start = (bf16[320,2560]{1,0:T(8,128)(2,1)S(1)}, bf16[320,2560]{1,0:T(8,128)(2,1)}, u32[]{:S(2)}) copy-start(bf16[320,2560]{1,0:T(8,128)(2,1)} %param.33) | copy-start | bytes 4915204
  8.0 4.4 copy-start.54
  8.0 4.4 copy-start.55
  185.5 8.8 %slice-start.6 = ((s8[6553600]{0:T(1024)(128)(4,1)}), s8[4194304]{0:T(1024)(128)(4,1)S(1)}, s32[]{:S(2)}) async-start(s8[6553600]{0:T(1024)(128)(4,1)} %bitcast.296), calls=%async_computation.6 | async-start | bytes 8388608
  186.4 7.8 %copy-start.43 = (bf16[512,1280]{1,0:T(8,128)(2,1)}, bf16[512,1280]{1,0:T(8,128)(2,1)S(1)}, u32[]{:S(2)}) copy-start(bf16[512,1280]{1,0:T(8,128)(2,1)S(1)} %get-tuple-element.209) | copy-start | bytes 3932164
  186.4 19.3 %copy-start.44 = (bf16[512,1280]{1,0:T(8,128)(2,1)}, bf16[512,1280]{1,0:T(8,128)(2,1)S(1)}, u32[]{:S(2)}) copy-start(bf16[512,1280]{1,0:T(8,128)(2,1)S(1)} %get-tuple-element.210) | copy-start | bytes 3932164
  189.0 5.3 copy-start.22
  189.0 5.3 slice-start.7
  199.8 4.6 copy-start.57
  204.4 49.0 %collective-permute-start = (bf16[512,1280]{1,0:T(8,128)(2,1)}, bf16[512,1280]{1,0:T(8,128)(2,1)}, u32[]{:S(2)}, u32[]{:S(2)}) collective-permute-start(bf16[512,1280]{1,0:T(8,128)(2,1)} %convolution_convert_fusion.8), channel_id=1, source_target_pairs={{0,1},{1,0},{2,3},{3,2},{4,5},{5,4},{6,7},{7,6},{8,9},{9,8},{10,11... | collective-permute-start | bytes 3932168 | tf_op jit(solution)/shard_map/ppermute | solution.py:462
  215.7 4.7 copy-start.58
  220.4 43.0 %collective-permute-start.1 = (bf16[512,1280]{1,0:T(8,128)(2,1)}, bf16[512,1280]{1,0:T(8,128)(2,1)}, u32[]{:S(2)}, u32[]{:S(2)}) collective-permute-start(bf16[512,1280]{1,0:T(8,128)(2,1)} %convolution_convert_fusion.9), channel_id=1, source_target_pairs={{0,1},{1,0},{2,3},{3,2},{4,5},{5,4},{6,7},{7,6},{8,9},{9,8},{10,11... | collective-permute-start | bytes 3932168 | tf_op jit(solution)/shard_map/ppermute | solution.py:462
  251.8 11.5 %copy-start.12 = (f32[512,1280]{1,0:T(8,128)S(1)}, f32[512,1280]{1,0:T(8,128)}, u32[]{:S(2)}) copy-start(f32[512,1280]{1,0:T(8,128)} %copy-done.11) | copy-start | bytes 7864324
  251.8 11.5 %copy-start.15 = (f32[512,1280]{1,0:T(8,128)S(1)}, f32[512,1280]{1,0:T(8,128)}, u32[]{:S(2)}) copy-start(f32[512,1280]{1,0:T(8,128)} %copy-done.14) | copy-start | bytes 7864324
  271.5 4.9 copy-start.17
  271.5 41.1 %copy-start.19 = (f32[512,1280]{1,0:T(8,128)}, f32[512,1280]{1,0:T(8,128)S(1)}, u32[]{:S(2)}) copy-start(f32[512,1280]{1,0:T(8,128)S(1)} %get-tuple-element.197) | copy-start | bytes 7864324
  297.4 22.9 %collective-permute-start.2 = (bf16[2,2,640,512]{3,2,1,0:T(8,128)(2,1)}, bf16[2,2,640,512]{3,2,1,0:T(8,128)(2,1)}, u32[]{:S(2)}, u32[]{:S(2)}) collective-permute-start(bf16[2,2,640,512]{3,2,1,0:T(8,128)(2,1)} %slice.193), channel_id=1, source_target_pairs={{0,2},{2,0},{4,6},{6,4},{1,3},{3,1},{5,7},{7,5},{8,10},{10,8},{12,... | collective-permute-start | bytes 7864328 | tf_op jit(solution)/shard_map/ppermute | solution.py:462
  311.3 292.9 %collective-permute-start.6 = (bf16[1024,1280]{1,0:T(8,128)(2,1)}, bf16[1024,1280]{1,0:T(8,128)(2,1)}, u32[]{:S(2)}, u32[]{:S(2)}) collective-permute-start(bf16[1024,1280]{1,0:T(8,128)(2,1)} %fusion.16), channel_id=1, source_target_pairs={{0,1},{1,0},{2,3},{3,2},{4,5},{5,4},{6,7},{7,6},{8,9},{9,8},{10,11... | collective-permute-start | bytes 7864328 | tf_op jit(solution)/shard_map/ppermute | solution.py:462
  322.7 20.5 %copy-start.24 = (bf16[2,2,640,512]{3,2,1,0:T(8,128)(2,1)}, bf16[2,2,640,512]{3,2,1,0:T(8,128)(2,1)S(1)}, u32[]{:S(2)}) copy-start(bf16[2,2,640,512]{3,2,1,0:T(8,128)(2,1)S(1)} %add_convert_fusion.2) | copy-start | bytes 7864324
  323.9 29.6 %collective-permute-start.3 = (bf16[2,640,512]{2,1,0:T(8,128)(2,1)}, bf16[2,640,512]{2,1,0:T(8,128)(2,1)}, u32[]{:S(2)}, u32[]{:S(2)}) collective-permute-start(bf16[2,640,512]{2,1,0:T(8,128)(2,1)} %slice_bitcast_fusion.2), channel_id=1, source_target_pairs={{0,4},{2,6},{4,0},{6,2},{1,5},{3,7},{5,1},{7,3},{8,12},{10,14},{12... | collective-permute-start | bytes 3932168 | tf_op jit(solution)/shard_map/ppermute | solution.py:462
  346.4 3.8 copy-start.38
  346.4 21.3 %collective-permute-start.4 = (bf16[2,2,640,512]{3,2,1,0:T(8,128)(2,1)}, bf16[2,2,640,512]{3,2,1,0:T(8,128)(2,1)}, u32[]{:S(2)}, u32[]{:S(2)}) collective-permute-start(bf16[2,2,640,512]{3,2,1,0:T(8,128)(2,1)} %slice.197), channel_id=1, source_target_pairs={{0,2},{2,0},{4,6},{6,4},{1,3},{3,1},{5,7},{7,5},{8,10},{10,8},{12,... | collective-permute-start | bytes 7864328 | tf_op jit(solution)/shard_map/ppermute | solution.py:462
  351.3 4.3 copy-start.5
  360.8 6.9 %slice-start = ((s8[5242880]{0:T(1024)(128)(4,1)}), s8[4194304]{0:T(1024)(128)(4,1)S(1)}, s32[]{:S(2)}) async-start(s8[5242880]{0:T(1024)(128)(4,1)} %bitcast.281), calls=%async_computation | async-start | bytes 8388608
  370.3 28.4 %collective-permute-start.5 = (bf16[2,640,512]{2,1,0:T(8,128)(2,1)S(1)}, bf16[2,640,512]{2,1,0:T(8,128)(2,1)S(1)}, u32[]{:S(2)}, u32[]{:S(2)}) collective-permute-start(bf16[2,640,512]{2,1,0:T(8,128)(2,1)S(1)} %slice_bitcast_fusion), channel_id=1, source_target_pairs={{0,4},{2,6},{4,0},{6,2},{1,5},{3,7},{5,1},{7,3},{8,12},{10,14},{12... | collective-permute-start | bytes 3932168 | tf_op jit(solution)/shard_map/ppermute | solution.py:462
  370.6 7.3 %slice-start.2 = ((s8[4915200]{0:T(1024)(128)(4,1)}), s8[4194304]{0:T(1024)(128)(4,1)S(1)}, s32[]{:S(2)}) async-start(s8[4915200]{0:T(1024)(128)(4,1)} %bitcast.292), calls=%async_computation.2 | async-start | bytes 8388608
  374.0 3.9 slice-start.3
  406.6 204.2 %collective-permute-start.7 = (bf16[1024,1280]{1,0:T(8,128)(2,1)}, bf16[1024,1280]{1,0:T(8,128)(2,1)}, u32[]{:S(2)}, u32[]{:S(2)}) collective-permute-start(bf16[1024,1280]{1,0:T(8,128)(2,1)} %pad_maximum_fusion.2), channel_id=1, source_target_pairs={{0,1},{1,0},{2,3},{3,2},{4,5},{5,4},{6,7},{7,6},{8,9},{9,8},{10,11... | collective-permute-start | bytes 7864328 | tf_op jit(solution)/shard_map/ppermute | solution.py:462
  571.5 5.1 copy-start.45
  595.0 4.2 copy-start.21
  604.3 4.1 copy-start.16
  604.3 4.1 copy-start.53
  (43 other events, 101.2 us)
